TPU v7x, 32 devices: a whole 2x2x4 slice. The times are simulated.
32 devices in a mesh: section: 2 (over core), seq: 4 (over y, x), fsdp: 4 (over z).
Axes of the slice: x: 2, y: 2, z: 4, core: 2. Of those that a mesh axis runs over, the one named last changes fastest.
Arguments:
- inputs: bfloat16 [2, 8, 1024, 1152], P(None, 'fsdp', 'seq'), may hold values from -6 to 6
- cotangent: bfloat16 [2, 8, 1024, 1152], P(None, 'fsdp', 'seq'), may hold values from -6 to 6
- segments: int32 [2, 8, 1024], P(None, 'fsdp', 'seq'), may hold values from 0 to 64, as said below
- w_query: bfloat16 [2, 1152, 1152], P('section', ('seq', 'fsdp')), may hold values from -0.1875 to 0.1875
- w_key: bfloat16 [2, 1152, 384], P('section', ('seq', 'fsdp')), may hold values from -0.1875 to 0.1875
- w_value: bfloat16 [2, 1152, 384], P('section', ('seq', 'fsdp')), may hold values from -0.1875 to 0.1875
- w_out: bfloat16 [2, 1152, 1152], P('section', None, ('seq', 'fsdp')), may hold values from -0.75 to 0.75
- w_gate: bfloat16 [2, 1152, 3072], P('section', ('seq', 'fsdp')), may hold values from -0.1875 to 0.1875
- w_up: bfloat16 [2, 1152, 3072], P('section', ('seq', 'fsdp')), may hold values from -0.1875 to 0.1875
- w_down: bfloat16 [2, 3072, 1152], P('section', None, ('seq', 'fsdp')), may hold values from -0.109375 to 0.109375
- norm_attn: bfloat16 [2, 1152], P('section', ('seq', 'fsdp')), may hold values from 0.25 to 1.75
- norm_mlp: bfloat16 [2, 1152], P('section', ('seq', 'fsdp')), may hold values from 0.25 to 1.75
Outputs:
- layer_out: bfloat16 [2, 2, 8, 1024, 1152], P('section', None, 'fsdp', 'seq')
- input_grad: bfloat16 [2, 2, 8, 1024, 1152], P('section', None, 'fsdp', 'seq')
- g_query: float32 [2, 1152, 1152], P('section', ('seq', 'fsdp'))
- g_key: float32 [2, 1152, 384], P('section', ('seq', 'fsdp'))
- g_value: float32 [2, 1152, 384], P('section', ('seq', 'fsdp'))
- g_out: float32 [2, 1152, 1152], P('section', None, ('seq', 'fsdp'))
- g_gate: float32 [2, 1152, 3072], P('section', ('seq', 'fsdp'))
- g_up: float32 [2, 1152, 3072], P('section', ('seq', 'fsdp'))
- g_down: float32 [2, 3072, 1152], P('section', None, ('seq', 'fsdp'))
- g_norm_attn: float32 [2, 1152], P('section', ('seq', 'fsdp'))
- g_norm_mlp: float32 [2, 1152], P('section', ('seq', 'fsdp'))
Inputs may be any that keep to these rules, and one draw needn't show every extreme that they name: `segments`: within a sequence the numbers never fall except into a trailing run of 0 (the masked tail, at most a quarter of the sequence); documents are numbered 1, 2, ... in order. In every micro-batch, on every index of fsdp, one of its 2 sequences is a single document 1 with no tail.
All inputs are finite; a program needn't handle non-finite values.
Results may differ from a plain program's by a relative error of at most 0.038.
Values may be sent and summed in bfloat16 or wider, within the bound.
No kernel may reach another device: no remote copies, remote signals or barrier semaphores. Data moves between devices by JAX's collectives and lax.ppermute only.
A program may use at most 512 MiB of HBM per device.

v0:
```python
import jax
import jax.numpy as jnp
from jax import lax
from jax.sharding import PartitionSpec as P

HEAD_SIZE = 64


epsilon = 1e-05
rope_base = 10000.0
neg_large = -1e30


def shifted(value, axis, steps):
    count = lax.axis_size(axis)
    leading, last = (max(0, -steps), min(count, count - steps))
    return lax.ppermute(value, axis, [(source, source + steps) for source in range(leading, last)])


def rope_turn(value_rows, positions, direction):
    head_count = value_rows.shape[-1] // HEAD_SIZE
    pieces = value_rows.reshape(value_rows.shape[:-1] + (head_count, HEAD_SIZE))
    half_dim = HEAD_SIZE // 2
    frequency = rope_base ** (-2.0 * jnp.arange(half_dim, dtype=jnp.float32) / HEAD_SIZE)
    angles = positions.astype(jnp.float32)[:, None] * frequency[None, :]
    cosine = jnp.cos(angles)[:, None, :]
    sine_part = direction * jnp.sin(angles)[:, None, :]
    first_half = pieces[..., :half_dim]
    second_half = pieces[..., half_dim:]
    turned = jnp.concatenate(
        [
            first_half * cosine - second_half * sine_part,
            second_half * cosine + first_half * sine_part,
        ],
        axis=-1,
    )
    return turned.reshape(value_rows.shape)


def visible_mask(q_pos, q_seg, k_pos, k_seg):
    same_doc = q_seg[:, :, None] == k_seg[:, None, :]
    causal = k_pos[None, None, :] <= q_pos[None, :, None]
    diagonal = k_pos[None, None, :] == q_pos[None, :, None]
    return same_doc & causal & ((q_seg[:, :, None] != 0) | diagonal)


def score_block(
    query_rows, keys_all, values_all, seg_all, q_pos, q_seg, start_offset, block_length
):
    seq_count, row_count, kv_heads, query_groups, head_dim = query_rows.shape
    k_block = lax.dynamic_slice_in_dim(keys_all, start_offset, block_length, 1).reshape(
        seq_count, block_length, kv_heads, head_dim
    )
    v_block = lax.dynamic_slice_in_dim(values_all, start_offset, block_length, 1).reshape(
        seq_count, block_length, kv_heads, head_dim
    )
    k_seg = lax.dynamic_slice_in_dim(seg_all, start_offset, block_length, 1)
    k_pos = start_offset + jnp.arange(block_length)
    raw_scores = (
        jnp.einsum("scngd,spnd->sngcp", query_rows, k_block, preferred_element_type=jnp.float32)
        * 0.125
    )
    allowed = visible_mask(q_pos, q_seg, k_pos, k_seg)
    return (jnp.where(allowed[:, None, None, :, :], raw_scores, neg_large), k_block, v_block)


def attend(query_rows, keys_all, values_all, seg_all, q_pos, q_seg):
    seq_count, row_count, kv_heads, query_groups, head_dim = query_rows.shape
    key_total = keys_all.shape[1]
    block_length = min(512, key_total)
    block_count = key_total // block_length

    def stat_step(carry, block_index):
        row_top, row_mass = carry
        scores, k_block, v_block = score_block(
            query_rows,
            keys_all,
            values_all,
            seg_all,
            q_pos,
            q_seg,
            block_index * block_length,
            block_length,
        )
        new_top = jnp.maximum(row_top, jnp.max(scores, axis=-1))
        row_mass = row_mass * jnp.exp(row_top - new_top) + jnp.sum(
            jnp.exp(scores - new_top[..., None]), axis=-1
        )
        return ((new_top, row_mass), None)

    stat_shape = (seq_count, kv_heads, query_groups, row_count)
    start_carry = (jnp.full(stat_shape, neg_large, jnp.float32), jnp.zeros(stat_shape, jnp.float32))
    (row_top, row_mass), _ = lax.scan(stat_step, start_carry, jnp.arange(block_count))
    log_total = row_top + jnp.log(row_mass)

    def out_step(summed, block_index):
        scores, k_block, v_block = score_block(
            query_rows,
            keys_all,
            values_all,
            seg_all,
            q_pos,
            q_seg,
            block_index * block_length,
            block_length,
        )
        probs = jnp.exp(scores - log_total[..., None]).astype(jnp.bfloat16)
        return (
            summed
            + jnp.einsum("sngcp,spnd->scngd", probs, v_block, preferred_element_type=jnp.float32),
            None,
        )

    summed, _ = lax.scan(
        out_step, jnp.zeros(query_rows.shape, jnp.float32), jnp.arange(block_count)
    )
    return (summed, log_total)


def query_side(query_rows, keys_all, values_all, seg_all, q_pos, q_seg, grad_out, log_total, delta):
    key_total = keys_all.shape[1]
    block_length = min(512, key_total)
    block_count = key_total // block_length

    def query_back_step(grad_query, block_index):
        scores, k_block, v_block = score_block(
            query_rows,
            keys_all,
            values_all,
            seg_all,
            q_pos,
            q_seg,
            block_index * block_length,
            block_length,
        )
        probs = jnp.exp(scores - log_total[..., None])
        grad_probs = jnp.einsum(
            "scngd,spnd->sngcp", grad_out, v_block, preferred_element_type=jnp.float32
        )
        grad_scores = (probs * (grad_probs - delta[..., None])).astype(jnp.bfloat16)
        grad_query = (
            grad_query
            + jnp.einsum(
                "sngcp,spnd->scngd", grad_scores, k_block, preferred_element_type=jnp.float32
            )
            * 0.125
        )
        return (grad_query, None)

    grad_query, _ = lax.scan(
        query_back_step, jnp.zeros(query_rows.shape, jnp.float32), jnp.arange(block_count)
    )
    return grad_query


def key_side(
    query_all, grad_out_all, log_all, delta_all, seg_all, own_keys, own_values, k_pos, k_seg
):
    seq_count, query_total, kv_heads, query_groups, head_dim = query_all.shape
    row_count = own_keys.shape[1]
    block_length = min(512, query_total)
    block_count = query_total // block_length
    key_rows = own_keys.reshape(seq_count, row_count, kv_heads, head_dim)
    value_rows = own_values.reshape(seq_count, row_count, kv_heads, head_dim)

    def key_back_step(carry, block_index):
        grad_keys, grad_values = carry
        start_offset = block_index * block_length
        query_block = lax.dynamic_slice_in_dim(query_all, start_offset, block_length, 1)
        grad_block = lax.dynamic_slice_in_dim(grad_out_all, start_offset, block_length, 1)
        log_block = lax.dynamic_slice_in_dim(log_all, start_offset, block_length, 3)
        delta_block = lax.dynamic_slice_in_dim(delta_all, start_offset, block_length, 3)
        block_seg = lax.dynamic_slice_in_dim(seg_all, start_offset, block_length, 1)
        block_pos = start_offset + jnp.arange(block_length)
        raw_scores = (
            jnp.einsum(
                "scngd,spnd->sngcp", query_block, key_rows, preferred_element_type=jnp.float32
            )
            * 0.125
        )
        allowed = visible_mask(block_pos, block_seg, k_pos, k_seg)
        scores = jnp.where(allowed[:, None, None, :, :], raw_scores, neg_large)
        probs = jnp.exp(scores - log_block[..., None])
        grad_probs = jnp.einsum(
            "scngd,spnd->sngcp", grad_block, value_rows, preferred_element_type=jnp.float32
        )
        grad_scores = (probs * (grad_probs - delta_block[..., None])).astype(jnp.bfloat16)
        grad_values = grad_values + jnp.einsum(
            "sngcp,scngd->spnd",
            probs.astype(jnp.bfloat16),
            grad_block,
            preferred_element_type=jnp.float32,
        )
        grad_keys = (
            grad_keys
            + jnp.einsum(
                "sngcp,scngd->spnd", grad_scores, query_block, preferred_element_type=jnp.float32
            )
            * 0.125
        )
        return ((grad_keys, grad_values), None)

    start_carry = (jnp.zeros(key_rows.shape, jnp.float32), jnp.zeros(key_rows.shape, jnp.float32))
    (grad_keys, grad_values), _ = lax.scan(key_back_step, start_carry, jnp.arange(block_count))
    return (
        grad_keys.reshape(seq_count, row_count, -1),
        grad_values.reshape(seq_count, row_count, -1),
    )


def layer_forward(x_in, params, q_pos, q_seg, seg_all):
    q_weight, k_weight, v_weight, o_weight, g_weight, u_weight, d_weight, gain_one, gain_two = (
        params
    )
    seq_count, row_count, width = x_in.shape
    kv_heads = k_weight.shape[1] // HEAD_SIZE
    query_groups = q_weight.shape[1] // k_weight.shape[1]
    x_float = x_in.astype(jnp.float32)
    scale_one = lax.rsqrt(jnp.mean(x_float * x_float, axis=-1, keepdims=True) + epsilon)
    normed = (x_float * scale_one * gain_one.astype(jnp.float32)).astype(jnp.bfloat16)
    q_raw = jnp.dot(normed, q_weight, preferred_element_type=jnp.float32)
    k_raw = jnp.dot(normed, k_weight, preferred_element_type=jnp.float32)
    v_raw = jnp.dot(normed, v_weight, preferred_element_type=jnp.float32)
    q_low = rope_turn(q_raw, q_pos, 1.0).astype(jnp.bfloat16)
    k_low = rope_turn(k_raw, q_pos, 1.0).astype(jnp.bfloat16)
    v_low = v_raw.astype(jnp.bfloat16)
    keys_all, values_all = (
        lax.all_gather(k_low, "seq", axis=1, tiled=True),
        lax.all_gather(v_low, "seq", axis=1, tiled=True),
    )
    query_rows = q_low.reshape(seq_count, row_count, kv_heads, query_groups, HEAD_SIZE)
    attended, log_total = attend(query_rows, keys_all, values_all, seg_all, q_pos, q_seg)
    attn_low = attended.reshape(seq_count, row_count, -1).astype(jnp.bfloat16)
    mixed = x_float + jnp.dot(attn_low, o_weight, preferred_element_type=jnp.float32)
    scale_two = lax.rsqrt(jnp.mean(mixed * mixed, axis=-1, keepdims=True) + epsilon)
    normed_two = (mixed * scale_two * gain_two.astype(jnp.float32)).astype(jnp.bfloat16)
    gate = jnp.dot(normed_two, g_weight, preferred_element_type=jnp.float32)
    up_val = jnp.dot(normed_two, u_weight, preferred_element_type=jnp.float32)
    hidden = (jax.nn.silu(gate) * up_val).astype(jnp.bfloat16)
    result = mixed + jnp.dot(hidden, d_weight, preferred_element_type=jnp.float32)
    kept = (
        x_float,
        scale_one,
        normed,
        query_rows,
        k_low,
        v_low,
        attended,
        log_total,
        attn_low,
        mixed,
        scale_two,
        normed_two,
        gate,
        up_val,
        hidden,
    )
    return (result, kept)


def layer_back(grad_in, kept, params, q_pos, q_seg, seg_all):
    q_weight, k_weight, v_weight, o_weight, g_weight, u_weight, d_weight, gain_one, gain_two = (
        params
    )
    (
        x_float,
        scale_one,
        normed,
        query_rows,
        k_low,
        v_low,
        attended,
        log_total,
        attn_low,
        mixed,
        scale_two,
        normed_two,
        gate,
        up_val,
        hidden,
    ) = kept
    seq_count, row_count, width = x_float.shape
    grad_float = grad_in.astype(jnp.float32)
    d_hidden = jnp.einsum("scd,fd->scf", grad_in, d_weight, preferred_element_type=jnp.float32)
    sigma = jax.nn.sigmoid(gate)
    d_gate = (d_hidden * up_val * sigma * (1.0 + gate * (1.0 - sigma))).astype(jnp.bfloat16)
    d_up = (d_hidden * gate * sigma).astype(jnp.bfloat16)
    d_normed_two = jnp.einsum("scf,df->scd", d_gate, g_weight, preferred_element_type=jnp.float32)
    d_normed_two = d_normed_two + jnp.einsum(
        "scf,df->scd", d_up, u_weight, preferred_element_type=jnp.float32
    )
    grad_gain_two = jnp.sum(d_normed_two * mixed * scale_two, axis=(0, 1))
    scaled_two = d_normed_two * gain_two.astype(jnp.float32)
    d_mixed = (
        grad_float
        + scale_two * scaled_two
        - mixed * scale_two**3 * jnp.mean(scaled_two * mixed, axis=-1, keepdims=True)
    )
    d_mixed_low = d_mixed.astype(jnp.bfloat16)
    d_attn = jnp.einsum("scd,qd->scq", d_mixed_low, o_weight, preferred_element_type=jnp.float32)
    d_attn_low = d_attn.astype(jnp.bfloat16).reshape(query_rows.shape)
    delta = jnp.einsum("scngd,scngd->sngc", d_attn_low.astype(jnp.float32), attended)
    keys_all, values_all = (
        lax.all_gather(k_low, "seq", axis=1, tiled=True),
        lax.all_gather(v_low, "seq", axis=1, tiled=True),
    )
    grad_query = query_side(
        query_rows, keys_all, values_all, seg_all, q_pos, q_seg, d_attn_low, log_total, delta
    )
    query_all, grad_out_all, log_all, delta_all = (
        lax.all_gather(query_rows, "seq", axis=1, tiled=True),
        lax.all_gather(d_attn_low, "seq", axis=1, tiled=True),
        lax.all_gather(log_total.astype(jnp.bfloat16), "seq", axis=3, tiled=True).astype(
            log_total.dtype
        ),
        lax.all_gather(delta.astype(jnp.bfloat16), "seq", axis=3, tiled=True).astype(delta.dtype),
    )
    own_keys, own_values = key_side(
        query_all, grad_out_all, log_all, delta_all, seg_all, k_low, v_low, q_pos, q_seg
    )
    d_q_raw = rope_turn(grad_query.reshape(seq_count, row_count, -1), q_pos, -1.0).astype(
        jnp.bfloat16
    )
    d_k_raw = rope_turn(own_keys, q_pos, -1.0).astype(jnp.bfloat16)
    d_v_raw = own_values.astype(jnp.bfloat16)
    d_normed = jnp.einsum("scq,dq->scd", d_q_raw, q_weight, preferred_element_type=jnp.float32)
    d_normed = d_normed + jnp.einsum(
        "sck,dk->scd", d_k_raw, k_weight, preferred_element_type=jnp.float32
    )
    d_normed = d_normed + jnp.einsum(
        "sck,dk->scd", d_v_raw, v_weight, preferred_element_type=jnp.float32
    )
    grad_gain_one = jnp.sum(d_normed * x_float * scale_one, axis=(0, 1))
    scaled_one = d_normed * gain_one.astype(jnp.float32)
    grad_x = (
        d_mixed
        + scale_one * scaled_one
        - x_float * scale_one**3 * jnp.mean(scaled_one * x_float, axis=-1, keepdims=True)
    )
    factors = (
        normed,
        normed_two,
        attn_low,
        hidden,
        d_q_raw,
        d_k_raw,
        d_v_raw,
        d_gate,
        d_up,
        d_mixed_low,
        grad_in,
    )
    return (grad_x, (grad_gain_one, grad_gain_two), factors)


def owned_columns(values, fsdp_index, seq_size, fsdp_size):
    width = values.shape[-1]
    pieces = values.reshape(
        values.shape[:-1] + (seq_size, fsdp_size, width // (seq_size * fsdp_size))
    )
    chosen = lax.dynamic_index_in_dim(pieces, fsdp_index, values.ndim, keepdims=False)
    return chosen.reshape(values.shape[:-1] + (-1,))


def weight_terms(factors, fsdp_index, seq_size, fsdp_size):
    (
        normed,
        normed_two,
        attn_low,
        hidden,
        d_q_raw,
        d_k_raw,
        d_v_raw,
        d_gate,
        d_up,
        d_mixed_low,
        grad_low,
    ) = factors
    normed_cols = owned_columns(normed, fsdp_index, seq_size, fsdp_size)
    normed_two_cols = owned_columns(normed_two, fsdp_index, seq_size, fsdp_size)
    mixed_cols = owned_columns(d_mixed_low, fsdp_index, seq_size, fsdp_size)
    grad_cols = owned_columns(grad_low, fsdp_index, seq_size, fsdp_size)
    grad_query_w = jnp.einsum(
        "scd,scq->dq", normed_cols, d_q_raw, preferred_element_type=jnp.float32
    )
    grad_key_w = jnp.einsum("scd,sck->dk", normed_cols, d_k_raw, preferred_element_type=jnp.float32)
    grad_value_w = jnp.einsum(
        "scd,sck->dk", normed_cols, d_v_raw, preferred_element_type=jnp.float32
    )
    grad_out_w = jnp.einsum("scq,scd->qd", attn_low, mixed_cols, preferred_element_type=jnp.float32)
    grad_gate_w = jnp.einsum(
        "scd,scf->df", normed_two_cols, d_gate, preferred_element_type=jnp.float32
    )
    grad_up_w = jnp.einsum("scd,scf->df", normed_two_cols, d_up, preferred_element_type=jnp.float32)
    grad_down_w = jnp.einsum("scf,scd->fd", hidden, grad_cols, preferred_element_type=jnp.float32)
    return (grad_query_w, grad_key_w, grad_value_w, grad_out_w, grad_gate_w, grad_up_w, grad_down_w)


def pick(condition, left_tree, right_tree):
    return jax.tree.map(
        lambda left_arr, right_arr: jnp.where(condition, left_arr, right_arr), left_tree, right_tree
    )


def local(
    inputs,
    cotangent,
    segments,
    w_query,
    w_key,
    w_value,
    w_out,
    w_gate,
    w_up,
    w_down,
    norm_attn,
    norm_mlp,
):
    section_index = lax.axis_index("section")
    is_first = section_index == 0
    is_last = section_index == 1
    fsdp_index = lax.axis_index("fsdp")
    seq_size = lax.axis_size("seq")
    fsdp_size = lax.axis_size("fsdp")
    micro_count = inputs.shape[0]
    seq_count = inputs.shape[1]
    row_count = inputs.shape[2]
    width = inputs.shape[3]
    seg_full = lax.all_gather(segments, "seq", axis=2, tiled=True)
    q_pos = lax.axis_index("seq") * row_count + jnp.arange(row_count)
    local_shards = (
        w_query[0],
        w_key[0],
        w_value[0],
        w_out[0],
        w_gate[0],
        w_up[0],
        w_down[0],
        norm_attn[0],
        norm_mlp[0],
    )
    gathered = (
        lax.all_gather(local_shards[0], ("seq", "fsdp"), axis=0, tiled=True),
        lax.all_gather(local_shards[1], ("seq", "fsdp"), axis=0, tiled=True),
        lax.all_gather(local_shards[2], ("seq", "fsdp"), axis=0, tiled=True),
        lax.all_gather(local_shards[3], ("seq", "fsdp"), axis=1, tiled=True),
        lax.all_gather(local_shards[4], ("seq", "fsdp"), axis=0, tiled=True),
        lax.all_gather(local_shards[5], ("seq", "fsdp"), axis=0, tiled=True),
        lax.all_gather(local_shards[6], ("seq", "fsdp"), axis=1, tiled=True),
        lax.all_gather(local_shards[7], ("seq", "fsdp"), axis=0, tiled=True),
        lax.all_gather(local_shards[8], ("seq", "fsdp"), axis=0, tiled=True),
    )
    incoming = jnp.zeros((seq_count, row_count, width), jnp.bfloat16)
    sent_list = []
    kept_list = []
    for timestep in range(micro_count + 1):
        micro_index = jnp.clip(timestep - section_index, 0, micro_count - 1)
        q_seg = lax.dynamic_index_in_dim(segments, micro_index, 0, keepdims=False)
        seg_all = lax.dynamic_index_in_dim(seg_full, micro_index, 0, keepdims=False)
        x_in = jnp.where(is_first, inputs[min(timestep, micro_count - 1)], incoming)
        result, kept = layer_forward(x_in, gathered, q_pos, q_seg, seg_all)
        sent = result.astype(jnp.bfloat16)
        sent_list.append(sent)
        kept_list.append(kept)
        if timestep < micro_count:
            incoming = shifted(sent, "section", 1)
    layer_out = jnp.stack(
        [
            jnp.where(is_first, sent_list[micro], sent_list[micro + 1])
            for micro in range(micro_count)
        ]
    )
    kept_sel = [
        pick(is_first, kept_list[micro], kept_list[micro + 1]) for micro in range(micro_count)
    ]
    back_params = (
        lax.all_gather(local_shards[0], ("seq", "fsdp"), axis=0, tiled=True),
        lax.all_gather(local_shards[1], ("seq", "fsdp"), axis=0, tiled=True),
        lax.all_gather(local_shards[2], ("seq", "fsdp"), axis=0, tiled=True),
        lax.all_gather(local_shards[3], ("seq", "fsdp"), axis=1, tiled=True),
        lax.all_gather(local_shards[4], ("seq", "fsdp"), axis=0, tiled=True),
        lax.all_gather(local_shards[5], ("seq", "fsdp"), axis=0, tiled=True),
        lax.all_gather(local_shards[6], ("seq", "fsdp"), axis=1, tiled=True),
        lax.all_gather(local_shards[7], ("seq", "fsdp"), axis=0, tiled=True),
        lax.all_gather(local_shards[8], ("seq", "fsdp"), axis=0, tiled=True),
    )
    received = jnp.zeros((seq_count, row_count, width), jnp.bfloat16)
    grad_sums = None
    gain_sums = None
    back_list = []
    for timestep in range(micro_count + 1):
        micro_index = jnp.clip(timestep - 1 + section_index, 0, micro_count - 1)
        valid = jnp.where(is_last, timestep < micro_count, timestep >= 1).astype(jnp.float32)
        q_seg = lax.dynamic_index_in_dim(segments, micro_index, 0, keepdims=False)
        seg_all = lax.dynamic_index_in_dim(seg_full, micro_index, 0, keepdims=False)
        kept = pick(
            is_last, kept_sel[min(timestep, micro_count - 1)], kept_sel[max(timestep - 1, 0)]
        )
        grad_in = jnp.where(is_last, cotangent[min(timestep, micro_count - 1)], received)
        grad_x, gain_terms, factors = layer_back(grad_in, kept, back_params, q_pos, q_seg, seg_all)
        all_factors = (
            lax.all_gather(factors[0], "fsdp", axis=0, tiled=True),
            lax.all_gather(factors[1], "fsdp", axis=0, tiled=True),
            lax.all_gather(factors[2], "fsdp", axis=0, tiled=True),
            lax.all_gather(factors[3], "fsdp", axis=0, tiled=True),
            lax.all_gather(factors[4], "fsdp", axis=0, tiled=True),
            lax.all_gather(factors[5], "fsdp", axis=0, tiled=True),
            lax.all_gather(factors[6], "fsdp", axis=0, tiled=True),
            lax.all_gather(factors[7], "fsdp", axis=0, tiled=True),
            lax.all_gather(factors[8], "fsdp", axis=0, tiled=True),
            lax.all_gather(factors[9], "fsdp", axis=0, tiled=True),
            lax.all_gather(factors[10], "fsdp", axis=0, tiled=True),
        )
        grad_terms = weight_terms(all_factors, fsdp_index, seq_size, fsdp_size)
        if grad_sums is None:
            grad_sums = tuple((valid * term for term in grad_terms))
            gain_sums = tuple((valid * term for term in gain_terms))
        else:
            grad_sums = tuple((total + valid * term for total, term in zip(grad_sums, grad_terms)))
            gain_sums = tuple((total + valid * term for total, term in zip(gain_sums, gain_terms)))
        sent_back = grad_x.astype(jnp.bfloat16)
        back_list.append(sent_back)
        if timestep < micro_count:
            received = shifted(sent_back, "section", -1)
    input_grad = jnp.stack(
        [jnp.where(is_last, back_list[micro], back_list[micro + 1]) for micro in range(micro_count)]
    )
    owned = (
        lax.psum_scatter(
            grad_sums[0].astype(jnp.bfloat16), "seq", scatter_dimension=0, tiled=True
        ).astype(jnp.float32),
        lax.psum_scatter(
            grad_sums[1].astype(jnp.bfloat16), "seq", scatter_dimension=0, tiled=True
        ).astype(jnp.float32),
        lax.psum_scatter(
            grad_sums[2].astype(jnp.bfloat16), "seq", scatter_dimension=0, tiled=True
        ).astype(jnp.float32),
        lax.psum_scatter(
            grad_sums[3].astype(jnp.bfloat16), "seq", scatter_dimension=1, tiled=True
        ).astype(jnp.float32),
        lax.psum_scatter(
            grad_sums[4].astype(jnp.bfloat16), "seq", scatter_dimension=0, tiled=True
        ).astype(jnp.float32),
        lax.psum_scatter(
            grad_sums[5].astype(jnp.bfloat16), "seq", scatter_dimension=0, tiled=True
        ).astype(jnp.float32),
        lax.psum_scatter(
            grad_sums[6].astype(jnp.bfloat16), "seq", scatter_dimension=1, tiled=True
        ).astype(jnp.float32),
    )
    gains_owned = (
        lax.psum_scatter(gain_sums[0], ("seq", "fsdp"), scatter_dimension=0, tiled=True),
        lax.psum_scatter(gain_sums[1], ("seq", "fsdp"), scatter_dimension=0, tiled=True),
    )
    return (
        layer_out[None],
        input_grad[None],
        owned[0][None],
        owned[1][None],
        owned[2][None],
        owned[3][None],
        owned[4][None],
        owned[5][None],
        owned[6][None],
        gains_owned[0][None],
        gains_owned[1][None],
    )


def solution(mesh):
    return jax.shard_map(
        local,
        mesh=mesh,
        in_specs=(
            P(None, "fsdp", "seq", None),
            P(None, "fsdp", "seq", None),
            P(None, "fsdp", "seq"),
            P("section", ("seq", "fsdp"), None),
            P("section", ("seq", "fsdp"), None),
            P("section", ("seq", "fsdp"), None),
            P("section", None, ("seq", "fsdp")),
            P("section", ("seq", "fsdp"), None),
            P("section", ("seq", "fsdp"), None),
            P("section", None, ("seq", "fsdp")),
            P("section", ("seq", "fsdp")),
            P("section", ("seq", "fsdp")),
        ),
        out_specs=(
            P("section", None, "fsdp", "seq", None),
            P("section", None, "fsdp", "seq", None),
            P("section", ("seq", "fsdp"), None),
            P("section", ("seq", "fsdp"), None),
            P("section", ("seq", "fsdp"), None),
            P("section", None, ("seq", "fsdp")),
            P("section", ("seq", "fsdp"), None),
            P("section", ("seq", "fsdp"), None),
            P("section", None, ("seq", "fsdp")),
            P("section", ("seq", "fsdp")),
            P("section", ("seq", "fsdp")),
        ),
        check_vma=False,
    )
```

profile of v0, /device:TPU:1, one launch (start us, length us, event | category | flops | bytes accessed | tf_op | source)
XLA Modules:
  0.0 5440.1 jit_solution(5809436294596967941)
XLA Ops:
  11.7 37.1 all-reduce.12
  48.8 45.9 all-gather.2
  101.7 37.9 all-gather.1
  160.6 44.3 while.144
  261.2 97.2 %all-gather.171.cloned.1.call-done = bf16[1,1152,3072]{2,1,0:T(8,128)(2,1)} async-done(((bf16[1,72,3072]{2,1,0:T(8,128)(2,1)}), bf16[1,1152,3072]{2,1,0:T(8,128)(2,1)}) %all-gather.171.cloned.1.call-update) | async-done | bytes 7077904 | tf_op jit(solution)/shard_map/all_gather | solution.py:447
  369.1 91.4 %all-gather.173.cloned.1.call-done = bf16[1,1152,3072]{2,1,0:T(8,128)(2,1)} async-done(((bf16[1,72,3072]{2,1,0:T(8,128)(2,1)}), bf16[1,1152,3072]{2,1,0:T(8,128)(2,1)}) %all-gather.173.cloned.1.call-update) | async-done | bytes 7077904 | tf_op jit(solution)/shard_map/all_gather | solution.py:448
  472.3 90.4 %all-gather.175.cloned.1.call-done = bf16[1,3072,1152]{1,2,0:T(8,128)(2,1)} async-done(((bf16[1,3072,72]{1,2,0:T(8,128)(2,1)}), bf16[1,3072,1152]{1,2,0:T(8,128)(2,1)}) %all-gather.175.cloned.1.call-update) | async-done | bytes 7077904 | tf_op jit(solution)/shard_map/all_gather | solution.py:449
  608.3 43.3 while.146
  766.9 43.2 while.148
  884.8 51.6 while.150
  982.9 72.2 %while.151 = (s32[]{:T(128)}, f32[2,256,6,64]{1,3,2,0:T(8,128)S(1)}, f32[2,256,6,64]{1,3,2,0:T(8,128)S(1)}, s32[2]{0:T(128)S(1)}, bf16[2,1024,6,3,64]{1,4,3,2,0:...) while((s32[]{:T(128)}, f32[2,256,6,64]{1,3,2,0:T(8,128)S(1)}, ...), condition=%wide.region_28.29_spmd.clone, body=%wide.region_27.28_spmd.clone.sunk | while | flops 2465400576 | bytes 71843576 | solution.py:204
  1157.4 50.1 while.152
  1214.2 70.5 %while.153 = (s32[]{:T(128)}, f32[2,256,6,64]{1,3,2,0:T(8,128)S(1)}, f32[2,256,6,64]{1,3,2,0:T(8,128)S(1)}, s32[2]{0:T(128)S(1)}, bf16[2,1024,6,3,64]{1,4,3,2,0:...) while((s32[]{:T(128)}, f32[2,256,6,64]{1,3,2,0:T(8,128)S(1)}, ...), condition=%wide.region_34.35_spmd.clone, body=%wide.region_33.34_spmd.clone.sunk | while | flops 2465400576 | bytes 71843576 | solution.py:204
  1383.4 49.8 while.154
  1452.1 70.5 %while.155 = (s32[]{:T(128)}, f32[2,256,6,64]{1,3,2,0:T(8,128)S(1)}, f32[2,256,6,64]{1,3,2,0:T(8,128)S(1)}, s32[2]{0:T(128)S(1)}, bf16[2,1024,6,3,64]{1,4,3,2,0:...) while((s32[]{:T(128)}, f32[2,256,6,64]{1,3,2,0:T(8,128)S(1)}, ...), condition=%wide.region_40.41_spmd.clone, body=%wide.region_39.40_spmd.clone.sunk | while | flops 2465400576 | bytes 71843576 | solution.py:204
  1550.9 47.9 all-gather.107.cloned.1.call-done
  1605.5 82.6 %all-gather.103.cloned.1.call-done = bf16[8,256,1152]{2,1,0:T(8,128)(2,1)} async-done(((bf16[2,256,1152]{2,1,0:T(8,128)(2,1)}), bf16[8,256,1152]{2,1,0:T(8,128)(2,1)}) %all-gather.103.cloned.1.call-update) | async-done | bytes 4718608 | tf_op jit(solution)/shard_map/all_gather | solution.py:502
  1694.8 82.7 %all-gather.111.cloned.1.call-done = bf16[8,256,1152]{2,1,0:T(8,128)(2,1)} async-done(((bf16[2,256,1152]{2,1,0:T(8,128)(2,1)}), bf16[8,256,1152]{2,1,0:T(8,128)(2,1)}) %all-gather.111.cloned.1.call-update) | async-done | bytes 4718608 | tf_op jit(solution)/shard_map/all_gather | solution.py:502
  1791.5 75.4 %all-gather.147.cloned.1.call-done = bf16[8,256,1152]{2,1,0:T(8,128)(2,1)} async-done(((bf16[2,256,1152]{2,1,0:T(8,128)(2,1)}), bf16[8,256,1152]{2,1,0:T(8,128)(2,1)}) %all-gather.147.cloned.1.call-update) | async-done | bytes 4718608 | tf_op jit(solution)/shard_map/all_gather | solution.py:503
  1873.6 82.8 %all-gather.143.cloned.1.call-done = bf16[8,256,1152]{2,1,0:T(8,128)(2,1)} async-done(((bf16[2,256,1152]{2,1,0:T(8,128)(2,1)}), bf16[8,256,1152]{2,1,0:T(8,128)(2,1)}) %all-gather.143.cloned.1.call-update) | async-done | bytes 4718608 | tf_op jit(solution)/shard_map/all_gather | solution.py:503
  1963.0 82.7 %all-gather.139.cloned.1.call-done = bf16[8,256,1152]{2,1,0:T(8,128)(2,1)} async-done(((bf16[2,256,1152]{2,1,0:T(8,128)(2,1)}), bf16[8,256,1152]{2,1,0:T(8,128)(2,1)}) %all-gather.139.cloned.1.call-update) | async-done | bytes 4718608 | tf_op jit(solution)/shard_map/all_gather | solution.py:503
  2052.3 82.8 %all-gather.129.cloned.1.call-done = bf16[8,256,1152]{2,1,0:T(8,128)(2,1)} async-done(((bf16[2,256,1152]{2,1,0:T(8,128)(2,1)}), bf16[8,256,1152]{2,1,0:T(8,128)(2,1)}) %all-gather.129.cloned.1.call-update) | async-done | bytes 4718608 | tf_op jit(solution)/shard_map/all_gather | solution.py:511
  2151.5 73.1 %all-gather.127.cloned.1.call-done = bf16[8,256,1152]{2,1,0:T(8,128)(2,1)} async-done(((bf16[2,256,1152]{2,1,0:T(8,128)(2,1)}), bf16[8,256,1152]{2,1,0:T(8,128)(2,1)}) %all-gather.127.cloned.1.call-update) | async-done | bytes 4718608 | tf_op jit(solution)/shard_map/all_gather | solution.py:504
  2230.1 83.8 %all-gather.105.cloned.1.call-done = bf16[8,256,1152]{2,1,0:T(8,128)(2,1)} async-done(((bf16[2,256,1152]{2,1,0:T(8,128)(2,1)}), bf16[8,256,1152]{2,1,0:T(8,128)(2,1)}) %all-gather.105.cloned.1.call-update) | async-done | bytes 4718608 | tf_op jit(solution)/shard_map/all_gather | solution.py:506
  2319.4 84.0 %all-gather.161.cloned.1.call-done = bf16[8,256,1152]{2,1,0:T(8,128)(2,1)} async-done(((bf16[2,256,1152]{2,1,0:T(8,128)(2,1)}), bf16[8,256,1152]{2,1,0:T(8,128)(2,1)}) %all-gather.161.cloned.1.call-update) | async-done | bytes 4718608 | tf_op jit(solution)/shard_map/all_gather | solution.py:512
  2410.1 82.8 %all-gather.133.cloned.1.call-done = bf16[8,256,1152]{2,1,0:T(8,128)(2,1)} async-done(((bf16[2,256,1152]{2,1,0:T(8,128)(2,1)}), bf16[8,256,1152]{2,1,0:T(8,128)(2,1)}) %all-gather.133.cloned.1.call-update) | async-done | bytes 4718608 | tf_op jit(solution)/shard_map/all_gather | solution.py:511
  2504.8 77.4 %all-gather.131.cloned.1.call-done = bf16[8,256,1152]{2,1,0:T(8,128)(2,1)} async-done(((bf16[2,256,1152]{2,1,0:T(8,128)(2,1)}), bf16[8,256,1152]{2,1,0:T(8,128)(2,1)}) %all-gather.131.cloned.1.call-update) | async-done | bytes 4718608 | tf_op jit(solution)/shard_map/all_gather | solution.py:504
  2588.1 83.5 %all-gather.109.cloned.1.call-done = bf16[8,256,1152]{2,1,0:T(8,128)(2,1)} async-done(((bf16[2,256,1152]{2,1,0:T(8,128)(2,1)}), bf16[8,256,1152]{2,1,0:T(8,128)(2,1)}) %all-gather.109.cloned.1.call-update) | async-done | bytes 4718608 | tf_op jit(solution)/shard_map/all_gather | solution.py:506
  2711.0 35.4 all-gather.117.cloned.1.call-done
  2749.0 35.0 all-gather.121.cloned.1.call-done
  2786.6 35.0 all-gather.115.cloned.1.call-done
  2824.1 87.5 %all-gather.137.cloned.1.call-done = bf16[8,256,1152]{2,1,0:T(8,128)(2,1)} async-done(((bf16[2,256,1152]{2,1,0:T(8,128)(2,1)}), bf16[8,256,1152]{2,1,0:T(8,128)(2,1)}) %all-gather.137.cloned.1.call-update) | async-done | bytes 4718608 | tf_op jit(solution)/shard_map/all_gather | solution.py:511
  2920.9 80.1 %all-gather.135.cloned.1.call-done = bf16[8,256,1152]{2,1,0:T(8,128)(2,1)} async-done(((bf16[2,256,1152]{2,1,0:T(8,128)(2,1)}), bf16[8,256,1152]{2,1,0:T(8,128)(2,1)}) %all-gather.135.cloned.1.call-update) | async-done | bytes 4718608 | tf_op jit(solution)/shard_map/all_gather | solution.py:504
  3006.7 212.7 %all-gather.159.cloned.1.call-done = bf16[8,256,3072]{2,1,0:T(8,128)(2,1)} async-done(((bf16[2,256,3072]{2,1,0:T(8,128)(2,1)}), bf16[8,256,3072]{2,1,0:T(8,128)(2,1)}) %all-gather.159.cloned.1.call-update) | async-done | bytes 12582928 | tf_op jit(solution)/shard_map/all_gather | solution.py:505
  3229.9 78.3 %all-gather.165.cloned.1.call-done = bf16[8,256,1152]{2,1,0:T(8,128)(2,1)} async-done(((bf16[2,256,1152]{2,1,0:T(8,128)(2,1)}), bf16[8,256,1152]{2,1,0:T(8,128)(2,1)}) %all-gather.165.cloned.1.call-update) | async-done | bytes 4718608 | tf_op jit(solution)/shard_map/all_gather | solution.py:512
  3317.5 80.1 %all-gather.113.cloned.1.call-done = bf16[8,256,1152]{2,1,0:T(8,128)(2,1)} async-done(((bf16[2,256,1152]{2,1,0:T(8,128)(2,1)}), bf16[8,256,1152]{2,1,0:T(8,128)(2,1)}) %all-gather.113.cloned.1.call-update) | async-done | bytes 4718608 | tf_op jit(solution)/shard_map/all_gather | solution.py:506
  3403.3 212.6 %all-gather.163.cloned.1.call-done = bf16[8,256,3072]{2,1,0:T(8,128)(2,1)} async-done(((bf16[2,256,3072]{2,1,0:T(8,128)(2,1)}), bf16[8,256,3072]{2,1,0:T(8,128)(2,1)}) %all-gather.163.cloned.1.call-update) | async-done | bytes 12582928 | tf_op jit(solution)/shard_map/all_gather | solution.py:505
  3626.6 207.3 %all-gather.157.cloned.1.call-done = bf16[8,256,3072]{2,1,0:T(8,128)(2,1)} async-done(((bf16[2,256,3072]{2,1,0:T(8,128)(2,1)}), bf16[8,256,3072]{2,1,0:T(8,128)(2,1)}) %all-gather.157.cloned.1.call-update) | async-done | bytes 12582928 | tf_op jit(solution)/shard_map/all_gather | solution.py:505
  3924.5 202.1 %all-gather.153.cloned.1.call-done = bf16[8,256,3072]{2,1,0:T(8,128)(2,1)} async-done(((bf16[2,256,3072]{2,1,0:T(8,128)(2,1)}), bf16[8,256,3072]{2,1,0:T(8,128)(2,1)}) %all-gather.153.cloned.1.call-update) | async-done | bytes 12582928 | tf_op jit(solution)/shard_map/all_gather | solution.py:510
  4137.2 207.3 %all-gather.155.cloned.1.call-done = bf16[8,256,3072]{2,1,0:T(8,128)(2,1)} async-done(((bf16[2,256,3072]{2,1,0:T(8,128)(2,1)}), bf16[8,256,3072]{2,1,0:T(8,128)(2,1)}) %all-gather.155.cloned.1.call-update) | async-done | bytes 12582928 | tf_op jit(solution)/shard_map/all_gather | solution.py:510
  4354.9 207.5 %all-gather.151.cloned.1.call-done = bf16[8,256,3072]{2,1,0:T(8,128)(2,1)} async-done(((bf16[2,256,3072]{2,1,0:T(8,128)(2,1)}), bf16[8,256,3072]{2,1,0:T(8,128)(2,1)}) %all-gather.151.cloned.1.call-update) | async-done | bytes 12582928 | tf_op jit(solution)/shard_map/all_gather | solution.py:510
  4573.7 206.8 %all-gather.145.cloned.1.call-done = bf16[8,256,3072]{2,1,0:T(8,128)(2,1)} async-done(((bf16[2,256,3072]{2,1,0:T(8,128)(2,1)}), bf16[8,256,3072]{2,1,0:T(8,128)(2,1)}) %all-gather.145.cloned.1.call-update) | async-done | bytes 12582928 | tf_op jit(solution)/shard_map/all_gather | solution.py:509
  4789.3 209.2 %all-gather.149.cloned.1.call-done = bf16[8,256,3072]{2,1,0:T(8,128)(2,1)} async-done(((bf16[2,256,3072]{2,1,0:T(8,128)(2,1)}), bf16[8,256,3072]{2,1,0:T(8,128)(2,1)}) %all-gather.149.cloned.1.call-update) | async-done | bytes 12582928 | tf_op jit(solution)/shard_map/all_gather | solution.py:509
  5008.8 207.7 %all-gather.141.cloned.1.call-done = bf16[8,256,3072]{2,1,0:T(8,128)(2,1)} async-done(((bf16[2,256,3072]{2,1,0:T(8,128)(2,1)}), bf16[8,256,3072]{2,1,0:T(8,128)(2,1)}) %all-gather.141.cloned.1.call-update) | async-done | bytes 12582928 | tf_op jit(solution)/shard_map/all_gather | solution.py:509
  5227.7 60.9 %all-reduce.11 = (f32[1152]{0:T(1024)S(1)}, f32[1152]{0:T(1024)S(1)}) all-reduce(f32[1152]{0:T(1024)S(1)} %multiply_add_fusion.4, f32[1152]{0:T(1024)S(1)} %copy-done.169), channel_id=19, replica_groups=mesh['section'=2,'seq'=4,'fsdp'=4] {'seq','fsdp'}, use_global_device_ids=true, to_apply=%region_52.53.clone | all-reduce | flops 2304 | bytes 18432
  5325.9 34.6 reduce-scatter.34.cloned.1.call-done
  5362.4 33.5 reduce-scatter.32.cloned.1.call-done
  5398.0 33.4 reduce-scatter.30.cloned.1.call-done
  (1133 shorter events, 1592.1 us)
Async XLA Ops:
  143.3 317.2 %all-gather.173.cloned.1.call-start = ((), (), s32[]{:S(2)}) async-start(), calls=%async_computation.60 | async-start | bytes 7520256 | tf_op jit(solution)/shard_map/all_gather | solution.py:448
  143.9 418.9 %all-gather.175.cloned.1.call-start = ((), (), s32[]{:S(2)}) async-start(), calls=%async_computation.61 | async-start | bytes 7520256 | tf_op jit(solution)/shard_map/all_gather | solution.py:449
  144.6 463.7 %all-gather.73.cloned.1.call-start = ((), (), s32[]{:S(2)}) async-start(), calls=%async_computation.10 | async-start | bytes 1966080 | tf_op jit(solution)/shard_map/all_gather | solution.py:228
  861.9 295.5 %all-gather.87.cloned.1.call-start = ((), (), s32[]{:S(2)}) async-start(), calls=%async_computation.17 | async-start | bytes 1966080 | tf_op jit(solution)/shard_map/all_gather | solution.py:304
  862.4 294.9 %all-gather.89.cloned.1.call-start = ((), (), s32[]{:S(2)}) async-start(), calls=%async_computation.18 | async-start | bytes 1966080 | tf_op jit(solution)/shard_map/all_gather | solution.py:305
  863.0 351.1 %all-gather.91.cloned.1.call-start = ((), (), s32[]{:S(2)}) async-start(), calls=%async_computation.19 | async-start | bytes 5898240 | tf_op jit(solution)/shard_map/all_gather | solution.py:311
  865.3 348.9 %all-gather.93.cloned.1.call-start = ((), (), s32[]{:S(2)}) async-start(), calls=%async_computation.20 | async-start | bytes 5898240 | tf_op jit(solution)/shard_map/all_gather | solution.py:312
  1135.6 247.7 %all-gather.95.cloned.1.call-start = ((), (), s32[]{:S(2)}) async-start(), calls=%async_computation.21 | async-start | bytes 1966080 | tf_op jit(solution)/shard_map/all_gather | solution.py:304
  1136.2 247.1 %all-gather.97.cloned.1.call-start = ((), (), s32[]{:S(2)}) async-start(), calls=%async_computation.22 | async-start | bytes 1966080 | tf_op jit(solution)/shard_map/all_gather | solution.py:305
  1137.3 314.8 %all-gather.99.cloned.1.call-start = ((), (), s32[]{:S(2)}) async-start(), calls=%async_computation.23 | async-start | bytes 5898240 | tf_op jit(solution)/shard_map/all_gather | solution.py:311
  1356.2 331.9 %all-gather.103.cloned.1.call-start = ((), (), s32[]{:S(2)}) async-start(), calls=%async_computation.25 | async-start | bytes 5898240 | tf_op jit(solution)/shard_map/all_gather | solution.py:502
  1356.8 420.7 %all-gather.111.cloned.1.call-start = ((), (), s32[]{:S(2)}) async-start(), calls=%async_computation.29 | async-start | bytes 5898240 | tf_op jit(solution)/shard_map/all_gather | solution.py:502
  1357.4 509.5 %all-gather.147.cloned.1.call-start = ((), (), s32[]{:S(2)}) async-start(), calls=%async_computation.47 | async-start | bytes 5898240 | tf_op jit(solution)/shard_map/all_gather | solution.py:503
  1358.1 598.3 %all-gather.143.cloned.1.call-start = ((), (), s32[]{:S(2)}) async-start(), calls=%async_computation.45 | async-start | bytes 5898240 | tf_op jit(solution)/shard_map/all_gather | solution.py:503
  1358.9 686.8 %all-gather.139.cloned.1.call-start = ((), (), s32[]{:S(2)}) async-start(), calls=%async_computation.43 | async-start | bytes 5898240 | tf_op jit(solution)/shard_map/all_gather | solution.py:503
  1359.4 775.7 %all-gather.129.cloned.1.call-start = ((), (), s32[]{:S(2)}) async-start(), calls=%async_computation.38 | async-start | bytes 5898240 | tf_op jit(solution)/shard_map/all_gather | solution.py:511
  1360.2 864.5 %all-gather.127.cloned.1.call-start = ((), (), s32[]{:S(2)}) async-start(), calls=%async_computation.37 | async-start | bytes 5898240 | tf_op jit(solution)/shard_map/all_gather | solution.py:504
  1368.5 945.4 %all-gather.105.cloned.1.call-start = ((), (), s32[]{:S(2)}) async-start(), calls=%async_computation.26 | async-start | bytes 5898240 | tf_op jit(solution)/shard_map/all_gather | solution.py:506
  1370.0 1033.4 %all-gather.161.cloned.1.call-start = ((), (), s32[]{:S(2)}) async-start(), calls=%async_computation.54 | async-start | bytes 5898240 | tf_op jit(solution)/shard_map/all_gather | solution.py:512
  1370.8 1122.1 %all-gather.133.cloned.1.call-start = ((), (), s32[]{:S(2)}) async-start(), calls=%async_computation.40 | async-start | bytes 5898240 | tf_op jit(solution)/shard_map/all_gather | solution.py:511
  1371.5 1210.7 %all-gather.131.cloned.1.call-start = ((), (), s32[]{:S(2)}) async-start(), calls=%async_computation.39 | async-start | bytes 5898240 | tf_op jit(solution)/shard_map/all_gather | solution.py:504
  1372.1 1299.4 %all-gather.109.cloned.1.call-start = ((), (), s32[]{:S(2)}) async-start(), calls=%async_computation.28 | async-start | bytes 5898240 | tf_op jit(solution)/shard_map/all_gather | solution.py:506
  1373.6 1334.9 %all-gather.123.cloned.1.call-start = ((), (), s32[]{:S(2)}) async-start(), calls=%async_computation.35 | async-start | bytes 1966080 | tf_op jit(solution)/shard_map/all_gather | solution.py:508
  1374.6 1371.9 %all-gather.117.cloned.1.call-start = ((), (), s32[]{:S(2)}) async-start(), calls=%async_computation.32 | async-start | bytes 1966080 | tf_op jit(solution)/shard_map/all_gather | solution.py:507
  1375.6 1408.4 %all-gather.121.cloned.1.call-start = ((), (), s32[]{:S(2)}) async-start(), calls=%async_computation.34 | async-start | bytes 1966080 | tf_op jit(solution)/shard_map/all_gather | solution.py:508
  1376.6 1445.0 %all-gather.115.cloned.1.call-start = ((), (), s32[]{:S(2)}) async-start(), calls=%async_computation.31 | async-start | bytes 1966080 | tf_op jit(solution)/shard_map/all_gather | solution.py:507
  1377.6 1534.0 %all-gather.137.cloned.1.call-start = ((), (), s32[]{:S(2)}) async-start(), calls=%async_computation.42 | async-start | bytes 5898240 | tf_op jit(solution)/shard_map/all_gather | solution.py:511
  1378.4 1622.6 %all-gather.135.cloned.1.call-start = ((), (), s32[]{:S(2)}) async-start(), calls=%async_computation.41 | async-start | bytes 5898240 | tf_op jit(solution)/shard_map/all_gather | solution.py:504
  1379.0 1840.4 %all-gather.159.cloned.1.call-start = ((), (), s32[]{:S(2)}) async-start(), calls=%async_computation.53 | async-start | bytes 15728640 | tf_op jit(solution)/shard_map/all_gather | solution.py:505
  1379.7 1928.5 %all-gather.165.cloned.1.call-start = ((), (), s32[]{:S(2)}) async-start(), calls=%async_computation.56 | async-start | bytes 5898240 | tf_op jit(solution)/shard_map/all_gather | solution.py:512
  1383.3 2014.4 %all-gather.113.cloned.1.call-start = ((), (), s32[]{:S(2)}) async-start(), calls=%async_computation.30 | async-start | bytes 5898240 | tf_op jit(solution)/shard_map/all_gather | solution.py:506
  1436.8 2179.1 %all-gather.163.cloned.1.call-start = ((), (), s32[]{:S(2)}) async-start(), calls=%async_computation.55 | async-start | bytes 15728640 | tf_op jit(solution)/shard_map/all_gather | solution.py:505
  1437.4 2396.4 %all-gather.157.cloned.1.call-start = ((), (), s32[]{:S(2)}) async-start(), calls=%async_computation.52 | async-start | bytes 15728640 | tf_op jit(solution)/shard_map/all_gather | solution.py:505
  1438.0 2432.1 %all-gather.125.cloned.1.call-start = ((), (), s32[]{:S(2)}) async-start(), calls=%async_computation.36 | async-start | bytes 1966080 | tf_op jit(solution)/shard_map/all_gather | solution.py:508
  1523.6 2384.1 %all-gather.119.cloned.1.call-start = ((), (), s32[]{:S(2)}) async-start(), calls=%async_computation.33 | async-start | bytes 1966080 | tf_op jit(solution)/shard_map/all_gather | solution.py:507
  1524.8 2601.7 %all-gather.153.cloned.1.call-start = ((), (), s32[]{:S(2)}) async-start(), calls=%async_computation.50 | async-start | bytes 15728640 | tf_op jit(solution)/shard_map/all_gather | solution.py:510
  1525.4 2819.2 %all-gather.155.cloned.1.call-start = ((), (), s32[]{:S(2)}) async-start(), calls=%async_computation.51 | async-start | bytes 15728640 | tf_op jit(solution)/shard_map/all_gather | solution.py:510
  1526.1 3036.3 %all-gather.151.cloned.1.call-start = ((), (), s32[]{:S(2)}) async-start(), calls=%async_computation.49 | async-start | bytes 15728640 | tf_op jit(solution)/shard_map/all_gather | solution.py:510
  1526.7 3253.8 %all-gather.145.cloned.1.call-start = ((), (), s32[]{:S(2)}) async-start(), calls=%async_computation.46 | async-start | bytes 15728640 | tf_op jit(solution)/shard_map/all_gather | solution.py:509
  1527.4 3471.0 %all-gather.149.cloned.1.call-start = ((), (), s32[]{:S(2)}) async-start(), calls=%async_computation.48 | async-start | bytes 15728640 | tf_op jit(solution)/shard_map/all_gather | solution.py:509
  1528.2 3688.3 %all-gather.141.cloned.1.call-start = ((), (), s32[]{:S(2)}) async-start(), calls=%async_computation.44 | async-start | bytes 15728640 | tf_op jit(solution)/shard_map/all_gather | solution.py:509
  1528.9 3762.5 %reduce-scatter.28.cloned.1.call-start = ((), (), s32[]{:S(2)}) async-start(), calls=%async_computation.66 | async-start | bytes 829440
  3006.7 2286.4 %reduce-scatter.22.cloned.1.call-start = ((), (), s32[]{:S(2)}) async-start(), calls=%async_computation.63 | async-start | bytes 829440
  3403.3 1894.2 %reduce-scatter.26.cloned.1.call-start = ((), (), s32[]{:S(2)}) async-start(), calls=%async_computation.65 | async-start | bytes 276480
  3873.4 1451.0 %reduce-scatter.24.cloned.1.call-start = ((), (), s32[]{:S(2)}) async-start(), calls=%async_computation.64 | async-start | bytes 276480
  3910.9 1449.5 %reduce-scatter.34.cloned.1.call-start = ((), (), s32[]{:S(2)}) async-start(), calls=%async_computation.69 | async-start | bytes 2211840
  3916.7 1479.3 %reduce-scatter.32.cloned.1.call-start = ((), (), s32[]{:S(2)}) async-start(), calls=%async_computation.68 | async-start | bytes 2211840
  4573.6 857.7 %reduce-scatter.30.cloned.1.call-start = ((), (), s32[]{:S(2)}) async-start(), calls=%async_computation.67 | async-start | bytes 2211840
  (237 other events, 7383.4 us)
Sparse Core Ops, SparseCore 0:
  10.7 72.2 all-gather.166
  101.8 43.3 all-gather.68
  147.1 42.2 all-gather.66
  191.9 63.8 all-gather.168
  258.4 99.9 all-gather.170
  361.0 99.4 all-gather.172
  463.2 99.4 all-gather.174
  866.4 57.7 all-gather.82
  925.8 56.9 all-gather.84
  1050.0 56.8 all-gather.90
  1135.7 58.2 all-gather.92
  1303.1 56.4 all-gather.98
  1361.4 56.9 all-gather.100
  1419.8 89.4 all-gather.176
  1510.9 87.8 all-gather.106
  1600.2 87.8 all-gather.102
  1689.5 87.8 all-gather.110
  1779.0 87.8 all-gather.146
  1868.5 87.8 all-gather.142
  1957.8 87.8 all-gather.138
  2047.3 87.8 all-gather.128
  2136.7 87.8 all-gather.126
  2226.1 87.8 all-gather.104
  2315.5 87.8 all-gather.160
  2405.0 87.8 all-gather.132
  2494.3 87.8 all-gather.130
  2583.6 87.8 all-gather.108
  2673.1 35.3 all-gather.122
  2710.5 35.9 all-gather.116
  2748.0 35.9 all-gather.120
  2785.6 35.9 all-gather.114
  2823.2 88.4 all-gather.136
  2913.1 87.8 all-gather.134
  3002.5 216.7 all-gather.158
  3220.8 87.3 all-gather.164
  3309.6 87.9 all-gather.112
  3399.0 216.7 all-gather.162
  3617.3 216.4 all-gather.156
  3835.3 34.8 all-gather.124
  3871.7 35.9 all-gather.118
  3909.1 217.3 all-gather.152
  4128.1 216.3 all-gather.154
  4345.9 216.3 all-gather.150
  4563.9 216.4 all-gather.144
  4782.0 216.3 all-gather.148
  5000.0 216.3 all-gather.140
  5327.4 32.9 reduce-scatter.33
  5363.5 32.4 reduce-scatter.31
  (15 shorter events, 434.5 us)
where the time goes:
time: 5450 us; the launch traced here: 5440 us
  waiting for transfers between devices  3920 us (72%)
  matrix products  826 us (15%)
  blocking collectives  227 us (4%)
  local copies, waits for them, and re-layouts  224 us (4%)
  other arithmetic  192 us (4%)
    all_gather x3, waiting for transfers between devices, local(): lax.all_gather(factors[3], 'fsdp', axis=0, tiled=True)  632 us
    all_gather x3, waiting for transfers between devices, local(): lax.all_gather(factors[7], 'fsdp', axis=0, tiled=True)  624 us
    all_gather x3, waiting for transfers between devices, local(): lax.all_gather(factors[8], 'fsdp', axis=0, tiled=True)  617 us
    all_gather x3, waiting for transfers between devices, local(): lax.all_gather(factors[9], 'fsdp', axis=0, tiled=True)  253 us
    all_gather x3, waiting for transfers between devices, local(): lax.all_gather(factors[4], 'fsdp', axis=0, tiled=True)  247 us
    all_gather x3, waiting for transfers between devices, local(): lax.all_gather(factors[1], 'fsdp', axis=0, tiled=True)  241 us
    all_gather x3, waiting for transfers between devices, local(): lax.all_gather(factors[2], 'fsdp', axis=0, tiled=True)  231 us
    all_gather x3, waiting for transfers between devices, local(): lax.all_gather(factors[0], 'fsdp', axis=0, tiled=True)  213 us
  transfers between devices with their start and end apart: 67, of which 46 were waited for; matrix products, arithmetic and copies ran while one was open for 21% of the time, Pallas kernels for 0%

commit v1 on v0

v1 whole, which is shorter than its diff:
```python
import functools

import jax
import jax.numpy as jnp
from jax import lax
from jax.experimental import pallas as pl
from jax.experimental.pallas import tpu as pltpu
from jax.sharding import PartitionSpec as P

HEAD = 64
PAIR = 2 * HEAD
EPSILON = 1e-05
ROPE_BASE = 10000.0
NEG = -1e30
GAIN_COLS = 64
LARGE = pl.CostEstimate(flops=1 << 34, bytes_accessed=1024, transcendentals=0)
SMALL = pl.CostEstimate(flops=1024, bytes_accessed=1024, transcendentals=0)
BF16 = jnp.bfloat16
F32 = jnp.float32
NT = (((1,), (1,)), ((), ()))
TN = (((0,), (0,)), ((), ()))
NN = (((1,), (0,)), ((), ()))


def dot(left, right, dims=NN):
    return lax.dot_general(left, right, dims, preferred_element_type=F32)


def swap_halves(value):
    lane = lax.broadcasted_iota(jnp.int32, value.shape, 1)
    ahead = pltpu.roll(value, PAIR - HEAD // 2, 1)
    behind = pltpu.roll(value, HEAD // 2, 1)
    return jnp.where(lane % HEAD < HEAD // 2, ahead, behind)


def rope_tables(positions):
    half = HEAD // 2
    frequency = ROPE_BASE ** (-2.0 * jnp.arange(half, dtype=F32) / HEAD)
    angles = positions.astype(F32)[:, None] * frequency[None, :]
    cosine, sine = jnp.cos(angles), jnp.sin(angles)
    return (
        jnp.concatenate([cosine] * 4, axis=1),
        jnp.concatenate([-sine, sine, -sine, sine], axis=1),
    )


def head_slots(ref, kinds, cos_ref, sin_ref, places, block):
    rows = ref.shape[0]

    def step(i, carry):
        at = pl.ds(pl.multiple_of(i * block, block), block)
        cosine, sine = cos_ref[at, :], sin_ref[at, :]
        for low in range(0, len(kinds), 2):
            pair = range(low, min(low + 2, len(kinds)))
            raw = ref[at, low * HEAD : (pair[-1] + 1) * HEAD].astype(F32)
            if len(pair) == 1:
                raw = jnp.concatenate([raw, raw], axis=1)
            turned = raw
            if any(kinds[slot] != "v" for slot in pair):
                turned = raw * cosine + swap_halves(raw) * sine
            for slot in pair:
                kind = kinds[slot]
                value = raw if kind == "v" else turned
                value = value[:, (slot - low) * HEAD : (slot - low + 1) * HEAD]
                if kind == "q":
                    value = value * 0.125
                dest, index = places[slot]
                dest[index, at, :] = value.astype(BF16)
        return carry

    lax.fori_loop(0, rows // block, step, 0)


def forward_kernel(hq, hk, same, *refs):
    if same:
        q_ref, cosq, sinq, segq, posq, segk, o_ref, qh, kvh, lse_ref, bias, oh, lsec = refs
    else:
        q_ref, kv_ref, cosq, sinq, cosk, sink, segq, posq, segk = refs[:9]
        o_ref, qh, kvh, lse_ref, bias, oh, lsec = refs[9:]
    rows, keys = bias.shape
    block = min(256, rows)
    count = rows // block
    group = hq // hk
    q_kinds, q_places = ["q"] * hq, [(qh, i) for i in range(hq)]
    kv_kinds = ["k"] * hk + ["v"] * hk
    kv_places = [(kvh, i) for i in range(2 * hk)]
    if same:
        head_slots(q_ref, q_kinds + kv_kinds, cosq, sinq, q_places + kv_places, block)
    else:
        head_slots(q_ref, q_kinds, cosq, sinq, q_places, block)
        head_slots(kv_ref, kv_kinds, cosk, sink, kv_places, block)
    for i in range(count):
        at = slice(i * block, (i + 1) * block)
        width = (i + 1) * block if same else keys
        seg_q, pos_q = segq[at, :], posq[at, :]
        seg_k = segk[:, :width]
        pos_k = lax.broadcasted_iota(jnp.int32, (block, width), 1)
        seen = (seg_q == seg_k) & (pos_k <= pos_q) & ((seg_q != 0) | (pos_k == pos_q))
        bias[at, :width] = jnp.where(seen, 0.0, NEG)

    def one_head(h, carry):
        g = lax.div(h, group)
        for i in range(count):
            at = slice(i * block, (i + 1) * block)
            width = (i + 1) * block if same else keys
            scores = dot(qh[h, at, :], kvh[g, :width, :], NT) + bias[at, :width]
            top = jnp.max(scores, axis=1, keepdims=True)
            probs = jnp.exp(scores - top)
            mass = jnp.sum(probs, axis=1, keepdims=True)
            summed = dot(probs.astype(BF16), kvh[hk + g, :width, :])
            oh[h, at, :] = summed / mass
            lane = lax.broadcasted_iota(jnp.int32, (block, 128), 1)
            lsec[at, :] = jnp.where(lane == h, top + jnp.log(mass), lsec[at, :])
        return carry

    lsec[...] = jnp.zeros_like(lsec)
    lax.fori_loop(0, hq, one_head, 0)
    for low in range(0, hq, 2):
        pair = [oh[slot] for slot in range(low, min(low + 2, hq))]
        value = jnp.concatenate(pair, axis=1) if len(pair) == 2 else pair[0]
        o_ref[:, low * HEAD : low * HEAD + value.shape[1]] = value.astype(BF16)
    lse_ref[...] = jnp.transpose(lsec[...])[: lse_ref.shape[0], :]


def unturn(heads, ref, cosine, sine, kinds, block):
    rows = ref.shape[0]

    def step(i, carry):
        at = pl.ds(pl.multiple_of(i * block, block), block)
        cos_part, sin_part = cosine[at, :], sine[at, :]
        for low in range(0, len(kinds), 2):
            pair = range(low, min(low + 2, len(kinds)))
            pieces = [heads[slot][0][heads[slot][1], at, :] for slot in pair]
            raw = jnp.concatenate(pieces if len(pieces) == 2 else pieces * 2, axis=1)
            if kinds[low] != "v":
                turned = raw * cos_part - swap_halves(raw) * sin_part
                if kinds[pair[-1]] == "v":
                    lane = lax.broadcasted_iota(jnp.int32, raw.shape, 1)
                    turned = jnp.where(lane < HEAD, turned, raw)
                raw = turned
            width = len(pieces) * HEAD
            ref[at, low * HEAD : low * HEAD + width] = raw[:, :width].astype(ref.dtype)
        return carry

    lax.fori_loop(0, rows // block, step, 0)


def backward_kernel(hq, hk, same, *refs):
    if same:
        qh, kvh, do_ref, o_ref, lse_ref, cosq, sinq, segq, posq, segk, w_ref = refs[:11]
        dqkv_ref, own_ref, bias, doh, delta, dqs, dks, dvs = refs[11:]
    else:
        qh, kvh, do_ref, o_ref, lse_ref = refs[:5]
        cosq, sinq, cosk, sink, segq, posq, segk = refs[5:12]
        dq_ref, dkv_ref, bias, doh, delta, dqs, dks, dvs = refs[12:]
    keys, rows = bias.shape
    block = min(256, rows)
    count = rows // block
    group = hq // hk
    for i in range(count):
        at = slice(i * block, (i + 1) * block)
        width = (i + 1) * block if same else keys
        seg_q, pos_q = segq[:, at], posq[:, at]
        seg_k = segk[:width, :]
        pos_k = lax.broadcasted_iota(jnp.int32, (width, block), 0)
        seen = (seg_q == seg_k) & (pos_k <= pos_q) & ((seg_q != 0) | (pos_k == pos_q))
        bias[:width, at] = jnp.where(seen, 0.0, NEG)
    for h in range(hq):
        doh[h] = do_ref[:, h * HEAD : (h + 1) * HEAD]
    wide = do_ref.shape[1]
    marks = lax.broadcasted_iota(jnp.int32, (delta.shape[0], wide), 1) // HEAD
    marks = (marks == lax.broadcasted_iota(jnp.int32, marks.shape, 0)).astype(F32)
    products = do_ref[...].astype(F32) * o_ref[...].astype(F32)
    delta[...] = lax.dot_general(
        marks, products, NT, precision=lax.Precision.HIGHEST, preferred_element_type=F32
    )

    def one_group(g, carry):
        dks[g] = jnp.zeros(dks.shape[1:], F32)
        dvs[g] = jnp.zeros(dvs.shape[1:], F32)

        def one_head(j, inner):
            h = g * group + j
            for i in range(count):
                at = slice(i * block, (i + 1) * block)
                width = (i + 1) * block if same else keys
                query, grad = qh[h, at, :], doh[h, at, :]
                key, value = kvh[g, :width, :], kvh[hk + g, :width, :]
                scores = dot(key, query, NT) + bias[:width, at]
                probs = jnp.exp(scores - lse_ref[pl.ds(h, 1), at])
                grad_probs = dot(value, grad, NT)
                grad_scores = (probs * (grad_probs - delta[pl.ds(h, 1), at])).astype(BF16)
                dvs[g, :width, :] += dot(probs.astype(BF16), grad)
                dks[g, :width, :] += dot(grad_scores, query)
                dqs[h, at, :] = dot(grad_scores, key, TN) * 0.125
            return inner

        lax.fori_loop(0, group, one_head, 0)
        return carry

    lax.fori_loop(0, hk, one_group, 0)
    q_heads = [(dqs, i) for i in range(hq)]
    kv_heads = [(dks, i) for i in range(hk)] + [(dvs, i) for i in range(hk)]
    kinds = ["k"] * hk + ["v"] * hk
    if same:
        unturn(q_heads + kv_heads, dqkv_ref, cosq, sinq, ["q"] * hq + kinds, block)

        def project(i, carry):
            at = pl.ds(pl.multiple_of(i * block, block), block)
            weight = w_ref[:, : dqkv_ref.shape[1]]
            own_ref[at, :] = dot(dqkv_ref[at, :], weight, NT).astype(BF16)
            return carry

        lax.fori_loop(0, count, project, 0)
    else:
        unturn(q_heads, dq_ref, cosq, sinq, ["q"] * hq, block)
        unturn(kv_heads, dkv_ref, cosk, sink, kinds, block)


def whole(value):
    zeros = (0,) * len(value.shape)
    return pl.BlockSpec(value.shape, lambda i: zeros, pipeline_mode=pl.Buffered(1))


def in_hbm(arrays):
    return [pltpu.with_memory_space_constraint(value, pltpu.HBM) for value in arrays]


def attention_forward(qkv, plan):
    hq, hk, same = plan["hq"], plan["hk"], plan["same"]
    rows = qkv.shape[0]
    if same:
        keys = rows
        args = [qkv, *plan["tables_q"], plan["seg_q_col"], plan["pos_q_col"], plan["seg_k_row"]]
    else:
        kv_all = plan["gather"](qkv[:, hq * HEAD :])
        keys = kv_all.shape[0]
        args = [qkv[:, : hq * HEAD], kv_all, *plan["tables_q"], *plan["tables_k"]]
        args += [plan["seg_q_col"], plan["pos_q_col"], plan["seg_k_row"]]
    lines = -(-hq // 8) * 8
    out_shape = (
        pltpu.HBM((rows, hq * HEAD), BF16),
        pltpu.HBM((hq, rows, HEAD), BF16),
        pltpu.HBM((2 * hk, keys, HEAD), BF16),
        pltpu.HBM((lines, rows), F32),
    )
    return pl.pallas_call(
        functools.partial(forward_kernel, hq, hk, same),
        out_shape=out_shape,
        grid=(1,),
        in_specs=[whole(value) for value in args],
        out_specs=[whole(value) for value in out_shape],
        scratch_shapes=[
            pltpu.VMEM((rows, keys), F32),
            pltpu.VMEM((hq, rows, HEAD), F32),
            pltpu.VMEM((rows, 128), F32),
        ],
        compiler_params=pltpu.CompilerParams(vmem_limit_bytes=30 * 2**20),
        cost_estimate=SMALL,
    )(*in_hbm(args))


def attention_backward(kept, d_out, w_attn, qkv_cols, plan):
    hq, hk, same = plan["hq"], plan["hk"], plan["same"]
    out, qh, kvh, lse = kept
    rows, keys = out.shape[0], kvh.shape[1]
    args = [qh, kvh, d_out, out, lse, *plan["tables_q"]]
    if not same:
        args += list(plan["tables_k"])
    args += [plan["seg_q_row"], plan["pos_q_row"], plan["seg_k_col"]]
    if same:
        args.append(w_attn)
        out_shape = (
            pltpu.HBM((rows, qkv_cols), BF16),
            jax.ShapeDtypeStruct((rows, w_attn.shape[0]), BF16),
        )
    else:
        out_shape = (
            jax.ShapeDtypeStruct((rows, hq * HEAD), BF16),
            jax.ShapeDtypeStruct((keys, 2 * hk * HEAD), F32),
        )
    result = pl.pallas_call(
        functools.partial(backward_kernel, hq, hk, same),
        out_shape=out_shape,
        grid=(1,),
        in_specs=[whole(value) for value in args],
        out_specs=[whole(value) for value in out_shape],
        scratch_shapes=[
            pltpu.VMEM((keys, rows), F32),
            pltpu.VMEM((hq, rows, HEAD), BF16),
            pltpu.VMEM((lse.shape[0], rows), F32),
            pltpu.VMEM((hq, rows, HEAD), F32),
            pltpu.VMEM((hk, keys, HEAD), F32),
            pltpu.VMEM((hk, keys, HEAD), F32),
        ],
        compiler_params=pltpu.CompilerParams(vmem_limit_bytes=40 * 2**20),
        cost_estimate=SMALL,
    )(*in_hbm(args))
    if same:
        return result
    d_kv = plan["scatter"](result[1]).astype(BF16)
    d_qkv = jnp.concatenate([result[0], d_kv], axis=1)
    return d_qkv, dot(d_qkv, w_attn[:, :qkv_cols], NT).astype(BF16)


def other_core(value):
    return lax.ppermute(value, "section", [(0, 1), (1, 0)])


def place(buffer, block, index):
    return lax.dynamic_update_index_in_dim(buffer, block, index, 0)


def pick(blocks, index):
    return lax.dynamic_index_in_dim(blocks, index, 0, False)


def flip(value, axis, step, group=None):
    size = group or lax.axis_size(axis)
    pairs = [(i, i - i % size + (i % size ^ step)) for i in range(lax.axis_size(axis))]
    return lax.ppermute(value, axis, pairs)


class Return:
    def __init__(self, first, second, places, core, parts, pinned=False):
        self.places, self.core, self.parts = places, core, parts
        self.received = in_hbm if pinned else list
        self.blocks = [v.reshape(2 * parts, -1, v.shape[1]) for v in (first, second)]
        to_x, to_y = self.packed(((1, 0), (3, 0)), ((2, 1), (3, 1)))
        self.near = [flip(to_x, "seq", 1, parts), flip(to_y, "seq", 2, parts)]

    def packed(self, *sends):
        rows, width = self.blocks[0].shape[1:]
        half = rows // 2

        def body(places_ref, core_ref, *refs):
            source, outs = iter(refs[: len(ins)]), refs[len(ins) :]
            for send, out in zip(sends, outs):
                for i, block in enumerate(send):
                    if isinstance(block[0], int):
                        first, second = next(source), next(source)
                        out[i] = jnp.where(core_ref[0] == 0, first[0], second[0])
                    else:
                        out[i] = next(source)[0]

        ins, in_specs = [], []
        for send in sends:
            for place_index, part in send:
                if isinstance(place_index, int):
                    ins += self.blocks

                    def index(i, o, c, place_index=place_index, part=part):
                        return (2 * o[place_index] + part, i, 0)

                    in_specs += [pl.BlockSpec((1, half, width), index)] * 2
                else:
                    ins += self.received([place_index])

                    def index(i, o, c, part=part):
                        return (part, i, 0)

                    in_specs.append(pl.BlockSpec((1, half, width), index))
        return pl.pallas_call(
            body,
            out_shape=[jax.ShapeDtypeStruct((len(send), rows, width), BF16) for send in sends],
            grid_spec=pltpu.PrefetchScalarGridSpec(
                num_scalar_prefetch=2,
                grid=(2,),
                in_specs=in_specs,
                out_specs=[
                    pl.BlockSpec((len(send), half, width), lambda i, o, c: (0, i, 0))
                    for send in sends
                ],
            ),
            compiler_params=pltpu.CompilerParams(vmem_limit_bytes=8 * 2**20),
            cost_estimate=SMALL,
        )(self.places, self.core, *ins)

    def onward(self):
        near_x, near_y = self.near
        to_y, to_x = self.packed(((2, 0), (near_x, 1)), ((1, 1), (near_y, 1)))
        self.far = [flip(to_y, "seq", 2, self.parts), flip(to_x, "seq", 1, self.parts)]

    def placed(self):
        near_x, near_y = self.near
        far_y, far_x = self.far
        rows, width = self.blocks[0].shape[1:]
        half, parts = rows // 2, self.parts

        def body(places_ref, core_ref, first_a, second_a, first_b, second_b, nx, ny, fy, fx, out):
            mine = core_ref[0] == 0
            out[2 * places_ref[0]] = jnp.where(mine, first_a[0], second_a[0])
            out[2 * places_ref[0] + 1] = jnp.where(mine, first_b[0], second_b[0])
            out[2 * places_ref[1]] = nx[0]
            out[2 * places_ref[1] + 1] = fx[0]
            out[2 * places_ref[2]] = fy[0]
            out[2 * places_ref[2] + 1] = ny[0]
            out[2 * places_ref[3]] = fy[1]
            out[2 * places_ref[3] + 1] = fx[1]

        def own(part):
            return pl.BlockSpec((1, half, width), lambda i, o, c: (2 * o[0] + part, i, 0))

        def spec(count):
            return pl.BlockSpec((count, half, width), lambda i, o, c: (0, i, 0))

        result = pl.pallas_call(
            body,
            out_shape=jax.ShapeDtypeStruct((2 * parts, rows, width), BF16),
            grid_spec=pltpu.PrefetchScalarGridSpec(
                num_scalar_prefetch=2,
                grid=(2,),
                in_specs=[own(0), own(0), own(1), own(1), spec(1), spec(1), spec(2), spec(2)],
                out_specs=spec(2 * parts),
            ),
            compiler_params=pltpu.CompilerParams(vmem_limit_bytes=12 * 2**20),
            cost_estimate=SMALL,
        )(
            self.places,
            self.core,
            *self.blocks,
            *self.blocks,
            *self.received((near_x, near_y, far_y, far_x)),
        )
        return result.reshape(parts, 2 * rows, width)


ANY = pl.BlockSpec(memory_space=pl.ANY)
VMEM = pl.BlockSpec(memory_space=pltpu.VMEM)


def shapes_of(arrays, pinned=()):
    kinds = [jax.ShapeDtypeStruct] * len(arrays) + [pltpu.HBM] * len(pinned)
    return [kind(v.shape, v.dtype) for kind, v in zip(kinds, (*arrays, *pinned))]


def hold(*arrays, pinned=()):
    def body(*refs):
        pass

    count = len(arrays) + len(pinned)
    return pl.pallas_call(
        body,
        out_shape=shapes_of(arrays, pinned),
        in_specs=[ANY] * count,
        out_specs=[ANY] * count,
        input_output_aliases={i: i for i in range(count)},
        compiler_params=pltpu.CompilerParams(vmem_limit_bytes=2**20),
        cost_estimate=SMALL,
    )(*arrays, *in_hbm(pinned))


def assemble(order, column, by_x, by_y, far_low, far_high, held, pinned):
    def body(order_ref, col, bx, by, low, high, *refs):
        out = refs[count]
        for i, source in enumerate((col, bx, by)):
            out[pl.ds(2 * order_ref[i], 2)] = source[...]
        out[2 * order_ref[3]] = low[...]
        out[2 * order_ref[3] + 1] = high[...]

    half, cols = column.shape[1:]
    rows = half // 3
    count = len(held) + len(pinned)

    def spec(count):
        return pl.BlockSpec((count, rows, cols), lambda i, o: (0, i, 0))

    single = pl.BlockSpec((rows, cols), lambda i, o: (i, 0))
    result = pl.pallas_call(
        body,
        out_shape=[jax.ShapeDtypeStruct((8, half, cols), column.dtype)]
        + shapes_of(held, pinned),
        grid_spec=pltpu.PrefetchScalarGridSpec(
            num_scalar_prefetch=1,
            grid=(3,),
            in_specs=[spec(2)] * 3 + [single] * 2 + [ANY] * count,
            out_specs=[spec(8)] + [ANY] * count,
        ),
        input_output_aliases={6 + i: 1 + i for i in range(count)},
        compiler_params=pltpu.CompilerParams(vmem_limit_bytes=16 * 2**20),
        cost_estimate=SMALL,
    )(order, column, by_x, by_y, far_low, far_high, *held, *in_hbm(pinned))
    return (result[0].reshape(8 * half, cols), *result[1:])


def gradient_chunk(d_qkv, attended, columns, scales):
    tokens, width = columns[0].shape
    first, last = d_qkv.shape[1], attended.shape[1]
    offset = first + GAIN_COLS
    rows = width // 3

    def body(d_ref, o_ref, a_ref, m_ref, own_a, val_a, own_b, val_b, r_a, r_b, out_ref):
        out_ref[:, :first] = dot(a_ref[...], d_ref[...], TN).astype(BF16)
        lane = lax.broadcasted_iota(jnp.int32, (tokens, GAIN_COLS), 1)
        gains = jnp.zeros((rows, GAIN_COLS), F32)
        for i, (own, val, r) in enumerate(((own_a, val_a, r_a), (own_b, val_b, r_b))):
            product = own[...].astype(F32) * val[...].astype(F32) * r[...]
            unit = jnp.where(lane == i, 1.0, 0.0).astype(BF16)
            gains += dot(product.astype(BF16), unit, TN)
        out_ref[:, first:offset] = gains.astype(BF16)
        out_ref[:, offset:] = dot(m_ref[...], o_ref[...], TN).astype(BF16)

    def part(cols):
        return pl.BlockSpec((tokens, cols), lambda i: (0, 0))

    block = pl.BlockSpec((tokens, rows), lambda i: (0, i))
    return pl.pallas_call(
        body,
        out_shape=pltpu.HBM((width, offset + last), BF16),
        grid=(3,),
        in_specs=[part(first), part(last)] + [block] * 6 + [part(1)] * 2,
        out_specs=pl.BlockSpec((rows, offset + last), lambda i: (i, 0)),
        compiler_params=pltpu.CompilerParams(vmem_limit_bytes=36 * 2**20),
        cost_estimate=LARGE,
    )(*in_hbm((d_qkv, attended, *columns, *scales)))


def norm_back(own, other, value, scale, gain, added, weight=None):
    tokens, width = own.shape
    rows = min(256, tokens)
    low, cols = (weight[1], weight[0].shape[1] - weight[1]) if weight else (0, 0)

    def body(own_ref, other_ref, value_ref, scale_ref, gain_ref, added_ref, *refs):
        grad = (own_ref[...].astype(F32) + other_ref[...].astype(F32)) * gain_ref[...]
        val, r = value_ref[...].astype(F32), scale_ref[...]
        mean = jnp.sum(grad * val, axis=1, keepdims=True) * (1.0 / width)
        result = added_ref[...].astype(F32) + r * grad - val * (r * r * r * mean)
        result = result.astype(BF16)
        refs[-2 if weight else -1][...] = result
        if weight:
            refs[-1][...] = dot(result, refs[0][:, low:]).astype(BF16)

    block = pl.BlockSpec((rows, width), lambda i: (i, 0))
    scales = pl.BlockSpec((rows, 1), lambda i: (i, 0))
    ins = [own, other, value, scale, gain[None, :], added]
    in_specs = [block, block, block, scales, pl.BlockSpec((1, width), lambda i: (0, 0)), block]
    out_shape, out_specs = [pltpu.HBM((tokens, width), BF16)], [block]
    if weight:
        ins.append(weight[0])
        in_specs.append(pl.BlockSpec(weight[0].shape, lambda i: (0, 0)))
        out_shape.append(pltpu.HBM((tokens, cols), BF16))
        out_specs.append(pl.BlockSpec((rows, cols), lambda i: (i, 0)))
    return pl.pallas_call(
        body,
        out_shape=out_shape,
        grid=(tokens // rows,),
        in_specs=in_specs,
        out_specs=out_specs,
        compiler_params=pltpu.CompilerParams(vmem_limit_bytes=24 * 2**20),
        cost_estimate=SMALL,
    )(*in_hbm(ins))


def row_specs(tokens, rows, widths):
    return [pl.BlockSpec((rows, width), lambda i: (i, 0)) for width in widths]


def mlp_forward(normed, weight):
    tokens, width = normed.shape
    rows, half_ff = min(256, tokens), weight.shape[1] // 3

    def body(b_ref, w_ref, gate_ref, up_ref, hidden_ref, part_ref):
        gate = dot(b_ref[...], w_ref[:, :half_ff])
        up = dot(b_ref[...], w_ref[:, half_ff : 2 * half_ff])
        hidden = (gate * jax.nn.sigmoid(gate) * up).astype(BF16)
        gate_ref[...] = gate.astype(BF16)
        up_ref[...] = up.astype(BF16)
        hidden_ref[...] = hidden
        part_ref[...] = dot(hidden, w_ref[:, 2 * half_ff :], NT).astype(BF16)

    widths = (half_ff, half_ff, half_ff, width)
    return pl.pallas_call(
        body,
        out_shape=[pltpu.HBM((tokens, w), BF16) for w in widths[:3]]
        + [jax.ShapeDtypeStruct((tokens, width), BF16)],
        grid=(tokens // rows,),
        in_specs=row_specs(tokens, rows, (width,)) + [VMEM],
        out_specs=row_specs(tokens, rows, widths),
        compiler_params=pltpu.CompilerParams(vmem_limit_bytes=22 * 2**20),
        cost_estimate=SMALL,
    )(normed, weight)


def mlp_backward(grad, gate, up, weight):
    tokens, width = grad.shape
    rows, half_ff = min(256, tokens), weight.shape[1] // 3

    def body(g_ref, gate_ref, up_ref, w_ref, d_gu_ref, part_ref):
        d_hidden = dot(g_ref[...], w_ref[:, 2 * half_ff :])
        z = gate_ref[...].astype(F32)
        sigma = jax.nn.sigmoid(z)
        d_gate = d_hidden * up_ref[...].astype(F32) * sigma * (1.0 + z * (1.0 - sigma))
        d_gate = d_gate.astype(BF16)
        d_up = (d_hidden * z * sigma).astype(BF16)
        d_gu_ref[:, :half_ff] = d_gate
        d_gu_ref[:, half_ff:] = d_up
        part = dot(d_gate, w_ref[:, :half_ff], NT)
        part += dot(d_up, w_ref[:, half_ff : 2 * half_ff], NT)
        part_ref[...] = part.astype(BF16)

    widths = (2 * half_ff, width)
    return pl.pallas_call(
        body,
        out_shape=[
            pltpu.HBM((tokens, widths[0]), BF16),
            jax.ShapeDtypeStruct((tokens, width), BF16),
        ],
        grid=(tokens // rows,),
        in_specs=row_specs(tokens, rows, (width, half_ff, half_ff)) + [VMEM],
        out_specs=row_specs(tokens, rows, widths),
        compiler_params=pltpu.CompilerParams(vmem_limit_bytes=22 * 2**20),
        cost_estimate=SMALL,
    )(*in_hbm((grad, gate, up)), weight)


def sum_step(order, add, add_pinned, pack, last, held, pinned):
    ins, in_specs, out_shape, out_specs = [], [], [], []

    def block(array, which, part, pinned=False):
        rows = array.shape[1] // 3
        (array,) = in_hbm([array]) if pinned else [array]
        spec = pl.BlockSpec((1, rows, array.shape[2]), lambda i, o: (2 * o[which] + part, i, 0))
        ins.append(array)
        in_specs.append(spec)

    def pair(half, cols):
        return pl.BlockSpec((2, half // 3, cols), lambda i, o: (0, i, 0))

    def single(half, cols):
        return pl.BlockSpec((half // 3, cols), lambda i, o: (i, 0))

    def size(terms):
        return terms[0].shape[1], sum(value.shape[2] for value in terms)

    def places(terms):
        low = 0
        for value in terms:
            yield slice(low, low + value.shape[2])
            low += value.shape[2]

    if add is not None:
        terms, got_x, got_y = add
        half, cols = size(terms)
        for value in terms:
            for which, part in ((0, 0), (0, 1), (2, 0), (1, 1)):
                block(value, which, part, add_pinned)
        ins += [got_x, got_y]
        in_specs += [pair(half, cols)] * 2
        out_shape += [jax.ShapeDtypeStruct((half, cols), BF16)] * 2
        out_shape += [jax.ShapeDtypeStruct((2, half, cols), BF16)]
        out_specs += [single(half, cols), single(half, cols), pair(half, cols)]
    if pack is not None:
        half, cols = size(pack)
        for value in pack:
            for which, part in ((1, 0), (3, 0), (2, 1), (3, 1)):
                block(value, which, part)
        out_shape += [jax.ShapeDtypeStruct((2, half, cols), BF16)] * 2
        out_specs += [pair(half, cols)] * 2
    if last:
        for chunk in last:
            half, cols = chunk[1].shape
            ins += list(chunk)
            in_specs += [pair(half, cols), single(half, cols), single(half, cols)]
        half, cols = size([chunk[0] for chunk in last])
        out_shape += [jax.ShapeDtypeStruct((2, half, cols), BF16)]
        out_specs += [pair(half, cols)]

    def plus(left, right):
        return (left.astype(F32) + right.astype(F32)).astype(BF16)

    count = len(held) + len(pinned)

    def body(order_ref, *refs):
        source = iter(refs[: len(ins)])
        target = iter(refs[len(ins) + count :])
        if add is not None:
            blocks = [[next(source) for _ in range(4)] for _ in add[0]]
            gx, gy = next(source), next(source)
            to_y, to_x, kept = (next(target) for _ in range(3))
            for (own_a, own_b, on_a, on_b), at in zip(blocks, places(add[0])):
                to_y[:, at] = plus(on_a[0], gx[1, :, at])
                to_x[:, at] = plus(on_b[0], gy[1, :, at])
                kept[0, :, at] = plus(own_a[0], gx[0, :, at])
                kept[1, :, at] = plus(own_b[0], gy[0, :, at])
        if pack is not None:
            outs = next(target), next(target)
            for at in places(pack):
                for out in outs:
                    for i in range(2):
                        out[i, :, at] = next(source)[0]
        if last:
            out = next(target)
            for at in places([chunk[0] for chunk in last]):
                kept, from_y, from_x = (next(source) for _ in range(3))
                out[0, :, at] = plus(kept[0], from_y[...])
                out[1, :, at] = plus(kept[1], from_x[...])

    result = pl.pallas_call(
        body,
        out_shape=out_shape + shapes_of(held, pinned),
        grid_spec=pltpu.PrefetchScalarGridSpec(
            num_scalar_prefetch=1,
            grid=(3,),
            in_specs=in_specs + [ANY] * count,
            out_specs=out_specs + [ANY] * count,
        ),
        input_output_aliases={1 + len(ins) + i: len(out_shape) + i for i in range(count)},
        compiler_params=pltpu.CompilerParams(vmem_limit_bytes=24 * 2**20),
        cost_estimate=SMALL,
    )(order, *ins, *held, *in_hbm(pinned))
    return result[: len(out_shape)], result[len(out_shape) :]


class Gather:
    def __init__(self, shards, order):
        self.shards, self.order = shards, order
        self.plane = lax.axis_size("seq") == 4
        self.gathered = {}
        self.columns, self.near, self.far = {}, {}, {}

    def gather(self, k, axes):
        array = self.shards[k][0]
        if id(array) not in self.gathered:
            self.gathered[id(array)] = lax.all_gather(array, axes, axis=0, tiled=True)
        return self.gathered[id(array)]

    def cut(self, k, value):
        low, high = self.shards[k][1:]
        return value[:, low:high]

    def step(self, *held, take=None, relay=None, begin=None, pinned=()):
        if not self.plane:
            if take is None:
                return (None, *held, *pinned)
            return (self.cut(take, self.gather(take, ("seq", "fsdp"))), *held, *pinned)
        free = [*held] + ([] if relay is None else [*self.near[relay]])
        fixed = [*pinned] + ([] if begin is None else [self.gather(begin, "fsdp")])
        whole = None
        if take is None:
            passed = hold(*free, pinned=fixed)
        else:
            args = (self.columns[take], *self.near[take], *self.far[take])
            whole, *passed = assemble(self.order, *args, free, fixed)
        free, fixed = passed[: len(free)], passed[len(free) :]
        if relay is not None:
            by_x, by_y = self.near[relay] = free[-2:]
            self.far[relay] = flip(by_y[0], "seq", 1), flip(by_x[1], "seq", 2)
        if begin is not None:
            self.gathered[id(self.shards[begin][0])] = fixed[-1]
            column = self.cut(begin, fixed[-1])
            column = column.reshape(2, column.shape[0] // 2, column.shape[1])
            self.columns[begin] = column
            self.near[begin] = flip(column, "seq", 1), flip(column, "seq", 2)
        return (whole, *free[: len(held)], *fixed[: len(pinned)])


class Sums:
    def __init__(self, order):
        self.order = order
        self.plane = lax.axis_size("seq") == 4
        self.terms, self.near, self.far, self.done, self.parts = {}, {}, {}, {}, {}

    def step(self, *held, pinned=(), add=None, pack=None, terms=None, last=(), wait=None, ready=()):
        if not self.plane:
            if pack:
                total = jnp.concatenate(terms, axis=1)
                total = lax.psum_scatter(total, ("seq", "fsdp"), scatter_dimension=0, tiled=True)
                self.parts[pack] = total
            if last:
                self.done[last] = jnp.concatenate([self.parts[name] for name in last], axis=1)
            return (*held, *pinned)
        if pack:
            self.terms[pack] = [v.reshape(8, v.shape[0] // 8, v.shape[1]) for v in terms]
        free = [*held] + ([*self.far[wait][1:]] if wait else [])
        fixed = [*pinned] + [self.done[name] for name in ready]
        outs, passed = sum_step(
            self.order,
            (self.terms.pop(add), *self.near.pop(add)) if add else None,
            add in ("gu0", "gu1"),
            self.terms[pack] if pack else None,
            [self.far.pop(name) for name in last],
            free,
            fixed,
        )
        outs = list(outs)
        free, fixed = passed[: len(free)], passed[len(free) :]
        if wait:
            self.far[wait] = (self.far[wait][0], *free[len(held) :])
        for name, value in zip(ready, fixed[len(pinned) :]):
            self.done[name] = value
        if add:
            to_y, to_x, kept = outs[:3]
            outs = outs[3:]
            self.far[add] = kept, flip(to_y, "seq", 2), flip(to_x, "seq", 1)
        if pack:
            to_x, to_y = outs[:2]
            outs = outs[2:]
            self.near[pack] = flip(to_x, "seq", 1), flip(to_y, "seq", 2)
        if last:
            total = outs[0].reshape(-1, outs[0].shape[2])
            self.done[last] = lax.psum_scatter(total, "fsdp", scatter_dimension=0, tiled=True)
        return (*free[: len(held)], *fixed[: len(pinned)])


def rms(value):
    return lax.rsqrt(jnp.mean(value * value, axis=-1, keepdims=True) + EPSILON)


def split_attention(chunk, qkv_cols):
    gains = chunk[:, qkv_cols : qkv_cols + 2].astype(F32).T
    return chunk[:, :qkv_cols], chunk[:, qkv_cols + GAIN_COLS :], gains[0], gains[1]


def mix(partial, other):
    return partial.astype(F32) + other.astype(F32)


def local(
    inputs,
    cotangent,
    segments,
    w_query,
    w_key,
    w_value,
    w_out,
    w_gate,
    w_up,
    w_down,
    norm_attn,
    norm_mlp,
):
    core = lax.axis_index("section")
    seq_index = lax.axis_index("seq")
    seq_size = lax.axis_size("seq")
    micro, per_dev, rows, width = inputs.shape
    query_width, key_width, ff = w_query.shape[2], w_key.shape[2], w_gate.shape[2]
    parts = micro * per_dev
    chunks = seq_size // parts
    part, chunk = seq_index % parts, seq_index // parts
    tokens = parts * rows
    length = tokens * chunks
    hq, hk = query_width // HEAD // 2, key_width // HEAD // 2
    qkv_cols = (query_width + 2 * key_width) // 2
    core_index = core[None].astype(jnp.int32)
    places = jnp.stack([part, part ^ 1, part ^ 2, part ^ 3]).astype(jnp.int32)
    order = jnp.stack([seq_index, seq_index ^ 1, seq_index ^ 2, seq_index ^ 3]).astype(jnp.int32)

    def chosen(first, second):
        return jnp.where(core == 0, first, second)

    def half(value, index):
        size = value.shape[1] // 2
        return value[:, index * size : (index + 1) * size]

    def shards(halves):
        mine = chosen(halves[0], halves[1])
        theirs = other_core(chosen(halves[1], halves[0]))
        return chosen(mine, theirs), chosen(theirs, mine)

    gains = jnp.pad(jnp.stack([norm_attn[0], norm_mlp[0]], axis=1), ((0, 0), (0, GAIN_COLS - 2)))
    out_t, down_t = w_out[0].T, w_down[0].T

    def attention_pieces(i):
        pieces = [half(w_query[0], i), half(w_key[0], i), half(w_value[0], i), gains]
        return jnp.concatenate(pieces + [half(out_t, i)], axis=1)

    attn_first, attn_second = shards([attention_pieces(0), attention_pieces(1)])
    mlp = (w_gate[0], w_up[0], down_t)
    mlp_first, mlp_second = shards(
        [jnp.concatenate([half(value, i) for value in mlp], axis=1) for i in range(2)]
    )
    attn_first, mlp_first = hold(pinned=(attn_first, mlp_first))
    second = jnp.concatenate([mlp_second, attn_second], axis=1)
    mlp_cols = mlp_second.shape[1]
    chunk_shards = [(attn_first, 0, attn_first.shape[1]), (mlp_first, 0, mlp_cols)]
    chunk_shards += [(second, mlp_cols, second.shape[1]), (second, 0, mlp_cols)]

    piece = rows // 2

    def own_rows(value):
        value = value.reshape(parts, rows, -1)
        return lax.dynamic_slice_in_dim(value, core * piece, piece, 1)

    def sent_rows(own):
        return [flip(pick(own, part ^ step), "seq", step, parts) for step in range(1, parts)]

    def sequence(own, got):
        mine = place(jnp.zeros_like(own), pick(own, part), part)
        for step, value in enumerate(got):
            mine = place(mine, value, part ^ (step + 1))
        other = other_core(mine)
        both = jnp.stack([chosen(mine, other), chosen(other, mine)], axis=1)
        return both.reshape(tokens, both.shape[-1])

    numbers = own_rows(segments).reshape(parts, piece, 1).astype(BF16)
    numbers = jnp.pad(numbers, ((0, 0), (0, 0), (0, 127)))
    own = jnp.concatenate([own_rows(inputs), own_rows(cotangent), numbers], axis=2)
    weights = Gather(chunk_shards, order)
    _, *got = weights.step(*sent_rows(own), begin=0)
    both = sequence(own, got)
    x_first, grad_last = both[:, :width], both[:, width : 2 * width]
    seg_q = both[:, 2 * width].astype(jnp.int32)

    groups = [[i * parts + n for i in range(chunks)] for n in range(parts)]

    def group_gather(value):
        if chunks == 1:
            return value
        return lax.all_gather(value, "seq", axis=0, tiled=True, axis_index_groups=groups)

    def group_scatter(value):
        return lax.psum_scatter(
            value, "seq", scatter_dimension=0, tiled=True, axis_index_groups=groups
        )

    seg_all = group_gather(seg_q)
    pos_q = chunk * tokens + jnp.arange(tokens, dtype=jnp.int32)
    plan = {
        "hq": hq,
        "hk": hk,
        "same": chunks == 1,
        "tables_q": rope_tables(pos_q),
        "tables_k": rope_tables(jnp.arange(length)),
        "seg_q_col": seg_q[:, None],
        "pos_q_col": pos_q[:, None],
        "seg_k_row": seg_all[None, :],
        "seg_q_row": seg_q[None, :],
        "pos_q_row": pos_q[None, :],
        "seg_k_col": seg_all[:, None],
        "gather": group_gather,
        "scatter": group_scatter,
    }

    half_ff = ff // 2
    sums = Sums(order)
    _, x_low, grad_last = weights.step(x_first, grad_last, relay=0)
    attn, x_low = weights.step(x_low, take=0, begin=1)
    kept = []
    for layer in range(2):
        w_qkv, w_out_t, gain_one, gain_two = split_attention(attn, qkv_cols)
        x = x_low.astype(F32)
        scale_one = rms(x)
        normed = (x * scale_one * gain_one).astype(BF16)
        attended = attention_forward(dot(normed, w_qkv), plan)
        transfers = {"relay": 1, "begin": 2} if layer == 0 else {"relay": 3}
        _, out = weights.step(pinned=attended[:1], **transfers)
        attended = (out, *attended[1:])
        own = dot(out, w_out_t, NT).astype(BF16)
        mixed = x + mix(own, other_core(own))
        scale_two = rms(mixed)
        normed_two = (mixed * scale_two * gain_two).astype(BF16)
        transfers = {"take": 1, "relay": 2} if layer == 0 else {"take": 3}
        mlp, normed_two = weights.step(normed_two, **transfers)
        gate, up, hidden, own = mlp_forward(normed_two, mlp)
        if layer == 0:
            next_attn, own = weights.step(own, take=2, begin=3)
        y_low = (mixed + mix(own, other_core(own))).astype(BF16)
        kept.append(
            {
                "w": (attn, mlp),
                "x": x_low,
                "r": scale_one,
                "a": normed,
                "attended": attended,
                "h": mixed.astype(BF16),
                "r2": scale_two,
                "b": normed_two,
                "gate": gate,
                "up": up,
                "hidden": hidden,
            }
        )
        if layer == 0:
            x_low, attn = y_low, next_attn

    grads = [None, None]
    grad_low = grad_last
    for layer in (1, 0):
        keep = kept[layer]
        w_attn, mlp = keep["w"]
        w_qkv, _, gain_one, gain_two = split_attention(w_attn, qkv_cols)
        grad_down = dot(grad_low, keep["hidden"], TN).astype(BF16)
        if layer == 1:
            (grad_low,) = sums.step(grad_low, pack="d1", terms=(grad_down,))
        else:
            (grad_low,) = sums.step(pinned=(grad_low,), add="A1", pack="d0", terms=(grad_down,))
            grads[1] = grad_low
        d_gu, own_two = mlp_backward(grad_low, keep["gate"], keep["up"], mlp)
        if layer == 1:
            own_two, d_gu = sums.step(own_two, pinned=(d_gu,), add="d1")
        else:
            own_two, *y_out.near, d_gu = sums.step(
                own_two, *y_out.near, pinned=(d_gu,), add="d0", wait="A1"
            )
            y_out.onward()
        other = other_core(own_two)
        terms = (dot(keep["b"], d_gu, TN).astype(BF16),)
        if layer == 1:
            (other,) = sums.step(other, pack="gu1", terms=terms, wait="d1")
            y_out = Return(kept[1]["x"], y_low, places, core_index, parts)
        else:
            (other,) = sums.step(other, pack="gu0", terms=terms, last=("A1", "d0"))
        d_mixed, d_out = norm_back(
            own_two,
            other,
            keep["h"],
            keep["r2"],
            gain_two,
            grad_low,
            (w_attn, qkv_cols + GAIN_COLS),
        )
        d_qkv, own_one = attention_backward(keep["attended"], d_out, w_attn, qkv_cols, plan)
        if layer == 1:
            own_one, *y_out.near, d_qkv = sums.step(
                own_one, *y_out.near, pinned=(d_qkv,), add="gu1"
            )
        else:
            own_one, *y_out.far, d_qkv = sums.step(
                own_one, *y_out.far, pinned=(d_qkv,), add="gu0", ready=(("d1", "gu1"),)
            )
        other = other_core(own_one)
        attn_terms = gradient_chunk(
            d_qkv,
            keep["attended"][0],
            (keep["a"], d_mixed, own_one, keep["x"], own_two, keep["h"]),
            (keep["r"], keep["r2"]),
        )
        last = ("d1", "gu1") if layer == 1 else ("gu0",)
        (other,) = sums.step(other, pack="A" + str(layer), terms=(attn_terms,))
        (other,) = sums.step(other, last=last)
        (grad_low,) = norm_back(own_one, other, keep["x"], keep["r"], gain_one, d_mixed)
        grads[layer] = grad_low
    layer_out = y_out.placed()
    *grads, layer_out = sums.step(pinned=(*grads, layer_out), add="A0")
    ready = ("A1", "d0"), ("gu0",)
    grads = sums.step(pinned=grads, last=("A0",), ready=ready)
    x_back = Return(*grads, places, core_index, parts, pinned=True)
    x_back.onward()
    *x_back.far, sums.done[("A0",)] = hold(pinned=(*x_back.far, sums.done[("A0",)]))
    input_grad = x_back.placed()
    layer_out = layer_out.reshape(1, micro, per_dev, rows, width)
    input_grad = input_grad.reshape(1, micro, per_dev, rows, width)

    def owned(first, second):
        keep = chosen(first, second)
        recv = other_core(chosen(second, first))
        return chosen(keep, recv).astype(F32), chosen(recv, keep).astype(F32)

    def joined(halves, start, size):
        at = slice(start, start + size // 2)
        return jnp.concatenate([halves[0][:, at], halves[1][:, at]], axis=1)

    done = sums.done
    cols = attn_terms.shape[1]
    gate, up = (
        owned(done[("gu0",)][:, low : low + half_ff], done[("d1", "gu1")][:, low + half_ff :][:, :half_ff])
        for low in (0, half_ff)
    )
    down = owned(done[("A1", "d0")][:, cols:], done[("d1", "gu1")][:, :half_ff])
    attn = owned(done[("A0",)], done[("A1", "d0")][:, :cols])
    start = query_width // 2
    g_query = joined(attn, 0, query_width)
    g_key = joined(attn, start, key_width)
    g_value = joined(attn, start + key_width // 2, key_width)
    g_out = joined(attn, qkv_cols + GAIN_COLS, query_width).T
    g_gate, g_up, g_down = joined(gate, 0, ff), joined(up, 0, ff), joined(down, 0, ff).T
    gains_owned = (attn[0] + attn[1])[:, qkv_cols : qkv_cols + 2].T
    outs = (g_query, g_key, g_value, g_out, g_gate, g_up, g_down, gains_owned[0], gains_owned[1])
    return (layer_out, input_grad) + tuple(value[None] for value in outs)


def solution(mesh):
    weight_rows = P("section", ("seq", "fsdp"), None)
    weight_cols = P("section", None, ("seq", "fsdp"))
    gain = P("section", ("seq", "fsdp"))
    layer = P("section", None, "fsdp", "seq", None)
    weights = (weight_rows,) * 3 + (weight_cols,) + (weight_rows,) * 2 + (weight_cols,)
    return jax.shard_map(
        local,
        mesh=mesh,
        in_specs=(
            P(None, "fsdp", "seq", None),
            P(None, "fsdp", "seq", None),
            P(None, "fsdp", "seq"),
        )
        + weights
        + (gain, gain),
        out_specs=(layer, layer) + weights + (gain, gain),
        check_vma=False,
    )
```

time: 5450 us -> 780 us (0.14)
  waiting for transfers between devices: 3920 us -> 186 us
  matrix products: 826 us -> 50.1 us
  Pallas kernels: 0 us -> 296 us
  blocking collectives: 227 us -> 26.2 us
  local copies, waits for them, and re-layouts: 224 us -> 73.6 us
  other arithmetic: 192 us -> 51 us
  starting transfers between devices: 15.1 us -> 74.1 us
    all_gather x56 -> x2, waiting for transfers between devices: 3760 us -> 17.9 us  [gather(): self.gathered[id(array)] = lax.all_gather(array, axes, axis=0, tiled=True)]
    dot_general x105 -> x8, matrix products: 826 us -> 50.1 us  [dot(): return lax.dot_general(left, right, dims, preferred_element_type=F32)]
    pallas_call x0 -> x44, Pallas kernels: none -> 296 us  [the longest x2 69.2 us: attention_backward(): pl.pallas_call(functools.partial(backward_kernel, hq, hk, same), out_shap...]
    ppermute x4 -> x66, waiting for transfers between devices: 11.7 us -> 163 us  [the longest x51 163 us: flip(): return lax.ppermute(value, axis, pairs)]
    unnamed x70 -> x8, waiting for transfers between devices: 148 us -> 0.1 us
    all_gather x9 -> x1, blocking collectives: 129 us -> 26.2 us  [gather(): self.gathered[id(array)] = lax.all_gather(array, axes, axis=0, tiled=True)]
    unnamed x2 -> x0, blocking collectives: 98 us -> none
    dynamic_slice x102 -> x1, local copies, waits for them, and re-layouts: 85.4 us -> 1.87 us  [own_rows(): return lax.dynamic_slice_in_dim(value, core * piece, piece, 1)]
  transfers between devices with their start and end apart: 67 -> 72, of which waited for: 46 -> 34; matrix products, arithmetic and copies ran while one was open for 21% -> 14% of each run, Pallas kernels for 0% -> 34%
where the time goes in v1:
time: 780 us; the launch traced here: 772 us
  Pallas kernels  296 us (38%)
  waiting for transfers between devices  186 us (24%)
  starting transfers between devices  74.1 us (9%)
  local copies, waits for them, and re-layouts  73.6 us (9%)
  other arithmetic  51 us (7%)
  matrix products  50.1 us (6%)
  blocking collectives  26.2 us (3%)
  between operations  15.9 us (2%)
    ppermute x51, waiting for transfers between devices, flip(): return lax.ppermute(value, axis, pairs)  163 us
    pallas_call x2, Pallas kernels, attention_backward(): pl.pallas_call(functools.partial(backward_kernel, hq, hk, same), out_shap...  69.2 us
    pallas_call x2, Pallas kernels, attention_forward(): pl.pallas_call(functools.partial(forward_kernel, hq, hk, same), out_shape...  51.2 us
    dot_general x8, matrix products, dot(): return lax.dot_general(left, right, dims, preferred_element_type=F32)  50.1 us
    unnamed x184, local copies, waits for them, and re-layouts  44.2 us
    ppermute x51, starting transfers between devices, flip(): return lax.ppermute(value, axis, pairs)  41.5 us
    pallas_call x2, Pallas kernels, mlp_backward(): pl.pallas_call(body, out_shape=[pltpu.HBM((tokens, widths[0]), BF16), jax...  34.2 us
    pallas_call x4, Pallas kernels, norm_back(): pl.pallas_call(body, out_shape=out_shape, grid=(tokens // rows,), in_spec...  33.2 us
  transfers between devices with their start and end apart: 72, of which 34 were waited for; matrix products, arithmetic and copies ran while one was open for 14% of the time, Pallas kernels for 34%

profile of v1, /device:TPU:1, one launch (start us, length us, event | category | flops | bytes accessed | tf_op | source)
XLA Modules:
  0.0 772.2 jit_solution(17827305261502681285)
XLA Ops:
  26.9 26.2 %all_gather.9.refs_3_ = bf16[288,1600]{1,0:T(8,128)(2,1)} all-gather(bf16[72,1600]{1,0:T(8,128)(2,1)} %get-tuple-element.147), channel_id=1, replica_groups=mesh['section'=2,'seq'=4,'fsdp'=4] {'fsdp'}, dimensions={0}, use_global_device_ids=true | all-gather | bytes 1152000 | tf_op jit(solution)/shard_map/all_gather | solution.py:724
  55.8 5.8 collective-permute-start.5
  72.8 12.6 %collective-permute-done.6.refs_2_ = bf16[2,144,1600]{2,1,0:T(8,128)(2,1)} collective-permute-done((bf16[2,144,1600]{2,1,0:T(8,128)(2,1)S(1)}, bf16[2,144,1600]{2,1,0:T(8,128)(2,1)}, u32[]{:S(2)}, u32[]{:S(2)}) %collective-permute-start.6) | collective-permute-done | bytes 921632 | tf_op jit(solution)/shard_map/ppermute | solution.py:321
  94.4 4.8 collective-permute-done.8.low
  103.3 3.7 shard_map.206
  116.6 4.5 fusion.10.refs_0_
  121.0 25.7 %shard_map.207 = (bf16[1024,576]{1,0:T(8,128)(2,1)}, bf16[9,1024,64]{2,1,0:T(8,128)(2,1)}, bf16[6,1024,64]{2,1,0:T(8,128)(2,1)}, f32[16,1024]{1,0:T(8,128)}) custom-call(f32[1024,960]{1,0:T(8,128)} %fusion.10.refs_0_, f32[1024,128]{1,0:T(8,128)} %get-tuple-element.402.refs_1_.refs_5_, f32[1024,128]{1,0:T(8,128)} %get-tuple-element.403.refs_2_.refs_6_, ...), custom_call_target="tpu_custom_call" | custom-call | flops 1024 | bytes 1024 | tf_op jit(solution)/shard_map/pallas_call | solution.py:247
  146.7 17.9 %all-gather.5.cloned.1.call-done.refs_3_ = bf16[288,6208]{1,0:T(8,128)(2,1)} async-done(((bf16[72,6208]{1,0:T(8,128)(2,1)}), bf16[288,6208]{1,0:T(8,128)(2,1)}) %all-gather.5.cloned.1.call-update) | async-done | bytes 3575824 | tf_op jit(solution)/shard_map/all_gather | solution.py:724
  168.3 3.9 convolution_convert_fusion.5
  172.3 3.8 collective-permute-start.14
  186.5 27.4 %collective-permute-done.12.low = bf16[144,4608]{1,0:T(8,128)(2,1)S(1)} collective-permute-done((bf16[144,4608]{1,0:T(8,128)(2,1)S(1)}, bf16[144,4608]{1,0:T(8,128)(2,1)S(1)}, u32[]{:S(2)}, u32[]{:S(2)}) %collective-permute-start.12) | collective-permute-done | bytes 1327136 | tf_op jit(solution)/shard_map/ppermute | solution.py:321
  214.9 4.7 shard_map.209
  221.3 14.3 %shard_map.210 = (bf16[1024,1536]{1,0:T(8,128)(2,1)}, bf16[1024,1536]{1,0:T(8,128)(2,1)}, bf16[1024,1536]{1,0:T(8,128)(2,1)}, bf16[1024,1152]{1,0:T(8,128)(2,1)}) custom-call(bf16[1024,1152]{1,0:T(8,128)(2,1)S(1)} %get-tuple-element.164.b_ref, bf16[1152,4608]{1,0:T(8,128)(2,1)S(1)} %bitcast.210), custom_call_target="tpu_custom_call" | custom-call | flops 1024 | bytes 1024 | tf_op jit(solution)/shard_map/pallas_call | solution.py:572
  237.1 5.3 collective-permute-start.21
  247.9 5.8 fusion.4
  257.5 4.4 fusion.8.refs_0_
  261.9 25.5 %shard_map.212 = (bf16[1024,576]{1,0:T(8,128)(2,1)}, bf16[9,1024,64]{2,1,0:T(8,128)(2,1)}, bf16[6,1024,64]{2,1,0:T(8,128)(2,1)}, f32[16,1024]{1,0:T(8,128)}) custom-call(f32[1024,960]{1,0:T(8,128)} %fusion.8.refs_0_, f32[1024,128]{1,0:T(8,128)} %get-tuple-element.402.refs_1_.refs_5_, f32[1024,128]{1,0:T(8,128)} %get-tuple-element.403.refs_2_.refs_6_, ...), custom_call_target="tpu_custom_call" | custom-call | flops 1024 | bytes 1024 | tf_op jit(solution)/shard_map/pallas_call | solution.py:247
  287.4 16.5 %collective-permute-done.19.refs_0_ = bf16[2,144,4608]{2,1,0:T(8,128)(2,1)} collective-permute-done((bf16[2,144,4608]{2,1,0:T(8,128)(2,1)}, bf16[2,144,4608]{2,1,0:T(8,128)(2,1)}, u32[]{:S(2)}, u32[]{:S(2)}) %collective-permute-start.19) | collective-permute-done | bytes 2654240 | tf_op jit(solution)/shard_map/ppermute | solution.py:321
  304.4 3.5 convolution_convert_fusion.4
  317.3 24.6 %collective-permute-done.22.low = bf16[144,4608]{1,0:T(8,128)(2,1)S(1)} collective-permute-done((bf16[144,4608]{1,0:T(8,128)(2,1)S(1)}, bf16[144,4608]{1,0:T(8,128)(2,1)S(1)}, u32[]{:S(2)}, u32[]{:S(2)}) %collective-permute-start.22) | collective-permute-done | bytes 1327136 | tf_op jit(solution)/shard_map/ppermute | solution.py:321
  343.7 5.0 shard_map.214
  348.7 14.0 %shard_map.215 = (bf16[1024,1536]{1,0:T(8,128)(2,1)}, bf16[1024,1536]{1,0:T(8,128)(2,1)}, bf16[1024,1536]{1,0:T(8,128)(2,1)}, bf16[1024,1152]{1,0:T(8,128)(2,1)S(1)}) custom-call(bf16[1024,1152]{1,0:T(8,128)(2,1)S(1)} %get-tuple-element.176.b_ref, bf16[1152,4608]{1,0:T(8,128)(2,1)S(1)} %bitcast.214), custom_call_target="tpu_custom_call" | custom-call | flops 1024 | bytes 1024 | tf_op jit(solution)/shard_map/pallas_call | solution.py:572
  362.7 6.2 convolution_convert_fusion.3
  372.2 17.3 %shard_map.217 = (bf16[1024,3072]{1,0:T(8,128)(2,1)}, bf16[1024,1152]{1,0:T(8,128)(2,1)S(1)}) custom-call(bf16[1024,1152]{1,0:T(8,128)(2,1)} %copy-done.19, bf16[1024,1536]{1,0:T(8,128)(2,1)} %get-tuple-element.183.gate_ref, bf16[1024,1536]{1,0:T(8,128)(2,1)} %get-tuple-element.184.up_ref, bf16[1152,4608]{1,0:T(8,128)(2,1)S(1)} %bitcast.215), custom_call_target="tpu_custom_call" | custom-call | flops 1024 | bytes 1024 | tf_op jit(solution)/shard_map/pallas_call | solution.py:602
  397.1 10.8 %convolution_convert_fusion.1 = bf16[1152,3072]{1,0:T(8,128)(2,1)S(1)} fusion(bf16[1024,1152]{1,0:T(8,128)(2,1)S(1)} %get-tuple-element.176.b_ref, bf16[1024,3072]{1,0:T(8,128)(2,1)} %get-tuple-element.187), kind=kOutput, calls=%fused_computation.1 | convolution fusion | flops 7251296256 | bytes 15728640 | tf_op jit(solution)/shard_map/dot_general | solution.py:26
  424.1 9.2 %shard_map.220 = (bf16[1024,1152]{1,0:T(8,128)(2,1)}, bf16[1024,576]{1,0:T(8,128)(2,1)}) custom-call(bf16[1024,1152]{1,0:T(8,128)(2,1)} %copy-done.32, bf16[1024,1152]{1,0:T(8,128)(2,1)} %copy-done.29, bf16[1024,1152]{1,0:T(8,128)(2,1)} %get-tuple-element.336.value_ref.val_b, f32[1024,1]{1,0:T(8,128)} %copy.142.scale_ref.r_b, ...), custom_call_target="tpu_custom_call" | custom-call | flops 1024 | bytes 1024 | tf_op jit(solution)/shard_map/pallas_call | solution.py:543
  433.3 34.6 %shard_map.221 = (bf16[1024,960]{1,0:T(8,128)(2,1)}, bf16[1024,1152]{1,0:T(8,128)(2,1)}) custom-call(bf16[9,1024,64]{2,1,0:T(8,128)(2,1)} %get-tuple-element.193.refs_0_, bf16[6,1024,64]{2,1,0:T(8,128)(2,1)} %get-tuple-element.194.refs_1_, bf16[1024,576]{1,0:T(8,128)(2,1)} %get-tuple-element.196.refs_2_, bf16[1024,576]{1,0:T(8,128)(2,1)} %get-tuple-element.175.refs_3_.o_ref, ...), custom_call_target="tpu_custom_call" | custom-call | flops 1024 | bytes 1024 | tf_op jit(solution)/shard_map/pallas_call | solution.py:282
  467.9 4.2 shard_map.223
  480.4 12.1 %shard_map.224 = bf16[1152,1600]{1,0:T(8,128)(2,1)} custom-call(bf16[1024,960]{1,0:T(8,128)(2,1)} %get-tuple-element.210.d_ref, bf16[1024,576]{1,0:T(8,128)(2,1)} %get-tuple-element.175.refs_3_.o_ref, bf16[1024,1152]{1,0:T(8,128)(2,1)} %copy-done.73, bf16[1024,1152]{1,0:T(8,128)(2,1)} %get-tuple-element.211.m_ref.added_ref, ...), custom_call_target="tpu_custom_call" | custom-call | flops 17179869184 | bytes 1024 | tf_op jit(solution)/shard_map/pallas_call | solution.py:507
  495.5 4.3 collective-permute-done.35.refs_4_
  505.3 7.2 shard_map.227.refs_10_
  512.5 6.0 convolution_convert_fusion.2
  518.5 7.5 collective-permute-done.38.refs_4_
  531.0 16.9 %shard_map.229 = (bf16[1024,3072]{1,0:T(8,128)(2,1)}, bf16[1024,1152]{1,0:T(8,128)(2,1)S(1)}) custom-call(bf16[1024,1152]{1,0:T(8,128)(2,1)} %get-tuple-element.219.g_ref.added_ref.refs_7_, bf16[1024,1536]{1,0:T(8,128)(2,1)} %get-tuple-element.220.gate_ref, bf16[1024,1536]{1,0:T(8,128)(2,1)} %get-tuple-element.221.up_ref, bf16[1152,4608]{1,0:T(8,128)(2,1)S(1)} %bitcast.213), custom_call_target="tpu_custom_call" | custom-call | flops 1024 | bytes 1024 | tf_op jit(solution)/shard_map/pallas_call | solution.py:602
  547.9 9.8 %collective-permute-done.42.refs_9_ = bf16[144,1600]{1,0:T(8,128)(2,1)S(1)} collective-permute-done((bf16[144,1600]{1,0:T(8,128)(2,1)S(1)}, bf16[144,1600]{1,0:T(8,128)(2,1)S(1)}, u32[]{:S(2)}, u32[]{:S(2)}) %collective-permute-start.42) | collective-permute-done | bytes 460832 | tf_op jit(solution)/shard_map/ppermute | solution.py:321
  559.0 3.5 collective-permute-start.46
  563.6 10.8 %convolution_convert_fusion = bf16[1152,3072]{1,0:T(8,128)(2,1)S(1)} fusion(bf16[1024,1152]{1,0:T(8,128)(2,1)S(1)} %copy-done.23, bf16[1024,3072]{1,0:T(8,128)(2,1)} %get-tuple-element.228), kind=kOutput, calls=%fused_computation | convolution fusion | flops 7251296256 | bytes 15728640 | tf_op jit(solution)/shard_map/dot_general | solution.py:26
  589.0 9.5 %shard_map.232 = (bf16[1024,1152]{1,0:T(8,128)(2,1)}, bf16[1024,576]{1,0:T(8,128)(2,1)}) custom-call(bf16[1024,1152]{1,0:T(8,128)(2,1)} %copy-done.31, bf16[1024,1152]{1,0:T(8,128)(2,1)} %copy-done.30, bf16[1024,1152]{1,0:T(8,128)(2,1)} %get-tuple-element.333.value_ref.val_b, f32[1024,1]{1,0:T(8,128)} %copy.146.scale_ref.r_b, ...), custom_call_target="tpu_custom_call" | custom-call | flops 1024 | bytes 1024 | tf_op jit(solution)/shard_map/pallas_call | solution.py:543
  598.4 34.6 %shard_map.233 = (bf16[1024,960]{1,0:T(8,128)(2,1)}, bf16[1024,1152]{1,0:T(8,128)(2,1)}) custom-call(bf16[9,1024,64]{2,1,0:T(8,128)(2,1)} %get-tuple-element.238.refs_0_, bf16[6,1024,64]{2,1,0:T(8,128)(2,1)} %get-tuple-element.239.refs_1_, bf16[1024,576]{1,0:T(8,128)(2,1)} %get-tuple-element.241.refs_2_, bf16[1024,576]{1,0:T(8,128)(2,1)} %get-tuple-element.162.refs_3_.o_ref, ...), custom_call_target="tpu_custom_call" | custom-call | flops 1024 | bytes 1024 | tf_op jit(solution)/shard_map/pallas_call | solution.py:282
  634.4 4.6 shard_map.235
  646.6 12.2 %shard_map.236 = bf16[1152,1600]{1,0:T(8,128)(2,1)} custom-call(bf16[1024,960]{1,0:T(8,128)(2,1)} %get-tuple-element.250.d_ref, bf16[1024,576]{1,0:T(8,128)(2,1)} %get-tuple-element.162.refs_3_.o_ref, bf16[1024,1152]{1,0:T(8,128)(2,1)} %copy-done.72, bf16[1024,1152]{1,0:T(8,128)(2,1)} %get-tuple-element.251.m_ref.added_ref, ...), custom_call_target="tpu_custom_call" | custom-call | flops 17179869184 | bytes 1024 | tf_op jit(solution)/shard_map/pallas_call | solution.py:507
  661.8 4.5 collective-permute-done.54.refs_1_
  675.9 7.3 shard_map.239.refs_6_
  683.2 8.4 %collective-permute-done.52.refs_4_ = bf16[2,144,1600]{2,1,0:T(8,128)(2,1)S(1)} collective-permute-done((bf16[2,144,1600]{2,1,0:T(8,128)(2,1)}, bf16[2,144,1600]{2,1,0:T(8,128)(2,1)S(1)}, u32[]{:S(2)}, u32[]{:S(2)}) %collective-permute-start.52) | collective-permute-done | bytes 921632 | tf_op jit(solution)/shard_map/ppermute | solution.py:321
  694.6 9.2 %collective-permute-done.56.refs_1_ = bf16[144,1600]{1,0:T(8,128)(2,1)S(1)} collective-permute-done((bf16[144,1600]{1,0:T(8,128)(2,1)S(1)}, bf16[144,1600]{1,0:T(8,128)(2,1)S(1)}, u32[]{:S(2)}, u32[]{:S(2)}) %collective-permute-start.56) | collective-permute-done | bytes 460832 | tf_op jit(solution)/shard_map/ppermute | solution.py:321
  703.9 4.7 reduce-scatter.11.cloned.1.call-done.refs_6_
  723.1 9.7 %collective-permute-done.58.refs_2_.nx = bf16[2,128,1152]{2,1,0:T(8,128)(2,1)S(1)} collective-permute-done((bf16[2,128,1152]{2,1,0:T(8,128)(2,1)S(1)}, bf16[2,128,1152]{2,1,0:T(8,128)(2,1)S(1)}, u32[]{:S(2)}, u32[]{:S(2)}) %collective-permute-start.58) | collective-permute-done | bytes 589856 | tf_op jit(solution)/shard_map/ppermute | solution.py:321
  740.6 9.7 %collective-permute-done.60.refs_0_ = bf16[2,128,1152]{2,1,0:T(8,128)(2,1)S(1)} collective-permute-done((bf16[2,128,1152]{2,1,0:T(8,128)(2,1)S(1)}, bf16[2,128,1152]{2,1,0:T(8,128)(2,1)S(1)}, u32[]{:S(2)}, u32[]{:S(2)}) %collective-permute-start.60) | collective-permute-done | bytes 589856 | tf_op jit(solution)/shard_map/ppermute | solution.py:321
  (425 shorter events, 221.9 us)
Async XLA Ops:
  7.2 94.0 %all-gather.3.cloned.1.call-start = ((), (), s32[]{:S(2)}) async-start(), calls=%async_computation.4 | async-start | bytes 3317760 | tf_op jit(solution)/shard_map/all_gather | solution.py:724
  19.1 34.0 %collective-permute-start = (bf16[128,2432]{1,0:T(8,128)(2,1)}, bf16[128,2432]{1,0:T(8,128)(2,1)S(1)}, u32[]{:S(2)}, u32[]{:S(2)}) collective-permute-start(bf16[128,2432]{1,0:T(8,128)(2,1)} %get-tuple-element.344), channel_id=1, source_target_pairs={{0,4},{4,0},{8,12},{12,8},{1,5},{5,1},{9,13},{13,9},{2,6},{6,2},{1... | collective-permute-start | bytes 1867784 | tf_op jit(solution)/shard_map/ppermute | solution.py:321
  21.3 31.8 %collective-permute-start.1 = (bf16[128,2432]{1,0:T(8,128)(2,1)}, bf16[128,2432]{1,0:T(8,128)(2,1)S(1)}, u32[]{:S(2)}, u32[]{:S(2)}) collective-permute-start(bf16[128,2432]{1,0:T(8,128)(2,1)} %get-tuple-element.343), channel_id=1, source_target_pairs={{0,8},{4,12},{8,0},{12,4},{1,9},{5,13},{9,1},{13,5},{2,10},{6,14},... | collective-permute-start | bytes 1867784 | tf_op jit(solution)/shard_map/ppermute | solution.py:321
  22.6 30.5 %collective-permute-start.2 = (bf16[128,2432]{1,0:T(8,128)(2,1)}, bf16[128,2432]{1,0:T(8,128)(2,1)S(1)}, u32[]{:S(2)}, u32[]{:S(2)}) collective-permute-start(bf16[128,2432]{1,0:T(8,128)(2,1)} %get-tuple-element.342), channel_id=1, source_target_pairs={{0,12},{4,8},{8,4},{12,0},{1,13},{5,9},{9,5},{13,1},{2,14},{6,10},... | collective-permute-start | bytes 1867784 | tf_op jit(solution)/shard_map/ppermute | solution.py:321
  26.9 137.7 %all-gather.5.cloned.1.call-start = ((), (), s32[]{:S(2)}) async-start(), calls=%async_computation.5 | async-start | bytes 4515840 | tf_op jit(solution)/shard_map/all_gather | solution.py:724
  62.4 23.0 %collective-permute-start.6 = (bf16[2,144,1600]{2,1,0:T(8,128)(2,1)S(1)}, bf16[2,144,1600]{2,1,0:T(8,128)(2,1)}, u32[]{:S(2)}, u32[]{:S(2)}) collective-permute-start(bf16[2,144,1600]{2,1,0:T(8,128)(2,1)S(1)} %bitcast.229), channel_id=1, source_target_pairs={{0,4},{4,0},{8,12},{12,8},{1,5},{5,1},{9,13},{13,9},{2,6},{6,2},{1... | collective-permute-start | bytes 2764808 | tf_op jit(solution)/shard_map/ppermute | solution.py:321
  63.7 22.6 %collective-permute-start.7 = (bf16[2,144,1600]{2,1,0:T(8,128)(2,1)S(1)}, bf16[2,144,1600]{2,1,0:T(8,128)(2,1)}, u32[]{:S(2)}, u32[]{:S(2)}) collective-permute-start(bf16[2,144,1600]{2,1,0:T(8,128)(2,1)S(1)} %bitcast.230), channel_id=1, source_target_pairs={{0,8},{4,12},{8,0},{12,4},{1,9},{5,13},{9,1},{13,5},{2,10},{6,14},... | collective-permute-start | bytes 2764808 | tf_op jit(solution)/shard_map/ppermute | solution.py:321
  67.1 567.3 %reduce-scatter.9.cloned.1.call-start = ((), (), s32[]{:S(2)}) async-start(), calls=%async_computation.6 | async-start | bytes 3317760 | tf_op jit(solution)/shard_map/reduce_scatter | solution.py:801
  107.0 57.6 %collective-permute-start.10 = (bf16[2,144,4608]{2,1,0:T(8,128)(2,1)}, bf16[2,144,4608]{2,1,0:T(8,128)(2,1)}, u32[]{:S(2)}, u32[]{:S(2)}) collective-permute-start(bf16[2,144,4608]{2,1,0:T(8,128)(2,1)} %bitcast.226), channel_id=1, source_target_pairs={{0,4},{4,0},{8,12},{12,8},{1,5},{5,1},{9,13},{13,9},{2,6},{6,2},{1... | collective-permute-start | bytes 7962632 | tf_op jit(solution)/shard_map/ppermute | solution.py:321
  108.1 56.8 %collective-permute-start.11 = (bf16[2,144,4608]{2,1,0:T(8,128)(2,1)}, bf16[2,144,4608]{2,1,0:T(8,128)(2,1)}, u32[]{:S(2)}, u32[]{:S(2)}) collective-permute-start(bf16[2,144,4608]{2,1,0:T(8,128)(2,1)} %bitcast.227), channel_id=1, source_target_pairs={{0,8},{4,12},{8,0},{12,4},{1,9},{5,13},{9,1},{13,5},{2,10},{6,14},... | collective-permute-start | bytes 7962632 | tf_op jit(solution)/shard_map/ppermute | solution.py:321
  166.2 19.3 %collective-permute-start.15 = (bf16[2,144,1600]{2,1,0:T(8,128)(2,1)S(1)}, bf16[2,144,1600]{2,1,0:T(8,128)(2,1)S(1)}, u32[]{:S(2)}, u32[]{:S(2)}) collective-permute-start(bf16[2,144,1600]{2,1,0:T(8,128)(2,1)S(1)} %bitcast.232), channel_id=1, source_target_pairs={{0,4},{4,0},{8,12},{12,8},{1,5},{5,1},{9,13},{13,9},{2,6},{6,2},{1... | collective-permute-start | bytes 2764808 | tf_op jit(solution)/shard_map/ppermute | solution.py:321
  167.1 19.4 %collective-permute-start.16 = (bf16[2,144,1600]{2,1,0:T(8,128)(2,1)S(1)}, bf16[2,144,1600]{2,1,0:T(8,128)(2,1)S(1)}, u32[]{:S(2)}, u32[]{:S(2)}) collective-permute-start(bf16[2,144,1600]{2,1,0:T(8,128)(2,1)S(1)} %bitcast.233), channel_id=1, source_target_pairs={{0,8},{4,12},{8,0},{12,4},{1,9},{5,13},{9,1},{13,5},{2,10},{6,14},... | collective-permute-start | bytes 2764808 | tf_op jit(solution)/shard_map/ppermute | solution.py:321
  177.4 36.5 %collective-permute-start.12 = (bf16[144,4608]{1,0:T(8,128)(2,1)S(1)}, bf16[144,4608]{1,0:T(8,128)(2,1)S(1)}, u32[]{:S(2)}, u32[]{:S(2)}) collective-permute-start(bf16[144,4608]{1,0:T(8,128)(2,1)S(1)} %slice_bitcast_fusion.3), channel_id=1, source_target_pairs={{0,4},{4,0},{8,12},{12,8},{1,5},{5,1},{9,13},{13,9},{2,6},{6,2},{1... | collective-permute-start | bytes 3981320 | tf_op jit(solution)/shard_map/ppermute | solution.py:321
  180.0 35.0 %collective-permute-start.13 = (bf16[144,4608]{1,0:T(8,128)(2,1)S(1)}, bf16[144,4608]{1,0:T(8,128)(2,1)S(1)}, u32[]{:S(2)}, u32[]{:S(2)}) collective-permute-start(bf16[144,4608]{1,0:T(8,128)(2,1)S(1)} %slice_bitcast_fusion.2), channel_id=1, source_target_pairs={{0,8},{4,12},{8,0},{12,4},{1,9},{5,13},{9,1},{13,5},{2,10},{6,14},... | collective-permute-start | bytes 3981320 | tf_op jit(solution)/shard_map/ppermute | solution.py:321
  245.9 58.0 %collective-permute-start.19 = (bf16[2,144,4608]{2,1,0:T(8,128)(2,1)}, bf16[2,144,4608]{2,1,0:T(8,128)(2,1)}, u32[]{:S(2)}, u32[]{:S(2)}) collective-permute-start(bf16[2,144,4608]{2,1,0:T(8,128)(2,1)} %bitcast.41.col), channel_id=1, source_target_pairs={{0,4},{4,0},{8,12},{12,8},{1,5},{5,1},{9,13},{13,9},{2,6},{6,2},{1... | collective-permute-start | bytes 7962632 | tf_op jit(solution)/shard_map/ppermute | solution.py:321
  246.6 57.8 %collective-permute-start.20 = (bf16[2,144,4608]{2,1,0:T(8,128)(2,1)}, bf16[2,144,4608]{2,1,0:T(8,128)(2,1)}, u32[]{:S(2)}, u32[]{:S(2)}) collective-permute-start(bf16[2,144,4608]{2,1,0:T(8,128)(2,1)} %bitcast.41.col), channel_id=1, source_target_pairs={{0,8},{4,12},{8,0},{12,4},{1,9},{5,13},{9,1},{13,5},{2,10},{6,14},... | collective-permute-start | bytes 7962632 | tf_op jit(solution)/shard_map/ppermute | solution.py:321
  311.9 29.9 %collective-permute-start.22 = (bf16[144,4608]{1,0:T(8,128)(2,1)S(1)}, bf16[144,4608]{1,0:T(8,128)(2,1)S(1)}, u32[]{:S(2)}, u32[]{:S(2)}) collective-permute-start(bf16[144,4608]{1,0:T(8,128)(2,1)S(1)} %slice_bitcast_fusion.1), channel_id=1, source_target_pairs={{0,4},{4,0},{8,12},{12,8},{1,5},{5,1},{9,13},{13,9},{2,6},{6,2},{1... | collective-permute-start | bytes 3981320 | tf_op jit(solution)/shard_map/ppermute | solution.py:321
  314.1 29.6 %collective-permute-start.23 = (bf16[144,4608]{1,0:T(8,128)(2,1)S(1)}, bf16[144,4608]{1,0:T(8,128)(2,1)S(1)}, u32[]{:S(2)}, u32[]{:S(2)}) collective-permute-start(bf16[144,4608]{1,0:T(8,128)(2,1)S(1)} %slice_bitcast_fusion), channel_id=1, source_target_pairs={{0,8},{4,12},{8,0},{12,4},{1,9},{5,13},{9,1},{13,5},{2,10},{6,14},... | collective-permute-start | bytes 3981320 | tf_op jit(solution)/shard_map/ppermute | solution.py:321
  371.2 19.1 %collective-permute-start.25 = (bf16[2,144,1536]{2,1,0:T(8,128)(2,1)S(1)}, bf16[2,144,1536]{2,1,0:T(8,128)(2,1)S(1)}, u32[]{:S(2)}, u32[]{:S(2)}) collective-permute-start(bf16[2,144,1536]{2,1,0:T(8,128)(2,1)S(1)} %get-tuple-element.180), channel_id=1, source_target_pairs={{0,4},{4,0},{8,12},{12,8},{1,5},{5,1},{9,13},{13,9},{2,6},{6,2},{1... | collective-permute-start | bytes 2654216 | tf_op jit(solution)/shard_map/ppermute | solution.py:321
  371.9 18.9 %collective-permute-start.26 = (bf16[2,144,1536]{2,1,0:T(8,128)(2,1)S(1)}, bf16[2,144,1536]{2,1,0:T(8,128)(2,1)S(1)}, u32[]{:S(2)}, u32[]{:S(2)}) collective-permute-start(bf16[2,144,1536]{2,1,0:T(8,128)(2,1)S(1)} %get-tuple-element.181), channel_id=1, source_target_pairs={{0,8},{4,12},{8,0},{12,4},{1,9},{5,13},{9,1},{13,5},{2,10},{6,14},... | collective-permute-start | bytes 2654216 | tf_op jit(solution)/shard_map/ppermute | solution.py:321
  396.1 20.5 %collective-permute-start.32 = (bf16[1024,1152]{1,0:T(8,128)(2,1)S(1)}, bf16[1024,1152]{1,0:T(8,128)(2,1)S(1)}, u32[]{:S(2)}, u32[]{:S(2)}) collective-permute-start(bf16[1024,1152]{1,0:T(8,128)(2,1)S(1)} %get-tuple-element.199), channel_id=1, source_target_pairs={{0,16},{16,0},{1,17},{17,1},{2,18},{18,2},{3,19},{19,3},{4,20},{20... | collective-permute-start | bytes 7077896 | tf_op jit(solution)/shard_map/ppermute | solution.py:307
  414.6 53.3 %collective-permute-start.30 = (bf16[2,144,3072]{2,1,0:T(8,128)(2,1)}, bf16[2,144,3072]{2,1,0:T(8,128)(2,1)S(1)}, u32[]{:S(2)}, u32[]{:S(2)}) collective-permute-start(bf16[2,144,3072]{2,1,0:T(8,128)(2,1)} %get-tuple-element.191), channel_id=1, source_target_pairs={{0,4},{4,0},{8,12},{12,8},{1,5},{5,1},{9,13},{13,9},{2,6},{6,2},{1... | collective-permute-start | bytes 5308424 | tf_op jit(solution)/shard_map/ppermute | solution.py:321
  415.5 52.4 %collective-permute-start.31 = (bf16[2,144,3072]{2,1,0:T(8,128)(2,1)}, bf16[2,144,3072]{2,1,0:T(8,128)(2,1)}, u32[]{:S(2)}, u32[]{:S(2)}) collective-permute-start(bf16[2,144,3072]{2,1,0:T(8,128)(2,1)} %get-tuple-element.192), channel_id=1, source_target_pairs={{0,8},{4,12},{8,0},{12,4},{1,9},{5,13},{9,1},{13,5},{2,10},{6,14},... | collective-permute-start | bytes 5308424 | tf_op jit(solution)/shard_map/ppermute | solution.py:321
  421.5 46.3 %collective-permute-start.33 = (bf16[2,128,1152]{2,1,0:T(8,128)(2,1)}, bf16[2,128,1152]{2,1,0:T(8,128)(2,1)S(1)}, u32[]{:S(2)}, u32[]{:S(2)}) collective-permute-start(bf16[2,128,1152]{2,1,0:T(8,128)(2,1)} %get-tuple-element.200), channel_id=1, source_target_pairs={{0,4},{4,0},{8,12},{12,8},{1,5},{5,1},{9,13},{13,9},{2,6},{6,2},{1... | collective-permute-start | bytes 1769480 | tf_op jit(solution)/shard_map/ppermute | solution.py:321
  422.2 45.6 %collective-permute-start.34 = (bf16[2,128,1152]{2,1,0:T(8,128)(2,1)S(1)}, bf16[2,128,1152]{2,1,0:T(8,128)(2,1)S(1)}, u32[]{:S(2)}, u32[]{:S(2)}) collective-permute-start(bf16[2,128,1152]{2,1,0:T(8,128)(2,1)S(1)} %get-tuple-element.201), channel_id=1, source_target_pairs={{0,8},{4,12},{8,0},{12,4},{1,9},{5,13},{9,1},{13,5},{2,10},{6,14},... | collective-permute-start | bytes 1769480 | tf_op jit(solution)/shard_map/ppermute | solution.py:321
  475.1 17.4 %collective-permute-start.37 = (bf16[1024,1152]{1,0:T(8,128)(2,1)}, bf16[1024,1152]{1,0:T(8,128)(2,1)S(1)}, u32[]{:S(2)}, u32[]{:S(2)}) collective-permute-start(bf16[1024,1152]{1,0:T(8,128)(2,1)} %get-tuple-element.203.own_a.own_ref), channel_id=1, source_target_pairs={{0,16},{16,0},{1,17},{17,1},{2,18},{18,2},{3,19},{19,3},{4,20},{20... | collective-permute-start | bytes 7077896 | tf_op jit(solution)/shard_map/ppermute | solution.py:307
  478.3 21.5 %collective-permute-start.35 = (bf16[144,3072]{1,0:T(8,128)(2,1)}, bf16[144,3072]{1,0:T(8,128)(2,1)S(1)}, u32[]{:S(2)}, u32[]{:S(2)}) collective-permute-start(bf16[144,3072]{1,0:T(8,128)(2,1)} %copy-done.58), channel_id=1, source_target_pairs={{0,8},{4,12},{8,0},{12,4},{1,9},{5,13},{9,1},{13,5},{2,10},{6,14},... | collective-permute-start | bytes 2654216 | tf_op jit(solution)/shard_map/ppermute | solution.py:321
  479.6 21.2 %collective-permute-start.36 = (bf16[144,3072]{1,0:T(8,128)(2,1)}, bf16[144,3072]{1,0:T(8,128)(2,1)S(1)}, u32[]{:S(2)}, u32[]{:S(2)}) collective-permute-start(bf16[144,3072]{1,0:T(8,128)(2,1)} %copy-done.56), channel_id=1, source_target_pairs={{0,4},{4,0},{8,12},{12,8},{1,5},{5,1},{9,13},{13,9},{2,6},{6,2},{1... | collective-permute-start | bytes 2654216 | tf_op jit(solution)/shard_map/ppermute | solution.py:321
  503.9 190.7 %reduce-scatter.13.cloned.1.call-start = ((), (), s32[]{:S(2)}) async-start(), calls=%async_computation.8 | async-start | bytes 2304000
  504.0 22.0 %collective-permute-start.38 = (bf16[2,144,1600]{2,1,0:T(8,128)(2,1)}, bf16[2,144,1600]{2,1,0:T(8,128)(2,1)S(1)}, u32[]{:S(2)}, u32[]{:S(2)}) collective-permute-start(bf16[2,144,1600]{2,1,0:T(8,128)(2,1)} %copy-done.54), channel_id=1, source_target_pairs={{0,4},{4,0},{8,12},{12,8},{1,5},{5,1},{9,13},{13,9},{2,6},{6,2},{1... | collective-permute-start | bytes 2764808 | tf_op jit(solution)/shard_map/ppermute | solution.py:321
  504.8 21.7 %collective-permute-start.39 = (bf16[2,144,1600]{2,1,0:T(8,128)(2,1)}, bf16[2,144,1600]{2,1,0:T(8,128)(2,1)S(1)}, u32[]{:S(2)}, u32[]{:S(2)}) collective-permute-start(bf16[2,144,1600]{2,1,0:T(8,128)(2,1)} %copy-done.52), channel_id=1, source_target_pairs={{0,8},{4,12},{8,0},{12,4},{1,9},{5,13},{9,1},{13,5},{2,10},{6,14},... | collective-permute-start | bytes 2764808 | tf_op jit(solution)/shard_map/ppermute | solution.py:321
  528.0 29.7 %collective-permute-start.40 = (bf16[2,144,1536]{2,1,0:T(8,128)(2,1)S(1)}, bf16[2,144,1536]{2,1,0:T(8,128)(2,1)S(1)}, u32[]{:S(2)}, u32[]{:S(2)}) collective-permute-start(bf16[2,144,1536]{2,1,0:T(8,128)(2,1)S(1)} %get-tuple-element.217), channel_id=1, source_target_pairs={{0,4},{4,0},{8,12},{12,8},{1,5},{5,1},{9,13},{13,9},{2,6},{6,2},{1... | collective-permute-start | bytes 2654216 | tf_op jit(solution)/shard_map/ppermute | solution.py:321
  528.8 28.9 %collective-permute-start.41 = (bf16[2,144,1536]{2,1,0:T(8,128)(2,1)S(1)}, bf16[2,144,1536]{2,1,0:T(8,128)(2,1)S(1)}, u32[]{:S(2)}, u32[]{:S(2)}) collective-permute-start(bf16[2,144,1536]{2,1,0:T(8,128)(2,1)S(1)} %get-tuple-element.218), channel_id=1, source_target_pairs={{0,8},{4,12},{8,0},{12,4},{1,9},{5,13},{9,1},{13,5},{2,10},{6,14},... | collective-permute-start | bytes 2654216 | tf_op jit(solution)/shard_map/ppermute | solution.py:321
  529.2 28.5 %collective-permute-start.42 = (bf16[144,1600]{1,0:T(8,128)(2,1)S(1)}, bf16[144,1600]{1,0:T(8,128)(2,1)S(1)}, u32[]{:S(2)}, u32[]{:S(2)}) collective-permute-start(bf16[144,1600]{1,0:T(8,128)(2,1)S(1)} %get-tuple-element.225), channel_id=1, source_target_pairs={{0,8},{4,12},{8,0},{12,4},{1,9},{5,13},{9,1},{13,5},{2,10},{6,14},... | collective-permute-start | bytes 1382408 | tf_op jit(solution)/shard_map/ppermute | solution.py:321
  530.2 27.5 %collective-permute-start.43 = (bf16[144,1600]{1,0:T(8,128)(2,1)S(1)}, bf16[144,1600]{1,0:T(8,128)(2,1)S(1)}, u32[]{:S(2)}, u32[]{:S(2)}) collective-permute-start(bf16[144,1600]{1,0:T(8,128)(2,1)S(1)} %get-tuple-element.226), channel_id=1, source_target_pairs={{0,4},{4,0},{8,12},{12,8},{1,5},{5,1},{9,13},{13,9},{2,6},{6,2},{1... | collective-permute-start | bytes 1382408 | tf_op jit(solution)/shard_map/ppermute | solution.py:321
  581.4 53.0 %collective-permute-start.47 = (bf16[2,144,3072]{2,1,0:T(8,128)(2,1)}, bf16[2,144,3072]{2,1,0:T(8,128)(2,1)}, u32[]{:S(2)}, u32[]{:S(2)}) collective-permute-start(bf16[2,144,3072]{2,1,0:T(8,128)(2,1)} %get-tuple-element.236), channel_id=1, source_target_pairs={{0,4},{4,0},{8,12},{12,8},{1,5},{5,1},{9,13},{13,9},{2,6},{6,2},{1... | collective-permute-start | bytes 5308424 | tf_op jit(solution)/shard_map/ppermute | solution.py:321
  582.2 52.2 %collective-permute-start.48 = (bf16[2,144,3072]{2,1,0:T(8,128)(2,1)}, bf16[2,144,3072]{2,1,0:T(8,128)(2,1)}, u32[]{:S(2)}, u32[]{:S(2)}) collective-permute-start(bf16[2,144,3072]{2,1,0:T(8,128)(2,1)} %get-tuple-element.237), channel_id=1, source_target_pairs={{0,8},{4,12},{8,0},{12,4},{1,9},{5,13},{9,1},{13,5},{2,10},{6,14},... | collective-permute-start | bytes 5308424 | tf_op jit(solution)/shard_map/ppermute | solution.py:321
  583.2 125.4 %reduce-scatter.11.cloned.1.call-start = ((), (), s32[]{:S(2)}) async-start(), calls=%async_computation.7 | async-start | bytes 2211840 | tf_op jit(solution)/shard_map/reduce_scatter | solution.py:801
  586.8 47.5 %collective-permute-start.49 = (bf16[2,128,1152]{2,1,0:T(8,128)(2,1)}, bf16[2,128,1152]{2,1,0:T(8,128)(2,1)}, u32[]{:S(2)}, u32[]{:S(2)}) collective-permute-start(bf16[2,128,1152]{2,1,0:T(8,128)(2,1)} %get-tuple-element.246), channel_id=1, source_target_pairs={{0,8},{4,12},{8,0},{12,4},{1,9},{5,13},{9,1},{13,5},{2,10},{6,14},... | collective-permute-start | bytes 1769480 | tf_op jit(solution)/shard_map/ppermute | solution.py:321
  587.3 47.1 %collective-permute-start.50 = (bf16[2,128,1152]{2,1,0:T(8,128)(2,1)}, bf16[2,128,1152]{2,1,0:T(8,128)(2,1)}, u32[]{:S(2)}, u32[]{:S(2)}) collective-permute-start(bf16[2,128,1152]{2,1,0:T(8,128)(2,1)} %get-tuple-element.247), channel_id=1, source_target_pairs={{0,4},{4,0},{8,12},{12,8},{1,5},{5,1},{9,13},{13,9},{2,6},{6,2},{1... | collective-permute-start | bytes 1769480 | tf_op jit(solution)/shard_map/ppermute | solution.py:321
  642.0 16.8 %collective-permute-start.51 = (bf16[1024,1152]{1,0:T(8,128)(2,1)}, bf16[1024,1152]{1,0:T(8,128)(2,1)}, u32[]{:S(2)}, u32[]{:S(2)}) collective-permute-start(bf16[1024,1152]{1,0:T(8,128)(2,1)} %get-tuple-element.252.own_a.own_ref), channel_id=1, source_target_pairs={{0,16},{16,0},{1,17},{17,1},{2,18},{18,2},{3,19},{19,3},{4,20},{20... | collective-permute-start | bytes 7077896 | tf_op jit(solution)/shard_map/ppermute | solution.py:307
  644.8 21.5 %collective-permute-start.54 = (bf16[144,3072]{1,0:T(8,128)(2,1)}, bf16[144,3072]{1,0:T(8,128)(2,1)S(1)}, u32[]{:S(2)}, u32[]{:S(2)}) collective-permute-start(bf16[144,3072]{1,0:T(8,128)(2,1)} %copy-done.57), channel_id=1, source_target_pairs={{0,8},{4,12},{8,0},{12,4},{1,9},{5,13},{9,1},{13,5},{2,10},{6,14},... | collective-permute-start | bytes 2654216 | tf_op jit(solution)/shard_map/ppermute | solution.py:321
  645.8 21.2 %collective-permute-start.55 = (bf16[144,3072]{1,0:T(8,128)(2,1)}, bf16[144,3072]{1,0:T(8,128)(2,1)S(1)}, u32[]{:S(2)}, u32[]{:S(2)}) collective-permute-start(bf16[144,3072]{1,0:T(8,128)(2,1)} %copy-done.55), channel_id=1, source_target_pairs={{0,4},{4,0},{8,12},{12,8},{1,5},{5,1},{9,13},{13,9},{2,6},{6,2},{1... | collective-permute-start | bytes 2654216 | tf_op jit(solution)/shard_map/ppermute | solution.py:321
  669.5 81.7 %reduce-scatter.15.cloned.1.call-start = ((), (), s32[]{:S(2)}) async-start(), calls=%async_computation.9 | async-start | bytes 1198080
  669.6 22.0 %collective-permute-start.52 = (bf16[2,144,1600]{2,1,0:T(8,128)(2,1)}, bf16[2,144,1600]{2,1,0:T(8,128)(2,1)S(1)}, u32[]{:S(2)}, u32[]{:S(2)}) collective-permute-start(bf16[2,144,1600]{2,1,0:T(8,128)(2,1)} %copy-done.53), channel_id=1, source_target_pairs={{0,4},{4,0},{8,12},{12,8},{1,5},{5,1},{9,13},{13,9},{2,6},{6,2},{1... | collective-permute-start | bytes 2764808 | tf_op jit(solution)/shard_map/ppermute | solution.py:321
  670.4 21.7 %collective-permute-start.53 = (bf16[2,144,1600]{2,1,0:T(8,128)(2,1)}, bf16[2,144,1600]{2,1,0:T(8,128)(2,1)S(1)}, u32[]{:S(2)}, u32[]{:S(2)}) collective-permute-start(bf16[2,144,1600]{2,1,0:T(8,128)(2,1)} %copy-done.51), channel_id=1, source_target_pairs={{0,8},{4,12},{8,0},{12,4},{1,9},{5,13},{9,1},{13,5},{2,10},{6,14},... | collective-permute-start | bytes 2764808 | tf_op jit(solution)/shard_map/ppermute | solution.py:321
  721.4 17.4 %collective-permute-start.63 = (bf16[72,1536]{1,0:T(8,128)(2,1)S(1)}, bf16[72,1536]{1,0:T(8,128)(2,1)S(1)}, u32[]{:S(2)}, u32[]{:S(2)}) collective-permute-start(bf16[72,1536]{1,0:T(8,128)(2,1)S(1)} %get-tuple-element.361), channel_id=1, source_target_pairs={{0,16},{16,0},{1,17},{17,1},{2,18},{18,2},{3,19},{19,3},{4,20},{20... | collective-permute-start | bytes 663560 | tf_op jit(solution)/shard_map/ppermute | solution.py:307
  722.0 16.8 %collective-permute-start.64 = (bf16[72,1536]{1,0:T(8,128)(2,1)S(1)}, bf16[72,1536]{1,0:T(8,128)(2,1)S(1)}, u32[]{:S(2)}, u32[]{:S(2)}) collective-permute-start(bf16[72,1536]{1,0:T(8,128)(2,1)S(1)} %get-tuple-element.362), channel_id=1, source_target_pairs={{0,16},{16,0},{1,17},{17,1},{2,18},{18,2},{3,19},{19,3},{4,20},{20... | collective-permute-start | bytes 663560 | tf_op jit(solution)/shard_map/ppermute | solution.py:307
  (114 other events, 1062.6 us)
Sparse Core Ops, SparseCore 0:
  27.0 64.9 all-gather.2
  94.2 70.3 all-gather.4
  504.1 52.8 reduce-scatter.8
  583.3 40.1 reduce-scatter.12
  669.7 38.8 reduce-scatter.10
  713.6 24.0 reduce-scatter.14

commit v2 on v1

--- a/solution.py
+++ b/solution.py
@@ -347,7 +347,7 @@
         for send in sends:
             for place_index, part in send:
                 if isinstance(place_index, int):
-                    ins += self.blocks
+                    ins += self.received(self.blocks)
 
                     def index(i, o, c, place_index=place_index, part=part):
                         return (2 * o[place_index] + part, i, 0)
@@ -418,8 +418,7 @@
         )(
             self.places,
             self.core,
-            *self.blocks,
-            *self.blocks,
+            *self.received(self.blocks * 2),
             *self.received((near_x, near_y, far_y, far_x)),
         )
         return result.reshape(parts, 2 * rows, width)
@@ -555,7 +554,7 @@
     return [pl.BlockSpec((rows, width), lambda i: (i, 0)) for width in widths]
 
 
-def mlp_forward(normed, weight):
+def mlp_forward(normed, weight, hidden_kind):
     tokens, width = normed.shape
     rows, half_ff = min(256, tokens), weight.shape[1] // 3
 
@@ -571,8 +570,8 @@
     widths = (half_ff, half_ff, half_ff, width)
     return pl.pallas_call(
         body,
-        out_shape=[pltpu.HBM((tokens, w), BF16) for w in widths[:3]]
-        + [jax.ShapeDtypeStruct((tokens, width), BF16)],
+        out_shape=[pltpu.HBM((tokens, w), BF16) for w in widths[:2]]
+        + [hidden_kind((tokens, half_ff), BF16), jax.ShapeDtypeStruct((tokens, width), BF16)],
         grid=(tokens // rows,),
         in_specs=row_specs(tokens, rows, (width,)) + [VMEM],
         out_specs=row_specs(tokens, rows, widths),
@@ -951,7 +950,9 @@
         normed_two = (mixed * scale_two * gain_two).astype(BF16)
         transfers = {"take": 1, "relay": 2} if layer == 0 else {"take": 3}
         mlp, normed_two = weights.step(normed_two, **transfers)
-        gate, up, hidden, own = mlp_forward(normed_two, mlp)
+        gate, up, hidden, own = mlp_forward(
+            normed_two, mlp, pltpu.HBM if layer == 0 else jax.ShapeDtypeStruct
+        )
         if layer == 0:
             next_attn, own = weights.step(own, take=2, begin=3)
         y_low = (mixed + mix(own, other_core(own))).astype(BF16)

time: 780 us -> 774 us (level)
    unnamed x184 -> x178, local copies, waits for them, and re-layouts: 44.2 us -> 41.7 us
where the time goes in v2:
time: 774 us; the launch traced here: 767 us
  Pallas kernels  298 us (39%)
  waiting for transfers between devices  186 us (24%)
  starting transfers between devices  73.4 us (9%)
  local copies, waits for them, and re-layouts  71.1 us (9%)
  matrix products  48.1 us (6%)
  other arithmetic  48 us (6%)
  blocking collectives  26.2 us (3%)
  between operations  15.9 us (2%)
    ppermute x51, waiting for transfers between devices, flip(): return lax.ppermute(value, axis, pairs)  163 us
    pallas_call x2, Pallas kernels, attention_backward(): pl.pallas_call(functools.partial(backward_kernel, hq, hk, same), out_shap...  69.3 us
    pallas_call x2, Pallas kernels, attention_forward(): pl.pallas_call(functools.partial(forward_kernel, hq, hk, same), out_shape...  51.2 us
    dot_general x8, matrix products, dot(): return lax.dot_general(left, right, dims, preferred_element_type=F32)  48.1 us
    unnamed x178, local copies, waits for them, and re-layouts  41.7 us
    ppermute x51, starting transfers between devices, flip(): return lax.ppermute(value, axis, pairs)  41.6 us
    pallas_call x2, Pallas kernels, mlp_backward(): pl.pallas_call(body, out_shape=[pltpu.HBM((tokens, widths[0]), BF16), jax...  34.2 us
    pallas_call x4, Pallas kernels, norm_back(): pl.pallas_call(body, out_shape=out_shape, grid=(tokens // rows,), in_spec...  33.2 us
  transfers between devices with their start and end apart: 72, of which 34 were waited for; matrix products, arithmetic and copies ran while one was open for 14% of the time, Pallas kernels for 34%

profile of v2, /device:TPU:1, one launch (start us, length us, event | category | flops | bytes accessed | tf_op | source)
XLA Modules:
  0.0 766.7 jit_solution(14461919173163740284)
XLA Ops:
  27.0 26.2 %all_gather.9.refs_3_ = bf16[288,1600]{1,0:T(8,128)(2,1)} all-gather(bf16[72,1600]{1,0:T(8,128)(2,1)} %get-tuple-element.147), channel_id=1, replica_groups=mesh['section'=2,'seq'=4,'fsdp'=4] {'fsdp'}, dimensions={0}, use_global_device_ids=true | all-gather | bytes 1152000 | tf_op jit(solution)/shard_map/all_gather | solution.py:723
  55.9 5.8 collective-permute-start.5
  72.9 12.6 %collective-permute-done.6.refs_2_ = bf16[2,144,1600]{2,1,0:T(8,128)(2,1)} collective-permute-done((bf16[2,144,1600]{2,1,0:T(8,128)(2,1)S(1)}, bf16[2,144,1600]{2,1,0:T(8,128)(2,1)}, u32[]{:S(2)}, u32[]{:S(2)}) %collective-permute-start.6) | collective-permute-done | bytes 921632 | tf_op jit(solution)/shard_map/ppermute | solution.py:321
  94.4 4.8 collective-permute-done.8.low
  103.4 3.7 shard_map.206
  116.6 4.4 fusion.10.refs_0_
  121.0 25.7 %shard_map.207 = (bf16[1024,576]{1,0:T(8,128)(2,1)}, bf16[9,1024,64]{2,1,0:T(8,128)(2,1)}, bf16[6,1024,64]{2,1,0:T(8,128)(2,1)}, f32[16,1024]{1,0:T(8,128)}) custom-call(f32[1024,960]{1,0:T(8,128)} %fusion.10.refs_0_, f32[1024,128]{1,0:T(8,128)} %get-tuple-element.402.refs_1_.refs_5_, f32[1024,128]{1,0:T(8,128)} %get-tuple-element.403.refs_2_.refs_6_, ...), custom_call_target="tpu_custom_call" | custom-call | flops 1024 | bytes 1024 | tf_op jit(solution)/shard_map/pallas_call | solution.py:247
  146.7 17.9 %all-gather.5.cloned.1.call-done.refs_3_ = bf16[288,6208]{1,0:T(8,128)(2,1)} async-done(((bf16[72,6208]{1,0:T(8,128)(2,1)}), bf16[288,6208]{1,0:T(8,128)(2,1)}) %all-gather.5.cloned.1.call-update) | async-done | bytes 3575824 | tf_op jit(solution)/shard_map/all_gather | solution.py:723
  168.4 3.9 convolution_convert_fusion.5
  172.3 3.7 collective-permute-start.14
  186.5 27.5 %collective-permute-done.12.low = bf16[144,4608]{1,0:T(8,128)(2,1)S(1)} collective-permute-done((bf16[144,4608]{1,0:T(8,128)(2,1)S(1)}, bf16[144,4608]{1,0:T(8,128)(2,1)S(1)}, u32[]{:S(2)}, u32[]{:S(2)}) %collective-permute-start.12) | collective-permute-done | bytes 1327136 | tf_op jit(solution)/shard_map/ppermute | solution.py:321
  215.0 4.7 shard_map.209
  221.3 14.3 %shard_map.210 = (bf16[1024,1536]{1,0:T(8,128)(2,1)}, bf16[1024,1536]{1,0:T(8,128)(2,1)}, bf16[1024,1536]{1,0:T(8,128)(2,1)}, bf16[1024,1152]{1,0:T(8,128)(2,1)}) custom-call(bf16[1024,1152]{1,0:T(8,128)(2,1)S(1)} %get-tuple-element.164.b_ref, bf16[1152,4608]{1,0:T(8,128)(2,1)S(1)} %bitcast.194), custom_call_target="tpu_custom_call" | custom-call | flops 1024 | bytes 1024 | tf_op jit(solution)/shard_map/pallas_call | solution.py:571
  237.1 5.3 collective-permute-start.21
  248.0 5.7 fusion.4
  257.5 4.5 fusion.8.refs_0_
  262.0 25.6 %shard_map.212 = (bf16[1024,576]{1,0:T(8,128)(2,1)}, bf16[9,1024,64]{2,1,0:T(8,128)(2,1)}, bf16[6,1024,64]{2,1,0:T(8,128)(2,1)}, f32[16,1024]{1,0:T(8,128)}) custom-call(f32[1024,960]{1,0:T(8,128)} %fusion.8.refs_0_, f32[1024,128]{1,0:T(8,128)} %get-tuple-element.402.refs_1_.refs_5_, f32[1024,128]{1,0:T(8,128)} %get-tuple-element.403.refs_2_.refs_6_, ...), custom_call_target="tpu_custom_call" | custom-call | flops 1024 | bytes 1024 | tf_op jit(solution)/shard_map/pallas_call | solution.py:247
  287.6 16.4 %collective-permute-done.19.refs_0_ = bf16[2,144,4608]{2,1,0:T(8,128)(2,1)} collective-permute-done((bf16[2,144,4608]{2,1,0:T(8,128)(2,1)}, bf16[2,144,4608]{2,1,0:T(8,128)(2,1)}, u32[]{:S(2)}, u32[]{:S(2)}) %collective-permute-start.19) | collective-permute-done | bytes 2654240 | tf_op jit(solution)/shard_map/ppermute | solution.py:321
  304.5 3.5 convolution_convert_fusion.4
  317.3 24.6 %collective-permute-done.22.low = bf16[144,4608]{1,0:T(8,128)(2,1)S(1)} collective-permute-done((bf16[144,4608]{1,0:T(8,128)(2,1)S(1)}, bf16[144,4608]{1,0:T(8,128)(2,1)S(1)}, u32[]{:S(2)}, u32[]{:S(2)}) %collective-permute-start.22) | collective-permute-done | bytes 1327136 | tf_op jit(solution)/shard_map/ppermute | solution.py:321
  343.7 5.0 shard_map.214
  348.8 13.8 %shard_map.215 = (bf16[1024,1536]{1,0:T(8,128)(2,1)}, bf16[1024,1536]{1,0:T(8,128)(2,1)}, bf16[1024,1536]{1,0:T(8,128)(2,1)S(1)}, bf16[1024,1152]{1,0:T(8,128)(2,1)S(1)}) custom-call(bf16[1024,1152]{1,0:T(8,128)(2,1)S(1)} %get-tuple-element.176.b_ref, bf16[1152,4608]{1,0:T(8,128)(2,1)S(1)} %bitcast.198), custom_call_target="tpu_custom_call" | custom-call | flops 1024 | bytes 1024 | tf_op jit(solution)/shard_map/pallas_call | solution.py:571
  362.5 4.2 convolution_convert_fusion.3
  370.0 17.3 %shard_map.217 = (bf16[1024,3072]{1,0:T(8,128)(2,1)}, bf16[1024,1152]{1,0:T(8,128)(2,1)S(1)}) custom-call(bf16[1024,1152]{1,0:T(8,128)(2,1)} %copy-done.14, bf16[1024,1536]{1,0:T(8,128)(2,1)} %get-tuple-element.183.gate_ref, bf16[1024,1536]{1,0:T(8,128)(2,1)} %get-tuple-element.184.up_ref, bf16[1152,4608]{1,0:T(8,128)(2,1)S(1)} %bitcast.199), custom_call_target="tpu_custom_call" | custom-call | flops 1024 | bytes 1024 | tf_op jit(solution)/shard_map/pallas_call | solution.py:601
  395.0 10.8 %convolution_convert_fusion.1 = bf16[1152,3072]{1,0:T(8,128)(2,1)S(1)} fusion(bf16[1024,1152]{1,0:T(8,128)(2,1)S(1)} %get-tuple-element.176.b_ref, bf16[1024,3072]{1,0:T(8,128)(2,1)} %get-tuple-element.187), kind=kOutput, calls=%fused_computation.1 | convolution fusion | flops 7251296256 | bytes 15728640 | tf_op jit(solution)/shard_map/dot_general | solution.py:26
  421.9 9.2 %shard_map.220 = (bf16[1024,1152]{1,0:T(8,128)(2,1)}, bf16[1024,576]{1,0:T(8,128)(2,1)}) custom-call(bf16[1024,1152]{1,0:T(8,128)(2,1)} %copy-done.27, bf16[1024,1152]{1,0:T(8,128)(2,1)} %copy-done.24, bf16[1024,1152]{1,0:T(8,128)(2,1)} %get-tuple-element.336.value_ref.val_b, f32[1024,1]{1,0:T(8,128)} %copy.142.scale_ref.r_b, ...), custom_call_target="tpu_custom_call" | custom-call | flops 1024 | bytes 1024 | tf_op jit(solution)/shard_map/pallas_call | solution.py:542
  431.1 34.6 %shard_map.221 = (bf16[1024,960]{1,0:T(8,128)(2,1)}, bf16[1024,1152]{1,0:T(8,128)(2,1)}) custom-call(bf16[9,1024,64]{2,1,0:T(8,128)(2,1)} %get-tuple-element.193.refs_0_, bf16[6,1024,64]{2,1,0:T(8,128)(2,1)} %get-tuple-element.194.refs_1_, bf16[1024,576]{1,0:T(8,128)(2,1)} %get-tuple-element.196.refs_2_, bf16[1024,576]{1,0:T(8,128)(2,1)} %get-tuple-element.175.refs_3_.o_ref, ...), custom_call_target="tpu_custom_call" | custom-call | flops 1024 | bytes 1024 | tf_op jit(solution)/shard_map/pallas_call | solution.py:282
  465.8 4.2 shard_map.223
  478.2 12.1 %shard_map.224 = bf16[1152,1600]{1,0:T(8,128)(2,1)} custom-call(bf16[1024,960]{1,0:T(8,128)(2,1)} %get-tuple-element.210.d_ref, bf16[1024,576]{1,0:T(8,128)(2,1)} %get-tuple-element.175.refs_3_.o_ref, bf16[1024,1152]{1,0:T(8,128)(2,1)} %copy-done.69, bf16[1024,1152]{1,0:T(8,128)(2,1)} %get-tuple-element.211.m_ref.added_ref, ...), custom_call_target="tpu_custom_call" | custom-call | flops 17179869184 | bytes 1024 | tf_op jit(solution)/shard_map/pallas_call | solution.py:506
  493.4 4.3 collective-permute-done.35.refs_4_
  503.1 7.2 shard_map.227.refs_10_
  510.4 6.0 convolution_convert_fusion.2
  516.4 7.4 collective-permute-done.38.refs_4_
  528.9 16.9 %shard_map.229 = (bf16[1024,3072]{1,0:T(8,128)(2,1)}, bf16[1024,1152]{1,0:T(8,128)(2,1)S(1)}) custom-call(bf16[1024,1152]{1,0:T(8,128)(2,1)} %get-tuple-element.219.g_ref.added_ref.refs_7_, bf16[1024,1536]{1,0:T(8,128)(2,1)} %get-tuple-element.220.gate_ref, bf16[1024,1536]{1,0:T(8,128)(2,1)} %get-tuple-element.221.up_ref, bf16[1152,4608]{1,0:T(8,128)(2,1)S(1)} %bitcast.197), custom_call_target="tpu_custom_call" | custom-call | flops 1024 | bytes 1024 | tf_op jit(solution)/shard_map/pallas_call | solution.py:601
  545.8 9.7 %collective-permute-done.42.refs_9_ = bf16[144,1600]{1,0:T(8,128)(2,1)S(1)} collective-permute-done((bf16[144,1600]{1,0:T(8,128)(2,1)S(1)}, bf16[144,1600]{1,0:T(8,128)(2,1)S(1)}, u32[]{:S(2)}, u32[]{:S(2)}) %collective-permute-start.42) | collective-permute-done | bytes 460832 | tf_op jit(solution)/shard_map/ppermute | solution.py:321
  561.5 10.8 %convolution_convert_fusion = bf16[1152,3072]{1,0:T(8,128)(2,1)S(1)} fusion(bf16[1024,1152]{1,0:T(8,128)(2,1)S(1)} %copy-done.18, bf16[1024,3072]{1,0:T(8,128)(2,1)} %get-tuple-element.228), kind=kOutput, calls=%fused_computation | convolution fusion | flops 7251296256 | bytes 15728640 | tf_op jit(solution)/shard_map/dot_general | solution.py:26
  586.8 9.4 %shard_map.232 = (bf16[1024,1152]{1,0:T(8,128)(2,1)}, bf16[1024,576]{1,0:T(8,128)(2,1)}) custom-call(bf16[1024,1152]{1,0:T(8,128)(2,1)} %copy-done.26, bf16[1024,1152]{1,0:T(8,128)(2,1)} %copy-done.25, bf16[1024,1152]{1,0:T(8,128)(2,1)} %get-tuple-element.333.value_ref.val_b, f32[1024,1]{1,0:T(8,128)} %copy.146.scale_ref.r_b, ...), custom_call_target="tpu_custom_call" | custom-call | flops 1024 | bytes 1024 | tf_op jit(solution)/shard_map/pallas_call | solution.py:542
  596.3 34.6 %shard_map.233 = (bf16[1024,960]{1,0:T(8,128)(2,1)}, bf16[1024,1152]{1,0:T(8,128)(2,1)}) custom-call(bf16[9,1024,64]{2,1,0:T(8,128)(2,1)} %get-tuple-element.238.refs_0_, bf16[6,1024,64]{2,1,0:T(8,128)(2,1)} %get-tuple-element.239.refs_1_, bf16[1024,576]{1,0:T(8,128)(2,1)} %get-tuple-element.241.refs_2_, bf16[1024,576]{1,0:T(8,128)(2,1)} %get-tuple-element.162.refs_3_.o_ref, ...), custom_call_target="tpu_custom_call" | custom-call | flops 1024 | bytes 1024 | tf_op jit(solution)/shard_map/pallas_call | solution.py:282
  632.1 4.6 shard_map.235
  644.4 12.1 %shard_map.236 = bf16[1152,1600]{1,0:T(8,128)(2,1)} custom-call(bf16[1024,960]{1,0:T(8,128)(2,1)} %get-tuple-element.250.d_ref, bf16[1024,576]{1,0:T(8,128)(2,1)} %get-tuple-element.162.refs_3_.o_ref, bf16[1024,1152]{1,0:T(8,128)(2,1)} %copy-done.68, bf16[1024,1152]{1,0:T(8,128)(2,1)} %get-tuple-element.251.m_ref.added_ref, ...), custom_call_target="tpu_custom_call" | custom-call | flops 17179869184 | bytes 1024 | tf_op jit(solution)/shard_map/pallas_call | solution.py:506
  659.6 4.5 collective-permute-done.54.refs_1_
  673.7 7.2 shard_map.239.refs_6_
  680.9 8.4 %collective-permute-done.52.refs_4_ = bf16[2,144,1600]{2,1,0:T(8,128)(2,1)S(1)} collective-permute-done((bf16[2,144,1600]{2,1,0:T(8,128)(2,1)}, bf16[2,144,1600]{2,1,0:T(8,128)(2,1)S(1)}, u32[]{:S(2)}, u32[]{:S(2)}) %collective-permute-start.52) | collective-permute-done | bytes 921632 | tf_op jit(solution)/shard_map/ppermute | solution.py:321
  692.3 9.3 %collective-permute-done.56.refs_1_ = bf16[144,1600]{1,0:T(8,128)(2,1)S(1)} collective-permute-done((bf16[144,1600]{1,0:T(8,128)(2,1)S(1)}, bf16[144,1600]{1,0:T(8,128)(2,1)S(1)}, u32[]{:S(2)}, u32[]{:S(2)}) %collective-permute-start.56) | collective-permute-done | bytes 460832 | tf_op jit(solution)/shard_map/ppermute | solution.py:321
  701.7 4.4 reduce-scatter.11.cloned.1.call-done.refs_6_
  718.9 9.2 %collective-permute-done.58.refs_2_.nx = bf16[2,128,1152]{2,1,0:T(8,128)(2,1)S(1)} collective-permute-done((bf16[2,128,1152]{2,1,0:T(8,128)(2,1)S(1)}, bf16[2,128,1152]{2,1,0:T(8,128)(2,1)S(1)}, u32[]{:S(2)}, u32[]{:S(2)}) %collective-permute-start.58) | collective-permute-done | bytes 589856 | tf_op jit(solution)/shard_map/ppermute | solution.py:321
  735.5 10.4 %collective-permute-done.60.refs_0_ = bf16[2,128,1152]{2,1,0:T(8,128)(2,1)S(1)} collective-permute-done((bf16[2,128,1152]{2,1,0:T(8,128)(2,1)S(1)}, bf16[2,128,1152]{2,1,0:T(8,128)(2,1)S(1)}, u32[]{:S(2)}, u32[]{:S(2)}) %collective-permute-start.60) | collective-permute-done | bytes 589856 | tf_op jit(solution)/shard_map/ppermute | solution.py:321
  750.9 3.6 shard_map.246
  (419 shorter events, 218.7 us)
Async XLA Ops:
  7.2 94.0 %all-gather.3.cloned.1.call-start = ((), (), s32[]{:S(2)}) async-start(), calls=%async_computation.4 | async-start | bytes 3317760 | tf_op jit(solution)/shard_map/all_gather | solution.py:723
  19.2 34.0 %collective-permute-start = (bf16[128,2432]{1,0:T(8,128)(2,1)}, bf16[128,2432]{1,0:T(8,128)(2,1)S(1)}, u32[]{:S(2)}, u32[]{:S(2)}) collective-permute-start(bf16[128,2432]{1,0:T(8,128)(2,1)} %get-tuple-element.344), channel_id=1, source_target_pairs={{0,4},{4,0},{8,12},{12,8},{1,5},{5,1},{9,13},{13,9},{2,6},{6,2},{1... | collective-permute-start | bytes 1867784 | tf_op jit(solution)/shard_map/ppermute | solution.py:321
  21.4 31.8 %collective-permute-start.1 = (bf16[128,2432]{1,0:T(8,128)(2,1)}, bf16[128,2432]{1,0:T(8,128)(2,1)S(1)}, u32[]{:S(2)}, u32[]{:S(2)}) collective-permute-start(bf16[128,2432]{1,0:T(8,128)(2,1)} %get-tuple-element.343), channel_id=1, source_target_pairs={{0,8},{4,12},{8,0},{12,4},{1,9},{5,13},{9,1},{13,5},{2,10},{6,14},... | collective-permute-start | bytes 1867784 | tf_op jit(solution)/shard_map/ppermute | solution.py:321
  22.6 30.5 %collective-permute-start.2 = (bf16[128,2432]{1,0:T(8,128)(2,1)}, bf16[128,2432]{1,0:T(8,128)(2,1)S(1)}, u32[]{:S(2)}, u32[]{:S(2)}) collective-permute-start(bf16[128,2432]{1,0:T(8,128)(2,1)} %get-tuple-element.342), channel_id=1, source_target_pairs={{0,12},{4,8},{8,4},{12,0},{1,13},{5,9},{9,5},{13,1},{2,14},{6,10},... | collective-permute-start | bytes 1867784 | tf_op jit(solution)/shard_map/ppermute | solution.py:321
  26.9 137.7 %all-gather.5.cloned.1.call-start = ((), (), s32[]{:S(2)}) async-start(), calls=%async_computation.5 | async-start | bytes 4515840 | tf_op jit(solution)/shard_map/all_gather | solution.py:723
  62.5 23.0 %collective-permute-start.6 = (bf16[2,144,1600]{2,1,0:T(8,128)(2,1)S(1)}, bf16[2,144,1600]{2,1,0:T(8,128)(2,1)}, u32[]{:S(2)}, u32[]{:S(2)}) collective-permute-start(bf16[2,144,1600]{2,1,0:T(8,128)(2,1)S(1)} %bitcast.213), channel_id=1, source_target_pairs={{0,4},{4,0},{8,12},{12,8},{1,5},{5,1},{9,13},{13,9},{2,6},{6,2},{1... | collective-permute-start | bytes 2764808 | tf_op jit(solution)/shard_map/ppermute | solution.py:321
  63.8 22.6 %collective-permute-start.7 = (bf16[2,144,1600]{2,1,0:T(8,128)(2,1)S(1)}, bf16[2,144,1600]{2,1,0:T(8,128)(2,1)}, u32[]{:S(2)}, u32[]{:S(2)}) collective-permute-start(bf16[2,144,1600]{2,1,0:T(8,128)(2,1)S(1)} %bitcast.214), channel_id=1, source_target_pairs={{0,8},{4,12},{8,0},{12,4},{1,9},{5,13},{9,1},{13,5},{2,10},{6,14},... | collective-permute-start | bytes 2764808 | tf_op jit(solution)/shard_map/ppermute | solution.py:321
  67.1 565.0 %reduce-scatter.9.cloned.1.call-start = ((), (), s32[]{:S(2)}) async-start(), calls=%async_computation.6 | async-start | bytes 3317760 | tf_op jit(solution)/shard_map/reduce_scatter | solution.py:800
  107.1 57.6 %collective-permute-start.10 = (bf16[2,144,4608]{2,1,0:T(8,128)(2,1)}, bf16[2,144,4608]{2,1,0:T(8,128)(2,1)}, u32[]{:S(2)}, u32[]{:S(2)}) collective-permute-start(bf16[2,144,4608]{2,1,0:T(8,128)(2,1)} %bitcast.210), channel_id=1, source_target_pairs={{0,4},{4,0},{8,12},{12,8},{1,5},{5,1},{9,13},{13,9},{2,6},{6,2},{1... | collective-permute-start | bytes 7962632 | tf_op jit(solution)/shard_map/ppermute | solution.py:321
  108.2 56.8 %collective-permute-start.11 = (bf16[2,144,4608]{2,1,0:T(8,128)(2,1)}, bf16[2,144,4608]{2,1,0:T(8,128)(2,1)}, u32[]{:S(2)}, u32[]{:S(2)}) collective-permute-start(bf16[2,144,4608]{2,1,0:T(8,128)(2,1)} %bitcast.211), channel_id=1, source_target_pairs={{0,8},{4,12},{8,0},{12,4},{1,9},{5,13},{9,1},{13,5},{2,10},{6,14},... | collective-permute-start | bytes 7962632 | tf_op jit(solution)/shard_map/ppermute | solution.py:321
  166.3 19.3 %collective-permute-start.15 = (bf16[2,144,1600]{2,1,0:T(8,128)(2,1)S(1)}, bf16[2,144,1600]{2,1,0:T(8,128)(2,1)S(1)}, u32[]{:S(2)}, u32[]{:S(2)}) collective-permute-start(bf16[2,144,1600]{2,1,0:T(8,128)(2,1)S(1)} %bitcast.216), channel_id=1, source_target_pairs={{0,4},{4,0},{8,12},{12,8},{1,5},{5,1},{9,13},{13,9},{2,6},{6,2},{1... | collective-permute-start | bytes 2764808 | tf_op jit(solution)/shard_map/ppermute | solution.py:321
  167.2 19.4 %collective-permute-start.16 = (bf16[2,144,1600]{2,1,0:T(8,128)(2,1)S(1)}, bf16[2,144,1600]{2,1,0:T(8,128)(2,1)S(1)}, u32[]{:S(2)}, u32[]{:S(2)}) collective-permute-start(bf16[2,144,1600]{2,1,0:T(8,128)(2,1)S(1)} %bitcast.217), channel_id=1, source_target_pairs={{0,8},{4,12},{8,0},{12,4},{1,9},{5,13},{9,1},{13,5},{2,10},{6,14},... | collective-permute-start | bytes 2764808 | tf_op jit(solution)/shard_map/ppermute | solution.py:321
  177.4 36.6 %collective-permute-start.12 = (bf16[144,4608]{1,0:T(8,128)(2,1)S(1)}, bf16[144,4608]{1,0:T(8,128)(2,1)S(1)}, u32[]{:S(2)}, u32[]{:S(2)}) collective-permute-start(bf16[144,4608]{1,0:T(8,128)(2,1)S(1)} %slice_bitcast_fusion.3), channel_id=1, source_target_pairs={{0,4},{4,0},{8,12},{12,8},{1,5},{5,1},{9,13},{13,9},{2,6},{6,2},{1... | collective-permute-start | bytes 3981320 | tf_op jit(solution)/shard_map/ppermute | solution.py:321
  180.0 35.0 %collective-permute-start.13 = (bf16[144,4608]{1,0:T(8,128)(2,1)S(1)}, bf16[144,4608]{1,0:T(8,128)(2,1)S(1)}, u32[]{:S(2)}, u32[]{:S(2)}) collective-permute-start(bf16[144,4608]{1,0:T(8,128)(2,1)S(1)} %slice_bitcast_fusion.2), channel_id=1, source_target_pairs={{0,8},{4,12},{8,0},{12,4},{1,9},{5,13},{9,1},{13,5},{2,10},{6,14},... | collective-permute-start | bytes 3981320 | tf_op jit(solution)/shard_map/ppermute | solution.py:321
  245.9 58.0 %collective-permute-start.19 = (bf16[2,144,4608]{2,1,0:T(8,128)(2,1)}, bf16[2,144,4608]{2,1,0:T(8,128)(2,1)}, u32[]{:S(2)}, u32[]{:S(2)}) collective-permute-start(bf16[2,144,4608]{2,1,0:T(8,128)(2,1)} %bitcast.41.col), channel_id=1, source_target_pairs={{0,4},{4,0},{8,12},{12,8},{1,5},{5,1},{9,13},{13,9},{2,6},{6,2},{1... | collective-permute-start | bytes 7962632 | tf_op jit(solution)/shard_map/ppermute | solution.py:321
  246.7 57.8 %collective-permute-start.20 = (bf16[2,144,4608]{2,1,0:T(8,128)(2,1)}, bf16[2,144,4608]{2,1,0:T(8,128)(2,1)}, u32[]{:S(2)}, u32[]{:S(2)}) collective-permute-start(bf16[2,144,4608]{2,1,0:T(8,128)(2,1)} %bitcast.41.col), channel_id=1, source_target_pairs={{0,8},{4,12},{8,0},{12,4},{1,9},{5,13},{9,1},{13,5},{2,10},{6,14},... | collective-permute-start | bytes 7962632 | tf_op jit(solution)/shard_map/ppermute | solution.py:321
  312.0 29.9 %collective-permute-start.22 = (bf16[144,4608]{1,0:T(8,128)(2,1)S(1)}, bf16[144,4608]{1,0:T(8,128)(2,1)S(1)}, u32[]{:S(2)}, u32[]{:S(2)}) collective-permute-start(bf16[144,4608]{1,0:T(8,128)(2,1)S(1)} %slice_bitcast_fusion.1), channel_id=1, source_target_pairs={{0,4},{4,0},{8,12},{12,8},{1,5},{5,1},{9,13},{13,9},{2,6},{6,2},{1... | collective-permute-start | bytes 3981320 | tf_op jit(solution)/shard_map/ppermute | solution.py:321
  314.1 29.6 %collective-permute-start.23 = (bf16[144,4608]{1,0:T(8,128)(2,1)S(1)}, bf16[144,4608]{1,0:T(8,128)(2,1)S(1)}, u32[]{:S(2)}, u32[]{:S(2)}) collective-permute-start(bf16[144,4608]{1,0:T(8,128)(2,1)S(1)} %slice_bitcast_fusion), channel_id=1, source_target_pairs={{0,8},{4,12},{8,0},{12,4},{1,9},{5,13},{9,1},{13,5},{2,10},{6,14},... | collective-permute-start | bytes 3981320 | tf_op jit(solution)/shard_map/ppermute | solution.py:321
  369.0 19.1 %collective-permute-start.25 = (bf16[2,144,1536]{2,1,0:T(8,128)(2,1)S(1)}, bf16[2,144,1536]{2,1,0:T(8,128)(2,1)S(1)}, u32[]{:S(2)}, u32[]{:S(2)}) collective-permute-start(bf16[2,144,1536]{2,1,0:T(8,128)(2,1)S(1)} %get-tuple-element.180), channel_id=1, source_target_pairs={{0,4},{4,0},{8,12},{12,8},{1,5},{5,1},{9,13},{13,9},{2,6},{6,2},{1... | collective-permute-start | bytes 2654216 | tf_op jit(solution)/shard_map/ppermute | solution.py:321
  369.8 18.9 %collective-permute-start.26 = (bf16[2,144,1536]{2,1,0:T(8,128)(2,1)S(1)}, bf16[2,144,1536]{2,1,0:T(8,128)(2,1)S(1)}, u32[]{:S(2)}, u32[]{:S(2)}) collective-permute-start(bf16[2,144,1536]{2,1,0:T(8,128)(2,1)S(1)} %get-tuple-element.181), channel_id=1, source_target_pairs={{0,8},{4,12},{8,0},{12,4},{1,9},{5,13},{9,1},{13,5},{2,10},{6,14},... | collective-permute-start | bytes 2654216 | tf_op jit(solution)/shard_map/ppermute | solution.py:321
  394.0 20.5 %collective-permute-start.32 = (bf16[1024,1152]{1,0:T(8,128)(2,1)S(1)}, bf16[1024,1152]{1,0:T(8,128)(2,1)S(1)}, u32[]{:S(2)}, u32[]{:S(2)}) collective-permute-start(bf16[1024,1152]{1,0:T(8,128)(2,1)S(1)} %get-tuple-element.199), channel_id=1, source_target_pairs={{0,16},{16,0},{1,17},{17,1},{2,18},{18,2},{3,19},{19,3},{4,20},{20... | collective-permute-start | bytes 7077896 | tf_op jit(solution)/shard_map/ppermute | solution.py:307
  412.5 53.3 %collective-permute-start.30 = (bf16[2,144,3072]{2,1,0:T(8,128)(2,1)}, bf16[2,144,3072]{2,1,0:T(8,128)(2,1)S(1)}, u32[]{:S(2)}, u32[]{:S(2)}) collective-permute-start(bf16[2,144,3072]{2,1,0:T(8,128)(2,1)} %get-tuple-element.191), channel_id=1, source_target_pairs={{0,4},{4,0},{8,12},{12,8},{1,5},{5,1},{9,13},{13,9},{2,6},{6,2},{1... | collective-permute-start | bytes 5308424 | tf_op jit(solution)/shard_map/ppermute | solution.py:321
  413.3 52.5 %collective-permute-start.31 = (bf16[2,144,3072]{2,1,0:T(8,128)(2,1)}, bf16[2,144,3072]{2,1,0:T(8,128)(2,1)}, u32[]{:S(2)}, u32[]{:S(2)}) collective-permute-start(bf16[2,144,3072]{2,1,0:T(8,128)(2,1)} %get-tuple-element.192), channel_id=1, source_target_pairs={{0,8},{4,12},{8,0},{12,4},{1,9},{5,13},{9,1},{13,5},{2,10},{6,14},... | collective-permute-start | bytes 5308424 | tf_op jit(solution)/shard_map/ppermute | solution.py:321
  419.3 46.4 %collective-permute-start.33 = (bf16[2,128,1152]{2,1,0:T(8,128)(2,1)}, bf16[2,128,1152]{2,1,0:T(8,128)(2,1)S(1)}, u32[]{:S(2)}, u32[]{:S(2)}) collective-permute-start(bf16[2,128,1152]{2,1,0:T(8,128)(2,1)} %get-tuple-element.200), channel_id=1, source_target_pairs={{0,4},{4,0},{8,12},{12,8},{1,5},{5,1},{9,13},{13,9},{2,6},{6,2},{1... | collective-permute-start | bytes 1769480 | tf_op jit(solution)/shard_map/ppermute | solution.py:321
  420.0 45.7 %collective-permute-start.34 = (bf16[2,128,1152]{2,1,0:T(8,128)(2,1)S(1)}, bf16[2,128,1152]{2,1,0:T(8,128)(2,1)S(1)}, u32[]{:S(2)}, u32[]{:S(2)}) collective-permute-start(bf16[2,128,1152]{2,1,0:T(8,128)(2,1)S(1)} %get-tuple-element.201), channel_id=1, source_target_pairs={{0,8},{4,12},{8,0},{12,4},{1,9},{5,13},{9,1},{13,5},{2,10},{6,14},... | collective-permute-start | bytes 1769480 | tf_op jit(solution)/shard_map/ppermute | solution.py:321
  473.0 17.3 %collective-permute-start.37 = (bf16[1024,1152]{1,0:T(8,128)(2,1)}, bf16[1024,1152]{1,0:T(8,128)(2,1)S(1)}, u32[]{:S(2)}, u32[]{:S(2)}) collective-permute-start(bf16[1024,1152]{1,0:T(8,128)(2,1)} %get-tuple-element.203.own_a.own_ref), channel_id=1, source_target_pairs={{0,16},{16,0},{1,17},{17,1},{2,18},{18,2},{3,19},{19,3},{4,20},{20... | collective-permute-start | bytes 7077896 | tf_op jit(solution)/shard_map/ppermute | solution.py:307
  476.2 21.5 %collective-permute-start.35 = (bf16[144,3072]{1,0:T(8,128)(2,1)}, bf16[144,3072]{1,0:T(8,128)(2,1)S(1)}, u32[]{:S(2)}, u32[]{:S(2)}) collective-permute-start(bf16[144,3072]{1,0:T(8,128)(2,1)} %copy-done.53), channel_id=1, source_target_pairs={{0,8},{4,12},{8,0},{12,4},{1,9},{5,13},{9,1},{13,5},{2,10},{6,14},... | collective-permute-start | bytes 2654216 | tf_op jit(solution)/shard_map/ppermute | solution.py:321
  477.4 21.2 %collective-permute-start.36 = (bf16[144,3072]{1,0:T(8,128)(2,1)}, bf16[144,3072]{1,0:T(8,128)(2,1)S(1)}, u32[]{:S(2)}, u32[]{:S(2)}) collective-permute-start(bf16[144,3072]{1,0:T(8,128)(2,1)} %copy-done.51), channel_id=1, source_target_pairs={{0,4},{4,0},{8,12},{12,8},{1,5},{5,1},{9,13},{13,9},{2,6},{6,2},{1... | collective-permute-start | bytes 2654216 | tf_op jit(solution)/shard_map/ppermute | solution.py:321
  501.8 190.6 %reduce-scatter.13.cloned.1.call-start = ((), (), s32[]{:S(2)}) async-start(), calls=%async_computation.8 | async-start | bytes 2304000
  501.8 22.0 %collective-permute-start.38 = (bf16[2,144,1600]{2,1,0:T(8,128)(2,1)}, bf16[2,144,1600]{2,1,0:T(8,128)(2,1)S(1)}, u32[]{:S(2)}, u32[]{:S(2)}) collective-permute-start(bf16[2,144,1600]{2,1,0:T(8,128)(2,1)} %copy-done.49), channel_id=1, source_target_pairs={{0,4},{4,0},{8,12},{12,8},{1,5},{5,1},{9,13},{13,9},{2,6},{6,2},{1... | collective-permute-start | bytes 2764808 | tf_op jit(solution)/shard_map/ppermute | solution.py:321
  502.7 21.7 %collective-permute-start.39 = (bf16[2,144,1600]{2,1,0:T(8,128)(2,1)}, bf16[2,144,1600]{2,1,0:T(8,128)(2,1)S(1)}, u32[]{:S(2)}, u32[]{:S(2)}) collective-permute-start(bf16[2,144,1600]{2,1,0:T(8,128)(2,1)} %copy-done.47), channel_id=1, source_target_pairs={{0,8},{4,12},{8,0},{12,4},{1,9},{5,13},{9,1},{13,5},{2,10},{6,14},... | collective-permute-start | bytes 2764808 | tf_op jit(solution)/shard_map/ppermute | solution.py:321
  525.9 29.7 %collective-permute-start.40 = (bf16[2,144,1536]{2,1,0:T(8,128)(2,1)S(1)}, bf16[2,144,1536]{2,1,0:T(8,128)(2,1)S(1)}, u32[]{:S(2)}, u32[]{:S(2)}) collective-permute-start(bf16[2,144,1536]{2,1,0:T(8,128)(2,1)S(1)} %get-tuple-element.217), channel_id=1, source_target_pairs={{0,4},{4,0},{8,12},{12,8},{1,5},{5,1},{9,13},{13,9},{2,6},{6,2},{1... | collective-permute-start | bytes 2654216 | tf_op jit(solution)/shard_map/ppermute | solution.py:321
  526.6 28.9 %collective-permute-start.41 = (bf16[2,144,1536]{2,1,0:T(8,128)(2,1)S(1)}, bf16[2,144,1536]{2,1,0:T(8,128)(2,1)S(1)}, u32[]{:S(2)}, u32[]{:S(2)}) collective-permute-start(bf16[2,144,1536]{2,1,0:T(8,128)(2,1)S(1)} %get-tuple-element.218), channel_id=1, source_target_pairs={{0,8},{4,12},{8,0},{12,4},{1,9},{5,13},{9,1},{13,5},{2,10},{6,14},... | collective-permute-start | bytes 2654216 | tf_op jit(solution)/shard_map/ppermute | solution.py:321
  527.0 28.5 %collective-permute-start.42 = (bf16[144,1600]{1,0:T(8,128)(2,1)S(1)}, bf16[144,1600]{1,0:T(8,128)(2,1)S(1)}, u32[]{:S(2)}, u32[]{:S(2)}) collective-permute-start(bf16[144,1600]{1,0:T(8,128)(2,1)S(1)} %get-tuple-element.225), channel_id=1, source_target_pairs={{0,8},{4,12},{8,0},{12,4},{1,9},{5,13},{9,1},{13,5},{2,10},{6,14},... | collective-permute-start | bytes 1382408 | tf_op jit(solution)/shard_map/ppermute | solution.py:321
  528.1 27.5 %collective-permute-start.43 = (bf16[144,1600]{1,0:T(8,128)(2,1)S(1)}, bf16[144,1600]{1,0:T(8,128)(2,1)S(1)}, u32[]{:S(2)}, u32[]{:S(2)}) collective-permute-start(bf16[144,1600]{1,0:T(8,128)(2,1)S(1)} %get-tuple-element.226), channel_id=1, source_target_pairs={{0,4},{4,0},{8,12},{12,8},{1,5},{5,1},{9,13},{13,9},{2,6},{6,2},{1... | collective-permute-start | bytes 1382408 | tf_op jit(solution)/shard_map/ppermute | solution.py:321
  579.2 52.9 %collective-permute-start.47 = (bf16[2,144,3072]{2,1,0:T(8,128)(2,1)}, bf16[2,144,3072]{2,1,0:T(8,128)(2,1)}, u32[]{:S(2)}, u32[]{:S(2)}) collective-permute-start(bf16[2,144,3072]{2,1,0:T(8,128)(2,1)} %get-tuple-element.236), channel_id=1, source_target_pairs={{0,4},{4,0},{8,12},{12,8},{1,5},{5,1},{9,13},{13,9},{2,6},{6,2},{1... | collective-permute-start | bytes 5308424 | tf_op jit(solution)/shard_map/ppermute | solution.py:321
  579.9 52.2 %collective-permute-start.48 = (bf16[2,144,3072]{2,1,0:T(8,128)(2,1)}, bf16[2,144,3072]{2,1,0:T(8,128)(2,1)}, u32[]{:S(2)}, u32[]{:S(2)}) collective-permute-start(bf16[2,144,3072]{2,1,0:T(8,128)(2,1)} %get-tuple-element.237), channel_id=1, source_target_pairs={{0,8},{4,12},{8,0},{12,4},{1,9},{5,13},{9,1},{13,5},{2,10},{6,14},... | collective-permute-start | bytes 5308424 | tf_op jit(solution)/shard_map/ppermute | solution.py:321
  581.0 125.1 %reduce-scatter.11.cloned.1.call-start = ((), (), s32[]{:S(2)}) async-start(), calls=%async_computation.7 | async-start | bytes 2211840 | tf_op jit(solution)/shard_map/reduce_scatter | solution.py:800
  584.6 47.5 %collective-permute-start.49 = (bf16[2,128,1152]{2,1,0:T(8,128)(2,1)}, bf16[2,128,1152]{2,1,0:T(8,128)(2,1)}, u32[]{:S(2)}, u32[]{:S(2)}) collective-permute-start(bf16[2,128,1152]{2,1,0:T(8,128)(2,1)} %get-tuple-element.246), channel_id=1, source_target_pairs={{0,8},{4,12},{8,0},{12,4},{1,9},{5,13},{9,1},{13,5},{2,10},{6,14},... | collective-permute-start | bytes 1769480 | tf_op jit(solution)/shard_map/ppermute | solution.py:321
  585.0 47.1 %collective-permute-start.50 = (bf16[2,128,1152]{2,1,0:T(8,128)(2,1)}, bf16[2,128,1152]{2,1,0:T(8,128)(2,1)}, u32[]{:S(2)}, u32[]{:S(2)}) collective-permute-start(bf16[2,128,1152]{2,1,0:T(8,128)(2,1)} %get-tuple-element.247), channel_id=1, source_target_pairs={{0,4},{4,0},{8,12},{12,8},{1,5},{5,1},{9,13},{13,9},{2,6},{6,2},{1... | collective-permute-start | bytes 1769480 | tf_op jit(solution)/shard_map/ppermute | solution.py:321
  639.7 16.9 %collective-permute-start.51 = (bf16[1024,1152]{1,0:T(8,128)(2,1)}, bf16[1024,1152]{1,0:T(8,128)(2,1)}, u32[]{:S(2)}, u32[]{:S(2)}) collective-permute-start(bf16[1024,1152]{1,0:T(8,128)(2,1)} %get-tuple-element.252.own_a.own_ref), channel_id=1, source_target_pairs={{0,16},{16,0},{1,17},{17,1},{2,18},{18,2},{3,19},{19,3},{4,20},{20... | collective-permute-start | bytes 7077896 | tf_op jit(solution)/shard_map/ppermute | solution.py:307
  642.6 21.5 %collective-permute-start.54 = (bf16[144,3072]{1,0:T(8,128)(2,1)}, bf16[144,3072]{1,0:T(8,128)(2,1)S(1)}, u32[]{:S(2)}, u32[]{:S(2)}) collective-permute-start(bf16[144,3072]{1,0:T(8,128)(2,1)} %copy-done.52), channel_id=1, source_target_pairs={{0,8},{4,12},{8,0},{12,4},{1,9},{5,13},{9,1},{13,5},{2,10},{6,14},... | collective-permute-start | bytes 2654216 | tf_op jit(solution)/shard_map/ppermute | solution.py:321
  643.6 21.2 %collective-permute-start.55 = (bf16[144,3072]{1,0:T(8,128)(2,1)}, bf16[144,3072]{1,0:T(8,128)(2,1)S(1)}, u32[]{:S(2)}, u32[]{:S(2)}) collective-permute-start(bf16[144,3072]{1,0:T(8,128)(2,1)} %copy-done.50), channel_id=1, source_target_pairs={{0,4},{4,0},{8,12},{12,8},{1,5},{5,1},{9,13},{13,9},{2,6},{6,2},{1... | collective-permute-start | bytes 2654216 | tf_op jit(solution)/shard_map/ppermute | solution.py:321
  667.3 79.5 %reduce-scatter.15.cloned.1.call-start = ((), (), s32[]{:S(2)}) async-start(), calls=%async_computation.9 | async-start | bytes 1198080
  667.4 22.0 %collective-permute-start.52 = (bf16[2,144,1600]{2,1,0:T(8,128)(2,1)}, bf16[2,144,1600]{2,1,0:T(8,128)(2,1)S(1)}, u32[]{:S(2)}, u32[]{:S(2)}) collective-permute-start(bf16[2,144,1600]{2,1,0:T(8,128)(2,1)} %copy-done.48), channel_id=1, source_target_pairs={{0,4},{4,0},{8,12},{12,8},{1,5},{5,1},{9,13},{13,9},{2,6},{6,2},{1... | collective-permute-start | bytes 2764808 | tf_op jit(solution)/shard_map/ppermute | solution.py:321
  668.2 21.7 %collective-permute-start.53 = (bf16[2,144,1600]{2,1,0:T(8,128)(2,1)}, bf16[2,144,1600]{2,1,0:T(8,128)(2,1)S(1)}, u32[]{:S(2)}, u32[]{:S(2)}) collective-permute-start(bf16[2,144,1600]{2,1,0:T(8,128)(2,1)} %copy-done.46), channel_id=1, source_target_pairs={{0,8},{4,12},{8,0},{12,4},{1,9},{5,13},{9,1},{13,5},{2,10},{6,14},... | collective-permute-start | bytes 2764808 | tf_op jit(solution)/shard_map/ppermute | solution.py:321
  717.2 17.2 %collective-permute-start.63 = (bf16[72,1536]{1,0:T(8,128)(2,1)S(1)}, bf16[72,1536]{1,0:T(8,128)(2,1)S(1)}, u32[]{:S(2)}, u32[]{:S(2)}) collective-permute-start(bf16[72,1536]{1,0:T(8,128)(2,1)S(1)} %get-tuple-element.361), channel_id=1, source_target_pairs={{0,16},{16,0},{1,17},{17,1},{2,18},{18,2},{3,19},{19,3},{4,20},{20... | collective-permute-start | bytes 663560 | tf_op jit(solution)/shard_map/ppermute | solution.py:307
  717.8 16.6 %collective-permute-start.64 = (bf16[72,1536]{1,0:T(8,128)(2,1)S(1)}, bf16[72,1536]{1,0:T(8,128)(2,1)S(1)}, u32[]{:S(2)}, u32[]{:S(2)}) collective-permute-start(bf16[72,1536]{1,0:T(8,128)(2,1)S(1)} %get-tuple-element.362), channel_id=1, source_target_pairs={{0,16},{16,0},{1,17},{17,1},{2,18},{18,2},{3,19},{19,3},{4,20},{20... | collective-permute-start | bytes 663560 | tf_op jit(solution)/shard_map/ppermute | solution.py:307
  (111 other events, 1019.1 us)
Sparse Core Ops, SparseCore 0:
  27.1 64.9 all-gather.2
  94.2 70.3 all-gather.4
  501.9 52.7 reduce-scatter.8
  581.1 39.9 reduce-scatter.12
  667.5 38.6 reduce-scatter.10
  710.5 23.9 reduce-scatter.14
